TPU v7x, 32 devices: a whole 2x2x4 slice. The times are simulated.
32 devices in a mesh: groups: 2 (over y), dp: 8 (over z, x), tp: 2 (over core).
Axes of the slice: x: 2, y: 2, z: 4, core: 2. Of those that a mesh axis runs over, the one named last changes fastest.
Arguments:
- tokens: bfloat16 [2048, 4096], P(('groups', 'dp')), parts along dimension 0, may hold values from -6 to 6
- pool: bfloat16 [256, 2, 64, 256], P(('groups', 'dp'), None, None, 'tp'), parts along dimension 0, may hold values from -6 to 6
- pages_count: int32 [16], P(('groups', 'dp')), parts along dimension 0, may hold values from 3 to 4, as said below
- owners: int32 [16, 4], P(('groups', 'dp')), parts along dimension 0, may hold values from 0 to 7, as said below
- slots: int32 [16, 4], P(('groups', 'dp')), parts along dimension 0, may hold values from 0 to 15
- homes: int32 [16, 2], P(('groups', 'dp')), parts along dimension 0, may hold values from 0 to 7, as said below
- home_slots: int32 [16, 2], P(('groups', 'dp')), parts along dimension 0, may hold values from 0 to 15, as said below
- norm_attn: float32 [4096], replicated, may hold values from 0.5 to 1.5
- wqkv: bfloat16 [4096, 2, 6, 128], P('dp', 'tp')
Outputs:
- attended: bfloat16 [2048, 1024], P(('groups', 'dp'), 'tp'), parts along dimension 0
- pool_out: bfloat16 [256, 2, 64, 256], P(('groups', 'dp'), None, None, 'tp'), parts along dimension 0
There are 2 independent parts, one for each index of `groups`. A program takes and returns all parts, laid end to end along the dimension named above; an argument that names none is the same for every part. Nothing has to cross between parts.
Inputs may be any that keep to these rules, and one draw needn't show every extreme that they name: `pages_count`: some request has 4. `owners`: the ranks listed for one request are distinct; entries past its page count are not read. `homes`: one request's new pages go to distinct ranks, and every rank receives exactly 2 new pages. `home_slots`: the slots that one rank receives are distinct.
All inputs are finite; a program needn't handle non-finite values.
Results may differ from a plain program's by a relative error of at most 0.011.
Values may be sent and summed in bfloat16 or wider, within the bound.
No kernel may reach another device: no remote copies, remote signals or barrier semaphores. Data moves between devices by JAX's collectives and lax.ppermute only.
A program may use at most 128 MiB of HBM per device.

v0:
```python
import math

import jax
import jax.numpy as jnp
from jax import lax
from jax.sharding import PartitionSpec as P


def rms_norm(values, gain):
    return values * lax.rsqrt(jnp.mean(values * values, axis=-1, keepdims=True) + 1e-05) * gain


def rotate(values, positions):
    half_size = values.shape[-1] // 2
    index_f = jnp.arange(half_size).astype(jnp.float32)
    inverse = jnp.exp(-(2.0 * index_f / values.shape[-1]) * jnp.log(500000.0))
    angles = positions[..., None] * inverse
    extra = values.ndim - angles.ndim
    angles = angles.reshape(angles.shape[:-1] + (1,) * extra + (half_size,))
    cosine = jnp.cos(angles)
    sine = jnp.sin(angles)
    first = values[..., :half_size]
    second = values[..., half_size:]
    return jnp.concatenate(
        [first * cosine - second * sine, second * cosine + first * sine], axis=-1
    )


def attend_part(queries, keys, values, allowed, scale):
    scores = (
        lax.dot_general(queries, keys, (((1,), (1,)), ((), ())), preferred_element_type=jnp.float32)
        * scale
    )
    scores = jnp.where(allowed, scores, -1e30)
    largest = jnp.max(scores, axis=1, keepdims=True)
    weights = jnp.exp(scores - largest)
    totals = jnp.sum(weights, axis=1, keepdims=True)
    summed = jnp.dot(weights.astype(jnp.bfloat16), values, preferred_element_type=jnp.float32)
    return (largest, totals, summed)


def row_adder(left, shard_piece):
    count_rows = shard_piece.shape[0]
    return jnp.dot(left, shard_piece.reshape(count_rows, -1), preferred_element_type=jnp.float32)


def local(tokens, pool, pages_count, owners, slots, homes, home_slots, norm_attn, wqkv):
    ranks = lax.axis_size("dp")
    token_rows, width = tokens.shape
    group = wqkv.shape[2] - 2
    blocks = group + 2
    head_size = wqkv.shape[3]
    page_rows = pool.shape[2]
    scale = 1.0 / math.sqrt(head_size)
    normed = rms_norm(tokens.astype(jnp.float32), norm_attn).astype(jnp.bfloat16)
    projected = row_adder(normed, lax.all_gather(wqkv, "dp", axis=0, tiled=True))
    projected = projected.reshape(token_rows, blocks, head_size)
    positions = (pages_count[0] * page_rows + jnp.arange(token_rows, dtype=jnp.int32)).astype(
        jnp.float32
    )
    queries = rotate(projected[:, :group], positions).astype(jnp.bfloat16)
    keys_new = rotate(projected[:, group], positions).astype(jnp.bfloat16)
    values_new = projected[:, group + 1].astype(jnp.bfloat16)
    lanes = jnp.arange(ranks, dtype=jnp.int32)
    fresh = jnp.stack(
        [keys_new.reshape(-1, page_rows, head_size), values_new.reshape(-1, page_rows, head_size)],
        axis=1,
    )
    to_home = homes[0][:, None] == lanes[None, :]
    outgoing = jnp.einsum(
        "jn,jkph->nkph", to_home.astype(jnp.bfloat16), fresh, preferred_element_type=jnp.float32
    ).astype(jnp.bfloat16)
    targets_out = jnp.sum(jnp.where(to_home, home_slots[0][:, None] + 1, 0), axis=0) - 1
    listed = jnp.arange(owners.shape[1], dtype=jnp.int32) < pages_count[0]
    from_owner = (owners[0][:, None] == lanes[None, :]) & listed[:, None]
    wanted = jnp.sum(jnp.where(from_owner, slots[0][:, None] + 1, 0), axis=0) - 1
    causal = jnp.arange(token_rows)[:, None] >= jnp.arange(token_rows)[None, :]
    asked, targets_in = (
        lax.all_to_all(wanted[:, None], "dp", split_axis=0, concat_axis=0, tiled=True),
        lax.all_to_all(targets_out[:, None], "dp", split_axis=0, concat_axis=0, tiled=True),
    )
    chosen = pool[jnp.maximum(asked[:, 0], 0)]
    replies = lax.all_to_all(chosen, "dp", split_axis=0, concat_axis=0, tiled=True)
    incoming = lax.all_to_all(outgoing, "dp", split_axis=0, concat_axis=0, tiled=True)
    landing = jnp.where(targets_in[:, 0] >= 0, targets_in[:, 0], pool.shape[0])
    pool_out = pool.at[landing].set(incoming, mode="drop")
    prefix_keys = replies[:, 0].reshape(ranks * page_rows, head_size)
    prefix_values = replies[:, 1].reshape(ranks * page_rows, head_size)
    prefix_live = jnp.repeat(wanted >= 0, page_rows)[None, :]
    outputs = []
    allowed = jnp.concatenate(
        [jnp.broadcast_to(prefix_live, (token_rows, ranks * page_rows)), causal], axis=1
    )
    all_keys = jnp.concatenate([prefix_keys, keys_new], axis=0)
    all_values = jnp.concatenate([prefix_values, values_new], axis=0)
    for member in range(group):
        merged = attend_part(queries[:, member], all_keys, all_values, allowed, scale)
        outputs.append((merged[2] / merged[1]).astype(jnp.bfloat16))
    attended = jnp.concatenate(outputs, axis=1)
    return (attended, pool_out)


def solution(mesh):
    in_specs = (
        P(("groups", "dp"), None),
        P(("groups", "dp"), None, None, "tp"),
        P(("groups", "dp")),
        P(("groups", "dp"), None),
        P(("groups", "dp"), None),
        P(("groups", "dp"), None),
        P(("groups", "dp"), None),
        P(),
        P("dp", "tp", None, None),
    )
    out_specs = (P(("groups", "dp"), "tp"), P(("groups", "dp"), None, None, "tp"))
    return jax.shard_map(local, mesh=mesh, in_specs=in_specs, out_specs=out_specs, check_vma=False)
```

profile of v0, /device:TPU:0, one launch (start us, length us, event | category | flops | bytes accessed | tf_op | source)
XLA Modules:
  0.0 152.1 jit_solution(1994201325253817338)
XLA Ops:
  7.2 0.0 copy-start
  7.2 0.0 copy-start.3
  7.2 0.0 copy-start.4
  7.2 0.0 copy-start.6
  7.2 0.0 copy-start.5
  7.2 0.0 all-gather.2.cloned.1.call-start
  7.3 1.1 copy.69
  8.4 2.3 %copy.49 = bf16[512,1,6,128]{0,3,2,1:T(8,128)(2,1)} copy(bf16[512,1,6,128]{3,0,2,1:T(8,128)(2,1)} %param.17) | data formatting | bytes 1572864 | tf_op args[8]
  10.7 0.0 copy-start.2
  10.7 0.0 all-gather.2.cloned.1.call-update
  11.4 0.0 copy-done.4
  11.4 0.0 copy-done.3
  11.4 0.1 select_reduce_fusion
  11.5 0.7 copy.50
  12.2 7.3 %all-to-all-start = ((s32[8,1,1]{2,1,0:T(1,128)}), s32[8,1,1]{2,1,0:T(1,128)S(1)}, u32[]{:S(2)}, u32[]{:S(2)}) async-start(s32[8,1,1]{2,1,0:T(1,128)} %copy.50), calls=%async_computation | async-start | bytes 8192 | tf_op jit(solution)/shard_map/all_to_all | solution.py:79
  19.4 0.0 copy-done.5
  19.4 0.0 copy-done.6
  19.4 0.1 select_reduce_fusion.1
  19.5 0.7 copy.53
  20.2 0.0 copy-done
  20.3 0.3 fusion.2
  20.6 5.3 %all-to-all-done = s32[8,1,1]{2,1,0:T(1,128)S(1)} async-done(((s32[8,1,1]{2,1,0:T(1,128)}), s32[8,1,1]{2,1,0:T(1,128)S(1)}, u32[]{:S(2)}, u32[]{:S(2)}) %all-to-all-start) | async-done | bytes 64 | tf_op jit(solution)/shard_map/all_to_all | solution.py:79
  25.8 3.3 %all-to-all-start.2 = ((s32[8,1,1]{2,1,0:T(1,128)}), s32[8,1,1]{2,1,0:T(1,128)S(1)}, u32[]{:S(2)}, u32[]{:S(2)}) async-start(s32[8,1,1]{2,1,0:T(1,128)} %copy.53), calls=%async_computation.2 | async-start | bytes 8192 | tf_op jit(solution)/shard_map/all_to_all | solution.py:80
  29.1 0.2 maximum_reduce_fusion
  29.3 1.3 gather_fusion
  30.6 4.9 %all-to-all-done.2 = s32[8,1,1]{2,1,0:T(1,128)S(1)} async-done(((s32[8,1,1]{2,1,0:T(1,128)}), s32[8,1,1]{2,1,0:T(1,128)S(1)}, u32[]{:S(2)}, u32[]{:S(2)}) %all-to-all-start.2) | async-done | bytes 64 | tf_op jit(solution)/shard_map/all_to_all | solution.py:80
  35.5 3.4 %all-to-all-start.1 = ((bf16[8,2,64,128]{3,2,1,0:T(8,128)(2,1)}), bf16[8,2,64,128]{3,2,1,0:T(8,128)(2,1)S(1)}, u32[]{:S(2)}, u32[]{:S(2)}) async-start(bf16[8,2,64,128]{3,2,1,0:T(8,128)(2,1)} %gather_fusion), calls=%async_computation.1 | async-start | bytes 524288 | tf_op jit(solution)/shard_map/all_to_all | solution.py:83
  38.9 0.1 broadcast_in_dim.41
  39.0 0.1 reshape.241
  39.1 0.2 reduce.1
  39.4 16.1 %all-to-all-done.1 = bf16[8,2,64,128]{3,2,1,0:T(8,128)(2,1)S(1)} async-done(((bf16[8,2,64,128]{3,2,1,0:T(8,128)(2,1)}), bf16[8,2,64,128]{3,2,1,0:T(8,128)(2,1)S(1)}, u32[]{:S(2)}, u32[]{:S(2)}) %all-to-all-start.1) | async-done | bytes 262176 | tf_op jit(solution)/shard_map/all_to_all | solution.py:83
  55.5 66.3 %all-gather.2.cloned.1.call-done = bf16[4096,1,6,128]{0,3,2,1:T(8,128)(2,1)} async-done(((bf16[512,1,6,128]{0,3,2,1:T(8,128)(2,1)}), bf16[4096,1,6,128]{0,3,2,1:T(8,128)(2,1)}) %all-gather.2.cloned.1.call-update) | async-done | bytes 6291472 | tf_op jit(solution)/shard_map/all_gather | solution.py:56
  121.8 0.0 copy-done.2
  121.8 4.6 %fusion = f32[128,6,128]{0,2,1:T(8,128)S(1)} fusion(bf16[4096,1,6,128]{0,3,2,1:T(8,128)(2,1)} %all-gather.2.cloned.1.call-done, bf16[128,4096]{1,0:T(8,128)(2,1)S(1)} %copy-done, f32[4096]{0:T(1024)S(1)} %copy-done.2, f32[128]{0:T(128)S(1)} %add_rsqrt_fusion), kind=kOutput, calls=%fused_computation.2 | convolution fusion | flops 807403520 | bytes 7750144 | tf_op jit(solution)/shard_map/dot_general | solution.py:44
  126.5 0.2 subtract_convert_fusion.1
  126.7 0.1 copy.51
  126.9 0.3 fusion.63
  127.2 0.3 fusion.62
  127.5 0.3 fusion.61
  127.9 0.3 fusion.60
  128.2 0.1 concatenate.40
  128.3 0.1 concatenate.41
  128.4 0.1 copy.52
  128.5 0.2 fusion.17
  128.7 0.2 fusion.19
  128.9 0.3 fusion.9
  129.2 0.3 fusion.10
  129.5 0.2 fusion.21
  129.7 0.3 fusion.11
  130.0 0.1 copy.54
  130.1 0.1 copy.55
  130.2 0.1 copy.56
  130.4 0.4 convolution_convert_fusion
  130.8 0.8 copy.58
  131.5 3.4 %all-to-all-start.3 = ((bf16[8,2,64,128]{3,2,1,0:T(8,128)(2,1)}), bf16[8,2,64,128]{3,2,1,0:T(8,128)(2,1)S(1)}, u32[]{:S(2)}, u32[]{:S(2)}) async-start(bf16[8,2,64,128]{3,2,1,0:T(8,128)(2,1)} %copy.58), calls=%async_computation.3 | async-start | bytes 524288 | tf_op jit(solution)/shard_map/all_to_all | solution.py:84
  135.0 0.2 fusion.23
  135.2 0.3 fusion.12
  135.5 0.8 copy.59
  136.3 7.4 %all-to-all-done.3 = bf16[8,2,64,128]{3,2,1,0:T(8,128)(2,1)S(1)} async-done(((bf16[8,2,64,128]{3,2,1,0:T(8,128)(2,1)}), bf16[8,2,64,128]{3,2,1,0:T(8,128)(2,1)S(1)}, u32[]{:S(2)}, u32[]{:S(2)}) %all-to-all-start.3) | async-done | bytes 262176 | tf_op jit(solution)/shard_map/all_to_all | solution.py:84
  143.6 0.8 scatter_fusion
  144.4 0.0 copy-start.1
  144.4 0.8 copy-done.1
  (21 shorter events, 0.2 us)
Async XLA Ops:
  7.2 13.1 %copy-start = (bf16[128,4096]{1,0:T(8,128)(2,1)S(1)}, bf16[128,4096]{1,0:T(8,128)(2,1)}, u32[]{:S(2)}) copy-start(bf16[128,4096]{1,0:T(8,128)(2,1)} %param.9) | copy-start | bytes 3145732
  7.2 4.2 %copy-start.3 = (s32[1,4]{1,0:T(1,128)S(1)}, s32[1,4]{1,0:T(1,128)}, u32[]{:S(2)}) copy-start(s32[1,4]{1,0:T(1,128)} %param.12) | copy-start | bytes 52
  7.2 4.2 %copy-start.4 = (s32[1,4]{1,0:T(1,128)S(1)}, s32[1,4]{1,0:T(1,128)}, u32[]{:S(2)}) copy-start(s32[1,4]{1,0:T(1,128)} %param.13) | copy-start | bytes 52
  7.2 12.2 %copy-start.6 = (s32[1,2]{1,0:T(1,128)S(1)}, s32[1,2]{1,0:T(1,128)}, u32[]{:S(2)}) copy-start(s32[1,2]{1,0:T(1,128)} %param.14) | copy-start | bytes 28
  7.2 12.2 %copy-start.5 = (s32[1,2]{1,0:T(1,128)S(1)}, s32[1,2]{1,0:T(1,128)}, u32[]{:S(2)}) copy-start(s32[1,2]{1,0:T(1,128)} %param.15) | copy-start | bytes 28
  7.2 114.6 %all-gather.2.cloned.1.call-start = ((), (), s32[]{:S(2)}) async-start(), calls=%async_computation.4 | async-start | bytes 7077888 | tf_op jit(solution)/shard_map/all_gather | solution.py:56
  10.7 111.1 %copy-start.2 = (f32[4096]{0:T(1024)S(1)}, f32[4096]{0:T(1024)}, u32[]{:S(2)}) copy-start(f32[4096]{0:T(1024)} %param.16) | copy-start | bytes 49156
  12.2 13.6 %all-to-all-start = ((s32[8,1,1]{2,1,0:T(1,128)}), s32[8,1,1]{2,1,0:T(1,128)S(1)}, u32[]{:S(2)}, u32[]{:S(2)}) async-start(s32[8,1,1]{2,1,0:T(1,128)} %copy.50), calls=%async_computation | async-start | bytes 8192 | tf_op jit(solution)/shard_map/all_to_all | solution.py:79
  25.8 9.7 %all-to-all-start.2 = ((s32[8,1,1]{2,1,0:T(1,128)}), s32[8,1,1]{2,1,0:T(1,128)S(1)}, u32[]{:S(2)}, u32[]{:S(2)}) async-start(s32[8,1,1]{2,1,0:T(1,128)} %copy.53), calls=%async_computation.2 | async-start | bytes 8192 | tf_op jit(solution)/shard_map/all_to_all | solution.py:80
  35.5 20.0 %all-to-all-start.1 = ((bf16[8,2,64,128]{3,2,1,0:T(8,128)(2,1)}), bf16[8,2,64,128]{3,2,1,0:T(8,128)(2,1)S(1)}, u32[]{:S(2)}, u32[]{:S(2)}) async-start(bf16[8,2,64,128]{3,2,1,0:T(8,128)(2,1)} %gather_fusion), calls=%async_computation.1 | async-start | bytes 524288 | tf_op jit(solution)/shard_map/all_to_all | solution.py:83
  131.5 12.1 %all-to-all-start.3 = ((bf16[8,2,64,128]{3,2,1,0:T(8,128)(2,1)}), bf16[8,2,64,128]{3,2,1,0:T(8,128)(2,1)S(1)}, u32[]{:S(2)}, u32[]{:S(2)}) async-start(bf16[8,2,64,128]{3,2,1,0:T(8,128)(2,1)} %copy.58), calls=%async_computation.3 | async-start | bytes 524288 | tf_op jit(solution)/shard_map/all_to_all | solution.py:84
  144.4 0.8 copy-start.1
Sparse Core Ops, SparseCore 0:
  10.8 110.9 all-gather.1
where the time goes:
time: 153 us; the launch traced here: 152 us
  waiting for transfers between devices  99.9 us (65%)
  starting transfers between devices  17.4 us (11%)
  between operations  15 us (10%)
  local copies, waits for them, and re-layouts  10.1 us (7%)
  matrix products  7.53 us (5%)
  other arithmetic  2.09 us (1%)
    all_gather x1, waiting for transfers between devices, local(): lax.all_gather(wqkv, 'dp', axis=0, tiled=True)  66.3 us
    all_to_all x1, waiting for transfers between devices, local(): lax.all_to_all(chosen, 'dp', split_axis=0, concat_axis=0, tiled=True)  16.1 us
    all_to_all x1, waiting for transfers between devices, local(): lax.all_to_all(outgoing, 'dp', split_axis=0, concat_axis=0, tiled=True)  7.37 us
    all_to_all x1, starting transfers between devices, local(): lax.all_to_all(wanted[:, None], 'dp', split_axis=0, concat_axis=0, tiled=...  7.25 us
    all_to_all x1, waiting for transfers between devices, local(): lax.all_to_all(wanted[:, None], 'dp', split_axis=0, concat_axis=0, tiled=...  5.26 us
    unnamed x17, local copies, waits for them, and re-layouts  4.99 us
    all_to_all x1, waiting for transfers between devices, local(): lax.all_to_all(targets_out[:, None], 'dp', split_axis=0, concat_axis=0, t...  4.88 us
    dot_general x1, matrix products, row_adder(): jnp.dot(left, shard_piece.reshape(count_rows, -1), preferred_element_type...  4.65 us
  transfers between devices with their start and end apart: 5, of which 5 were waited for; matrix products, arithmetic and copies ran while one was open for 3% of the time, Pallas kernels for 0%

commit v1 on v0

v1 whole, which is shorter than its diff:
```python
import math

import jax
import jax.numpy as jnp
from jax import lax
from jax.sharding import PartitionSpec as P

PERMUTE_LIMIT = 4


def exclusive(size, distance):
    return [(rank, rank ^ distance) for rank in range(size)]


def rotary_tables(positions, head_size):
    half_size = head_size // 2
    index_f = jnp.arange(half_size).astype(jnp.float32)
    inverse = jnp.exp(-(2.0 * index_f / head_size) * jnp.log(500000.0))
    angles = positions[:, None] * inverse[None, :]
    return jnp.cos(angles), jnp.sin(angles)


def rotate(values, cosine, sine):
    half_size = values.shape[-1] // 2
    first = values[..., :half_size]
    second = values[..., half_size:]
    cosine = cosine[:, None, :]
    sine = sine[:, None, :]
    return jnp.concatenate([first * cosine - second * sine, second * cosine + first * sine], axis=-1)


def attend_part(queries, keys, values, allowed, scale):
    scores = (
        lax.dot_general(queries, keys, (((1,), (1,)), ((), ())), preferred_element_type=jnp.float32)
        * scale
    )
    scores = jnp.where(allowed, scores, -1e30)
    largest = jnp.max(scores, axis=1, keepdims=True)
    weights = jnp.exp(scores - largest)
    totals = jnp.sum(weights, axis=1, keepdims=True)
    summed = jnp.dot(weights.astype(jnp.bfloat16), values, preferred_element_type=jnp.float32)
    return (largest, totals, summed)


def gather_info(info, ranks):
    me = lax.axis_index("dp")
    table = jnp.zeros((ranks, info.shape[0]), jnp.int32).at[me].set(info)
    distance = 1
    while distance < ranks:
        table = table + lax.ppermute(table, "dp", exclusive(ranks, distance))
        distance *= 2
    return table


def project(tokens, gain, weight, ranks):
    me = lax.axis_index("dp")
    core = lax.axis_index("tp")
    rows = weight.shape[0]
    span = 2 * rows
    members = ranks // 2
    token_rows = tokens.shape[0]
    member = me // 2
    other = lax.ppermute(weight, "dp", exclusive(ranks, 1))
    own_first = (me % 2) == core
    direct_weight = jnp.where(own_first, weight, other)
    passed_weight = jnp.where(own_first, other, weight)
    direct_gain = lax.dynamic_slice(gain, (member * span + core * rows,), (rows,))
    passed_gain = lax.dynamic_slice(gain, (member * span + (1 - core) * rows,), (rows,))

    def multiply(direct, passed):
        left = (direct.astype(jnp.float32) * direct_gain).astype(jnp.bfloat16)
        right = (passed.astype(jnp.float32) * passed_gain).astype(jnp.bfloat16)
        return jnp.dot(left, direct_weight, preferred_element_type=jnp.float32) + jnp.dot(
            right, passed_weight, preferred_element_type=jnp.float32
        )

    def half_for(target, which):
        return lax.dynamic_slice(
            tokens, (0, target * span + which * rows), (token_rows, rows)
        )

    total = multiply(half_for(member, core), half_for(member, 1 - core))
    if members <= PERMUTE_LIMIT:
        order = [2, 3, 1] if members == 4 else list(range(1, members))
        received = [
            lax.ppermute(half_for(member ^ step, core), "dp", exclusive(ranks, 2 * step))
            for step in order
        ]
        swapped = [lax.ppermute(piece, "tp", [(0, 1), (1, 0)]) for piece in received]
        returned = [
            lax.ppermute(
                multiply(direct, passed).astype(jnp.bfloat16), "dp", exclusive(ranks, 2 * step)
            )
            for step, direct, passed in zip(order, received, swapped)
        ]
        for piece in returned:
            total = total + piece.astype(jnp.float32)
        return total
    groups = [[2 * index + side for index in range(members)] for side in range(2)]
    blocks = tokens.reshape(token_rows, members, span).transpose(1, 0, 2)
    blocks = lax.all_to_all(
        blocks, "dp", split_axis=0, concat_axis=0, axis_index_groups=groups, tiled=True
    )
    direct = lax.dynamic_slice(blocks, (0, 0, core * rows), (members, token_rows, rows))
    passed = lax.dynamic_slice(blocks, (0, 0, (1 - core) * rows), (members, token_rows, rows))
    parts = multiply(direct.reshape(-1, rows), passed.reshape(-1, rows)).astype(jnp.bfloat16)
    parts = lax.all_to_all(
        parts.reshape(members, token_rows, -1),
        "dp",
        split_axis=0,
        concat_axis=0,
        axis_index_groups=groups,
        tiled=True,
    )
    return jnp.sum(parts.astype(jnp.float32), axis=0)


def local(tokens, pool, pages_count, owners, slots, homes, home_slots, norm_attn, wqkv):
    ranks = lax.axis_size("dp")
    me = lax.axis_index("dp")
    token_rows, width = tokens.shape
    group = wqkv.shape[2] - 2
    blocks = group + 2
    head_size = wqkv.shape[3]
    page_rows = pool.shape[2]
    scale = 1.0 / math.sqrt(head_size)
    prefix = owners.shape[1]

    raw = project(tokens, norm_attn, wqkv.reshape(wqkv.shape[0], -1), ranks)

    lanes = jnp.arange(ranks, dtype=jnp.int32)
    listed = jnp.arange(prefix, dtype=jnp.int32) < pages_count[0]
    info = jnp.concatenate(
        [jnp.where(listed, owners[0], -1), slots[0], homes[0], home_slots[0]]
    )
    table = gather_info(info, ranks)
    asked = jnp.sum(
        jnp.where(table[:, :prefix] == me, table[:, prefix : 2 * prefix], 0), axis=1
    )
    new_pages = homes.shape[1]
    home_table = table[:, 2 * prefix : 2 * prefix + new_pages]
    home_slot_table = table[:, 2 * prefix + new_pages :]
    targets_in = jnp.sum(jnp.where(home_table == me, home_slot_table + 1, 0), axis=1) - 1

    chosen = pool[asked]
    replies = lax.all_to_all(chosen, "dp", split_axis=0, concat_axis=0, tiled=True)

    wide = tokens.astype(jnp.float32)
    row_scale = lax.rsqrt(jnp.mean(wide * wide, axis=-1, keepdims=True) + 1e-05)
    positions = (pages_count[0] * page_rows + jnp.arange(token_rows, dtype=jnp.int32)).astype(
        jnp.float32
    )
    cosine, sine = rotary_tables(positions, head_size)
    projected = (raw * row_scale).reshape(token_rows, blocks, head_size)
    queries = rotate(projected[:, :group], cosine, sine).astype(jnp.bfloat16)
    keys_new = rotate(projected[:, group : group + 1], cosine, sine)[:, 0].astype(jnp.bfloat16)
    values_new = projected[:, group + 1].astype(jnp.bfloat16)

    fresh = jnp.stack(
        [keys_new.reshape(-1, page_rows, head_size), values_new.reshape(-1, page_rows, head_size)],
        axis=1,
    )
    to_home = homes[0][:, None] == lanes[None, :]
    outgoing = sum(
        jnp.where(to_home[index][:, None, None, None], fresh[index][None], 0)
        for index in range(new_pages)
    ).astype(jnp.bfloat16)
    incoming = lax.all_to_all(outgoing, "dp", split_axis=0, concat_axis=0, tiled=True)
    landing = jnp.where(targets_in >= 0, targets_in, pool.shape[0])
    pool_out = pool.at[landing].set(incoming, mode="drop")

    causal = jnp.arange(token_rows)[:, None] >= jnp.arange(token_rows)[None, :]
    prefix_keys = replies[:, 0].reshape(ranks * page_rows, head_size)
    prefix_values = replies[:, 1].reshape(ranks * page_rows, head_size)
    wanted = jnp.any((owners[0][:, None] == lanes[None, :]) & listed[:, None], axis=0)
    prefix_live = jnp.repeat(wanted, page_rows)[None, :]
    outputs = []
    allowed = jnp.concatenate(
        [jnp.broadcast_to(prefix_live, (token_rows, ranks * page_rows)), causal], axis=1
    )
    all_keys = jnp.concatenate([prefix_keys, keys_new], axis=0)
    all_values = jnp.concatenate([prefix_values, values_new], axis=0)
    for member in range(group):
        merged = attend_part(queries[:, member], all_keys, all_values, allowed, scale)
        outputs.append((merged[2] / merged[1]).astype(jnp.bfloat16))
    attended = jnp.concatenate(outputs, axis=1)
    return (attended, pool_out)


def solution(mesh):
    in_specs = (
        P(("groups", "dp"), None),
        P(("groups", "dp"), None, None, "tp"),
        P(("groups", "dp")),
        P(("groups", "dp"), None),
        P(("groups", "dp"), None),
        P(("groups", "dp"), None),
        P(("groups", "dp"), None),
        P(),
        P("dp", "tp", None, None),
    )
    out_specs = (P(("groups", "dp"), "tp"), P(("groups", "dp"), None, None, "tp"))
    return jax.shard_map(local, mesh=mesh, in_specs=in_specs, out_specs=out_specs, check_vma=False)
```

time: 153 us -> 85.7 us (0.56)
  waiting for transfers between devices: 99.9 us -> 31.2 us
  between operations: 15 us -> 1.66 us
  starting transfers between devices: 17.4 us -> 28.2 us
  matrix products: 7.53 us -> 11.1 us
  other arithmetic: 2.09 us -> 4.58 us
  local copies, waits for them, and re-layouts: 10.1 us -> 8.47 us
    all_gather x1 -> x0, waiting for transfers between devices: 66.3 us -> none  [local(): lax.all_gather(wqkv, 'dp', axis=0, tiled=True)]
    ppermute x0 -> x13, waiting for transfers between devices: none -> 18.6 us  [the longest x3 12.4 us: gather_info(): table = table + lax.ppermute(table, 'dp', exclusive(ranks, distance))]
    ppermute x0 -> x13, starting transfers between devices: none -> 17.1 us  [the longest x3 5.61 us: gather_info(): table = table + lax.ppermute(table, 'dp', exclusive(ranks, distance))]
    all_to_all x2 -> x0, starting transfers between devices: 10.5 us -> none  [the longest x1 7.25 us: local(): lax.all_to_all(wanted[:, None], 'dp', split_axis=0, concat_axis=0, tiled=...]
    all_to_all x2 -> x0, waiting for transfers between devices: 10.1 us -> none  [the longest x1 5.26 us: local(): lax.all_to_all(wanted[:, None], 'dp', split_axis=0, concat_axis=0, tiled=...]
    all_to_all x1, waiting for transfers between devices: 16.1 us -> 6.32 us  [local(): lax.all_to_all(chosen, 'dp', split_axis=0, concat_axis=0, tiled=True)]
    dot_general x2 -> x8, matrix products: 5 us -> 8.53 us  [the longest x4 4.28 us: multiply(): jnp.dot(left, direct_weight, preferred_element_type=jnp.float32)]
    all_to_all x1, starting transfers between devices: 3.41 us -> 6.05 us  [local(): lax.all_to_all(chosen, 'dp', split_axis=0, concat_axis=0, tiled=True)]
  transfers between devices with their start and end apart: 5 -> 15, of which waited for: 5 -> 7; matrix products, arithmetic and copies ran while one was open for 3% -> 20% of each run, Pallas kernels for 0% -> 0%
where the time goes in v1:
time: 85.7 us; the launch traced here: 85.1 us
  waiting for transfers between devices  31.2 us (36%)
  starting transfers between devices  28.2 us (33%)
  matrix products  11.1 us (13%)
  local copies, waits for them, and re-layouts  8.47 us (10%)
  other arithmetic  4.58 us (5%)
  between operations  1.66 us (2%)
    ppermute x3, waiting for transfers between devices, gather_info(): table = table + lax.ppermute(table, 'dp', exclusive(ranks, distance))  12.4 us
    all_to_all x1, waiting for transfers between devices, local(): lax.all_to_all(chosen, 'dp', split_axis=0, concat_axis=0, tiled=True)  6.32 us
    all_to_all x1, waiting for transfers between devices, local(): lax.all_to_all(outgoing, 'dp', split_axis=0, concat_axis=0, tiled=True)  6.25 us
    ppermute x3, waiting for transfers between devices, project(): lax.ppermute(multiply(direct, passed).astype(jnp.bfloat16), 'dp', exclusi...  6.19 us
    all_to_all x1, starting transfers between devices, local(): lax.all_to_all(chosen, 'dp', split_axis=0, concat_axis=0, tiled=True)  6.05 us
    ppermute x3, starting transfers between devices, gather_info(): table = table + lax.ppermute(table, 'dp', exclusive(ranks, distance))  5.61 us
    all_to_all x1, starting transfers between devices, local(): lax.all_to_all(outgoing, 'dp', split_axis=0, concat_axis=0, tiled=True)  5.06 us
    dot_general x4, matrix products, multiply(): jnp.dot(left, direct_weight, preferred_element_type=jnp.float32)  4.28 us
  transfers between devices with their start and end apart: 15, of which 7 were waited for; matrix products, arithmetic and copies ran while one was open for 20% of the time, Pallas kernels for 0%

profile of v1, /device:TPU:0, one launch (start us, length us, event | category | flops | bytes accessed | tf_op | source)
XLA Modules:
  0.0 85.1 jit_solution(17093677551775403728)
XLA Ops:
  0.6 1.1 %copy.46 = bf16[16,2,64,128]{3,2,1,0:T(8,128)(2,1)S(1)} copy(bf16[16,2,64,128]{3,2,1,0:T(8,128)(2,1)} %param.12) | data formatting | bytes 1048576
  1.8 0.2 copy-done.2
  2.0 0.3 copy.25
  2.2 3.0 %collective-permute-start = (bf16[512,768]{0,1:T(8,128)(2,1)S(1)}, bf16[512,768]{0,1:T(8,128)(2,1)S(1)}, u32[]{:S(2)}, u32[]{:S(2)}) collective-permute-start(bf16[512,768]{0,1:T(8,128)(2,1)S(1)} %bitcast.65), channel_id=1, source_target_pairs={{0,2},{2,0},{4,6},{6,4},{8,10},{10,8},{12,14},{14,12},{1,3},{3,1},... | collective-permute-start | bytes 2359304 | tf_op jit(solution)/shard_map/ppermute | solution.py:63
  5.3 0.7 constant_dynamic-slice_fusion.3
  6.0 2.6 %collective-permute-start.1 = (bf16[128,512]{1,0:T(8,128)(2,1)}, bf16[128,512]{1,0:T(8,128)(2,1)}, u32[]{:S(2)}, u32[]{:S(2)}) collective-permute-start(bf16[128,512]{1,0:T(8,128)(2,1)} %get-tuple-element.22), channel_id=1, source_target_pairs={{0,8},{2,10},{4,12},{6,14},{8,0},{10,2},{12,4},{14,6},{1,9},{3,11}... | collective-permute-start | bytes 393224 | tf_op jit(solution)/shard_map/ppermute | solution.py:86
  8.6 1.3 %collective-permute-start.4 = (bf16[128,512]{1,0:T(8,128)(2,1)}, bf16[128,512]{1,0:T(8,128)(2,1)}, u32[]{:S(2)}, u32[]{:S(2)}) collective-permute-start(bf16[128,512]{1,0:T(8,128)(2,1)} %get-tuple-element.23), channel_id=1, source_target_pairs={{0,12},{2,14},{4,8},{6,10},{8,4},{10,6},{12,0},{14,2},{1,13},{3,15... | collective-permute-start | bytes 393224 | tf_op jit(solution)/shard_map/ppermute | solution.py:86
  9.9 0.2 collective-permute-start.7
  10.9 0.8 and_reduce_fusion
  11.6 0.7 broadcast_select_fusion.2
  12.4 0.9 %collective-permute-start.10 = (s32[8,12]{1,0:T(8,128)S(1)}, s32[8,12]{1,0:T(8,128)S(1)}, u32[]{:S(2)}, u32[]{:S(2)}) collective-permute-start(s32[8,12]{1,0:T(8,128)S(1)} %scatter.14), channel_id=1, source_target_pairs={{0,2},{2,0},{4,6},{6,4},{8,10},{10,8},{12,14},{14,12},{1,3},{3,1},... | collective-permute-start | bytes 1160 | tf_op jit(solution)/shard_map/ppermute | solution.py:50
  13.2 0.3 multiply_reduce_fusion
  13.6 0.2 multiply_cosine_fusion.1
  13.9 9.0 %collective-permute-done.10 = s32[8,12]{1,0:T(8,128)S(1)} collective-permute-done((s32[8,12]{1,0:T(8,128)S(1)}, s32[8,12]{1,0:T(8,128)S(1)}, u32[]{:S(2)}, u32[]{:S(2)}) %collective-permute-start.10) | collective-permute-done | bytes 416 | tf_op jit(solution)/shard_map/ppermute | solution.py:50
  22.9 1.9 %collective-permute-start.11 = (s32[8,12]{1,0:T(8,128)S(1)}, s32[8,12]{1,0:T(8,128)S(1)}, u32[]{:S(2)}, u32[]{:S(2)}) collective-permute-start(s32[8,12]{1,0:T(8,128)S(1)} %add.161), channel_id=1, source_target_pairs={{0,4},{2,6},{4,0},{6,2},{8,12},{10,14},{12,8},{14,10},{1,5},{3,7},... | collective-permute-start | bytes 1160 | tf_op jit(solution)/shard_map/ppermute | solution.py:50
  24.8 0.1 fusion.67
  24.9 1.7 %collective-permute-done.11 = s32[8,12]{1,0:T(8,128)S(1)} collective-permute-done((s32[8,12]{1,0:T(8,128)S(1)}, s32[8,12]{1,0:T(8,128)S(1)}, u32[]{:S(2)}, u32[]{:S(2)}) %collective-permute-start.11) | collective-permute-done | bytes 416 | tf_op jit(solution)/shard_map/ppermute | solution.py:50
  26.6 2.8 %collective-permute-start.12 = (s32[8,12]{1,0:T(8,128)S(1)}, s32[8,12]{1,0:T(8,128)S(1)}, u32[]{:S(2)}, u32[]{:S(2)}) collective-permute-start(s32[8,12]{1,0:T(8,128)S(1)} %add.162), channel_id=1, source_target_pairs={{0,8},{2,10},{4,12},{6,14},{8,0},{10,2},{12,4},{14,6},{1,9},{3,11}... | collective-permute-start | bytes 1160 | tf_op jit(solution)/shard_map/ppermute | solution.py:50
  29.4 1.7 %collective-permute-done.12 = s32[8,12]{1,0:T(8,128)S(1)} collective-permute-done((s32[8,12]{1,0:T(8,128)S(1)}, s32[8,12]{1,0:T(8,128)S(1)}, u32[]{:S(2)}, u32[]{:S(2)}) %collective-permute-start.12) | collective-permute-done | bytes 416 | tf_op jit(solution)/shard_map/ppermute | solution.py:50
  31.1 0.2 select_reduce_fusion.1
  31.3 1.3 %gather_fusion = bf16[8,2,64,128]{3,2,1,0:T(8,128)(2,1)} fusion(bf16[16,2,64,128]{3,2,1,0:T(8,128)(2,1)S(1)} %copy.46, s32[1024]{0:T(1024)S(1)} %pad_clamp_fusion), kind=kCustom, calls=%fused_computation | custom fusion | bytes 524320 | tf_op jit(solution)/shard_map/gather | solution.py:145
  32.6 6.1 %all-to-all-start = ((bf16[8,2,64,128]{3,2,1,0:T(8,128)(2,1)}), bf16[8,2,64,128]{3,2,1,0:T(8,128)(2,1)S(1)}, u32[]{:S(2)}, u32[]{:S(2)}) async-start(bf16[8,2,64,128]{3,2,1,0:T(8,128)(2,1)} %gather_fusion), calls=%async_computation | async-start | bytes 524288 | tf_op jit(solution)/shard_map/all_to_all | solution.py:146
  38.6 0.8 fusion.78
  39.7 0.2 select_reduce_fusion
  39.9 0.5 collective-permute-start.5
  40.5 6.3 %all-to-all-done = bf16[8,2,64,128]{3,2,1,0:T(8,128)(2,1)S(1)} async-done(((bf16[8,2,64,128]{3,2,1,0:T(8,128)(2,1)}), bf16[8,2,64,128]{3,2,1,0:T(8,128)(2,1)S(1)}, u32[]{:S(2)}, u32[]{:S(2)}) %all-to-all-start) | async-done | bytes 262176 | tf_op jit(solution)/shard_map/all_to_all | solution.py:146
  46.9 0.7 fusion.77
  47.6 0.2 broadcast_select_fusion.1
  47.7 1.3 %fusion.32 = f32[128,768]{1,0:T(8,128)S(1)} fusion(bf16[512,768]{0,1:T(8,128)(2,1)S(1)} %get-tuple-element.21, bf16[128,512]{1,0:T(8,128)(2,1)} %collective-permute-done.2, f32[512]{0:T(512)S(1)} %get-tuple-element.34), kind=kOutput, calls=%fused_computation.67 | convolution fusion | flops 100859904 | bytes 1312768 | tf_op jit(solution)/shard_map/dot_general | solution.py:73
  49.0 1.3 %fusion.8 = bf16[128,768]{1,0:T(8,128)(2,1)S(1)} fusion(f32[128,768]{1,0:T(8,128)S(1)} %fusion.32, bf16[512,768]{0,1:T(8,128)(2,1)S(1)} %get-tuple-element.20, bf16[128,512]{1,0:T(8,128)(2,1)} %collective-permute-done.1, f32[512]{0:T(512)S(1)} %get-tuple-element.33), kind=kOutput, calls=%fused_computation.19 | convolution fusion | flops 101056512 | bytes 1509376 | tf_op jit(solution)/shard_map/dot_general | solution.py:73
  50.3 0.6 collective-permute-start.3
  51.0 1.3 %fusion.33 = f32[128,768]{1,0:T(8,128)S(1)} fusion(bf16[512,768]{0,1:T(8,128)(2,1)S(1)} %get-tuple-element.21, bf16[128,512]{1,0:T(8,128)(2,1)} %collective-permute-done.5, f32[512]{0:T(512)S(1)} %get-tuple-element.34), kind=kOutput, calls=%fused_computation.68 | convolution fusion | flops 100859904 | bytes 1312768 | tf_op jit(solution)/shard_map/dot_general | solution.py:73
  52.3 1.3 %fusion.9 = bf16[128,768]{1,0:T(8,128)(2,1)S(1)} fusion(f32[128,768]{1,0:T(8,128)S(1)} %fusion.33, bf16[512,768]{0,1:T(8,128)(2,1)S(1)} %get-tuple-element.20, bf16[128,512]{1,0:T(8,128)(2,1)} %collective-permute-done.4, f32[512]{0:T(512)S(1)} %get-tuple-element.33), kind=kOutput, calls=%fused_computation.20 | convolution fusion | flops 101056512 | bytes 1509376 | tf_op jit(solution)/shard_map/dot_general | solution.py:73
  53.6 1.9 %collective-permute-start.6 = (bf16[128,768]{1,0:T(8,128)(2,1)S(1)}, bf16[128,768]{1,0:T(8,128)(2,1)S(1)}, u32[]{:S(2)}, u32[]{:S(2)}) collective-permute-start(bf16[128,768]{1,0:T(8,128)(2,1)S(1)} %fusion.9), channel_id=1, source_target_pairs={{0,12},{2,14},{4,8},{6,10},{8,4},{10,6},{12,0},{14,2},{1,13},{3,15... | collective-permute-start | bytes 589832 | tf_op jit(solution)/shard_map/ppermute | solution.py:91
  55.4 1.3 %fusion.34 = f32[128,768]{1,0:T(8,128)S(1)} fusion(bf16[512,768]{0,1:T(8,128)(2,1)S(1)} %get-tuple-element.21, bf16[128,512]{1,0:T(8,128)(2,1)} %collective-permute-done.8, f32[512]{0:T(512)S(1)} %get-tuple-element.34), kind=kOutput, calls=%fused_computation.69 | convolution fusion | flops 100859904 | bytes 1312768 | tf_op jit(solution)/shard_map/dot_general | solution.py:73
  56.7 1.3 %fusion.10 = bf16[128,768]{1,0:T(8,128)(2,1)S(1)} fusion(f32[128,768]{1,0:T(8,128)S(1)} %fusion.34, bf16[512,768]{0,1:T(8,128)(2,1)S(1)} %get-tuple-element.20, bf16[128,512]{1,0:T(8,128)(2,1)} %collective-permute-done.7, f32[512]{0:T(512)S(1)} %get-tuple-element.33), kind=kOutput, calls=%fused_computation.21 | convolution fusion | flops 101056512 | bytes 1509376 | tf_op jit(solution)/shard_map/dot_general | solution.py:73
  58.0 1.2 %collective-permute-start.9 = (bf16[128,768]{1,0:T(8,128)(2,1)S(1)}, bf16[128,768]{1,0:T(8,128)(2,1)S(1)}, u32[]{:S(2)}, u32[]{:S(2)}) collective-permute-start(bf16[128,768]{1,0:T(8,128)(2,1)S(1)} %fusion.10), channel_id=1, source_target_pairs={{0,4},{2,6},{4,0},{6,2},{8,12},{10,14},{12,8},{14,10},{1,5},{3,7},... | collective-permute-start | bytes 589832 | tf_op jit(solution)/shard_map/ppermute | solution.py:91
  59.2 0.4 fusion.31
  59.6 4.3 %collective-permute-done.3 = bf16[128,768]{1,0:T(8,128)(2,1)S(1)} collective-permute-done((bf16[128,768]{1,0:T(8,128)(2,1)S(1)}, bf16[128,768]{1,0:T(8,128)(2,1)S(1)}, u32[]{:S(2)}, u32[]{:S(2)}) %collective-permute-start.3) | collective-permute-done | bytes 196640 | tf_op jit(solution)/shard_map/ppermute | solution.py:91
  63.9 1.8 %collective-permute-done.9 = bf16[128,768]{1,0:T(8,128)(2,1)S(1)} collective-permute-done((bf16[128,768]{1,0:T(8,128)(2,1)S(1)}, bf16[128,768]{1,0:T(8,128)(2,1)S(1)}, u32[]{:S(2)}, u32[]{:S(2)}) %collective-permute-start.9) | collective-permute-done | bytes 196640 | tf_op jit(solution)/shard_map/ppermute | solution.py:91
  65.8 0.4 fusion.3
  66.2 0.2 copy.26
  66.4 0.2 fusion.49
  66.6 0.1 copy.28
  66.8 0.3 copy-done.4
  67.1 0.3 fusion.82
  67.4 0.3 fusion.81
  67.8 0.3 fusion.80
  68.1 0.3 fusion.79
  68.5 0.1 copy.29
  68.6 0.8 select_add_fusion
  69.4 5.1 %all-to-all-start.1 = ((bf16[8,2,64,128]{3,2,1,0:T(8,128)(2,1)}), bf16[8,2,64,128]{3,2,1,0:T(8,128)(2,1)S(1)}, u32[]{:S(2)}, u32[]{:S(2)}) async-start(bf16[8,2,64,128]{3,2,1,0:T(8,128)(2,1)} %select_add_fusion), calls=%async_computation.1 | async-start | bytes 524288 | tf_op jit(solution)/shard_map/all_to_all | solution.py:168
  74.5 0.2 fusion.15
  74.7 0.2 fusion.17
  74.9 0.3 fusion.11
  75.2 0.3 fusion.12
  75.5 0.2 fusion.19
  75.7 0.3 fusion.13
  76.0 0.2 fusion.21
  76.2 0.3 fusion.14
  76.5 0.8 copy.35
  77.3 6.2 %all-to-all-done.1 = bf16[8,2,64,128]{3,2,1,0:T(8,128)(2,1)S(1)} async-done(((bf16[8,2,64,128]{3,2,1,0:T(8,128)(2,1)}), bf16[8,2,64,128]{3,2,1,0:T(8,128)(2,1)S(1)}, u32[]{:S(2)}, u32[]{:S(2)}) %all-to-all-start.1) | async-done | bytes 262176 | tf_op jit(solution)/shard_map/all_to_all | solution.py:168
  83.6 0.8 scatter_fusion
  84.4 0.8 copy-done.1
  (52 shorter events, 0.7 us)
Async XLA Ops:
  0.6 1.3 %copy-start.2 = (bf16[512,1,6,128]{3,0,2,1:T(8,128)(2,1)S(1)}, bf16[512,1,6,128]{3,0,2,1:T(8,128)(2,1)}, u32[]{:S(2)}) copy-start(bf16[512,1,6,128]{3,0,2,1:T(8,128)(2,1)} %param.19) | copy-start | bytes 2359300
  1.9 3.3 %copy-start = (bf16[128,4096]{1,0:T(8,128)(2,1)S(1)}, bf16[128,4096]{1,0:T(8,128)(2,1)}, u32[]{:S(2)}) copy-start(bf16[128,4096]{1,0:T(8,128)(2,1)} %param.11) | copy-start | bytes 3145732
  1.9 8.9 %copy-start.9 = (s32[1,4]{1,0:T(1,128)S(1)}, s32[1,4]{1,0:T(1,128)}, u32[]{:S(2)}) copy-start(s32[1,4]{1,0:T(1,128)} %param.14) | copy-start | bytes 52
  1.9 8.9 %copy-start.8 = (s32[2]{0:T(128)S(1)}, s32[2]{0:T(128)}, u32[]{:S(2)}) copy-start(s32[2]{0:T(128)} %constant.94.clone.1) | copy-start | bytes 28
  1.9 9.7 %copy-start.5 = (s32[1,2]{1,0:T(1,128)S(1)}, s32[1,2]{1,0:T(1,128)}, u32[]{:S(2)}) copy-start(s32[1,2]{1,0:T(1,128)} %param.17) | copy-start | bytes 28
  1.9 9.7 %copy-start.6 = (s32[1,4]{1,0:T(1,128)S(1)}, s32[1,4]{1,0:T(1,128)}, u32[]{:S(2)}) copy-start(s32[1,4]{1,0:T(1,128)} %param.15) | copy-start | bytes 52
  1.9 9.7 %copy-start.7 = (s32[1,2]{1,0:T(1,128)S(1)}, s32[1,2]{1,0:T(1,128)}, u32[]{:S(2)}) copy-start(s32[1,2]{1,0:T(1,128)} %param.16) | copy-start | bytes 28
  2.2 45.3 %collective-permute-start = (bf16[512,768]{0,1:T(8,128)(2,1)S(1)}, bf16[512,768]{0,1:T(8,128)(2,1)S(1)}, u32[]{:S(2)}, u32[]{:S(2)}) collective-permute-start(bf16[512,768]{0,1:T(8,128)(2,1)S(1)} %bitcast.65), channel_id=1, source_target_pairs={{0,2},{2,0},{4,6},{6,4},{8,10},{10,8},{12,14},{14,12},{1,3},{3,1},... | collective-permute-start | bytes 2359304 | tf_op jit(solution)/shard_map/ppermute | solution.py:63
  6.0 33.9 %collective-permute-start.1 = (bf16[128,512]{1,0:T(8,128)(2,1)}, bf16[128,512]{1,0:T(8,128)(2,1)}, u32[]{:S(2)}, u32[]{:S(2)}) collective-permute-start(bf16[128,512]{1,0:T(8,128)(2,1)} %get-tuple-element.22), channel_id=1, source_target_pairs={{0,8},{2,10},{4,12},{6,14},{8,0},{10,2},{12,4},{14,6},{1,9},{3,11}... | collective-permute-start | bytes 393224 | tf_op jit(solution)/shard_map/ppermute | solution.py:86
  8.6 31.4 %collective-permute-start.4 = (bf16[128,512]{1,0:T(8,128)(2,1)}, bf16[128,512]{1,0:T(8,128)(2,1)}, u32[]{:S(2)}, u32[]{:S(2)}) collective-permute-start(bf16[128,512]{1,0:T(8,128)(2,1)} %get-tuple-element.23), channel_id=1, source_target_pairs={{0,12},{2,14},{4,8},{6,10},{8,4},{10,6},{12,0},{14,2},{1,13},{3,15... | collective-permute-start | bytes 393224 | tf_op jit(solution)/shard_map/ppermute | solution.py:86
  9.9 30.5 %collective-permute-start.7 = (bf16[128,512]{1,0:T(8,128)(2,1)}, bf16[128,512]{1,0:T(8,128)(2,1)}, u32[]{:S(2)}, u32[]{:S(2)}) collective-permute-start(bf16[128,512]{1,0:T(8,128)(2,1)} %get-tuple-element.24), channel_id=1, source_target_pairs={{0,4},{2,6},{4,0},{6,2},{8,12},{10,14},{12,8},{14,10},{1,5},{3,7},... | collective-permute-start | bytes 393224 | tf_op jit(solution)/shard_map/ppermute | solution.py:86
  12.4 10.5 %collective-permute-start.10 = (s32[8,12]{1,0:T(8,128)S(1)}, s32[8,12]{1,0:T(8,128)S(1)}, u32[]{:S(2)}, u32[]{:S(2)}) collective-permute-start(s32[8,12]{1,0:T(8,128)S(1)} %scatter.14), channel_id=1, source_target_pairs={{0,2},{2,0},{4,6},{6,4},{8,10},{10,8},{12,14},{14,12},{1,3},{3,1},... | collective-permute-start | bytes 1160 | tf_op jit(solution)/shard_map/ppermute | solution.py:50
  22.9 3.7 %collective-permute-start.11 = (s32[8,12]{1,0:T(8,128)S(1)}, s32[8,12]{1,0:T(8,128)S(1)}, u32[]{:S(2)}, u32[]{:S(2)}) collective-permute-start(s32[8,12]{1,0:T(8,128)S(1)} %add.161), channel_id=1, source_target_pairs={{0,4},{2,6},{4,0},{6,2},{8,12},{10,14},{12,8},{14,10},{1,5},{3,7},... | collective-permute-start | bytes 1160 | tf_op jit(solution)/shard_map/ppermute | solution.py:50
  26.6 4.5 %collective-permute-start.12 = (s32[8,12]{1,0:T(8,128)S(1)}, s32[8,12]{1,0:T(8,128)S(1)}, u32[]{:S(2)}, u32[]{:S(2)}) collective-permute-start(s32[8,12]{1,0:T(8,128)S(1)} %add.162), channel_id=1, source_target_pairs={{0,8},{2,10},{4,12},{6,14},{8,0},{10,2},{12,4},{14,6},{1,9},{3,11}... | collective-permute-start | bytes 1160 | tf_op jit(solution)/shard_map/ppermute | solution.py:50
  32.6 14.3 %all-to-all-start = ((bf16[8,2,64,128]{3,2,1,0:T(8,128)(2,1)}), bf16[8,2,64,128]{3,2,1,0:T(8,128)(2,1)S(1)}, u32[]{:S(2)}, u32[]{:S(2)}) async-start(bf16[8,2,64,128]{3,2,1,0:T(8,128)(2,1)} %gather_fusion), calls=%async_computation | async-start | bytes 524288 | tf_op jit(solution)/shard_map/all_to_all | solution.py:146
  39.9 7.9 %collective-permute-start.2 = (bf16[128,512]{1,0:T(8,128)(2,1)}, bf16[128,512]{1,0:T(8,128)(2,1)}, u32[]{:S(2)}, u32[]{:S(2)}) collective-permute-start(bf16[128,512]{1,0:T(8,128)(2,1)} %collective-permute-done.1), channel_id=1, source_target_pairs={{0,1},{1,0},{2,3},{3,2},{4,5},{5,4},{6,7},{7,6},{8,9},{9,8},{10,11... | collective-permute-start | bytes 393224 | tf_op jit(solution)/shard_map/ppermute | solution.py:89
  39.9 11.0 %collective-permute-start.5 = (bf16[128,512]{1,0:T(8,128)(2,1)}, bf16[128,512]{1,0:T(8,128)(2,1)}, u32[]{:S(2)}, u32[]{:S(2)}) collective-permute-start(bf16[128,512]{1,0:T(8,128)(2,1)} %collective-permute-done.4), channel_id=1, source_target_pairs={{0,1},{1,0},{2,3},{3,2},{4,5},{5,4},{6,7},{7,6},{8,9},{9,8},{10,11... | collective-permute-start | bytes 393224 | tf_op jit(solution)/shard_map/ppermute | solution.py:89
  40.4 15.0 %collective-permute-start.8 = (bf16[128,512]{1,0:T(8,128)(2,1)}, bf16[128,512]{1,0:T(8,128)(2,1)}, u32[]{:S(2)}, u32[]{:S(2)}) collective-permute-start(bf16[128,512]{1,0:T(8,128)(2,1)} %collective-permute-done.7), channel_id=1, source_target_pairs={{0,1},{1,0},{2,3},{3,2},{4,5},{5,4},{6,7},{7,6},{8,9},{9,8},{10,11... | collective-permute-start | bytes 393224 | tf_op jit(solution)/shard_map/ppermute | solution.py:89
  50.3 13.6 %collective-permute-start.3 = (bf16[128,768]{1,0:T(8,128)(2,1)S(1)}, bf16[128,768]{1,0:T(8,128)(2,1)S(1)}, u32[]{:S(2)}, u32[]{:S(2)}) collective-permute-start(bf16[128,768]{1,0:T(8,128)(2,1)S(1)} %fusion.8), channel_id=1, source_target_pairs={{0,8},{2,10},{4,12},{6,14},{8,0},{10,2},{12,4},{14,6},{1,9},{3,11}... | collective-permute-start | bytes 589832 | tf_op jit(solution)/shard_map/ppermute | solution.py:91
  53.6 10.4 %collective-permute-start.6 = (bf16[128,768]{1,0:T(8,128)(2,1)S(1)}, bf16[128,768]{1,0:T(8,128)(2,1)S(1)}, u32[]{:S(2)}, u32[]{:S(2)}) collective-permute-start(bf16[128,768]{1,0:T(8,128)(2,1)S(1)} %fusion.9), channel_id=1, source_target_pairs={{0,12},{2,14},{4,8},{6,10},{8,4},{10,6},{12,0},{14,2},{1,13},{3,15... | collective-permute-start | bytes 589832 | tf_op jit(solution)/shard_map/ppermute | solution.py:91
  58.0 7.8 %collective-permute-start.9 = (bf16[128,768]{1,0:T(8,128)(2,1)S(1)}, bf16[128,768]{1,0:T(8,128)(2,1)S(1)}, u32[]{:S(2)}, u32[]{:S(2)}) collective-permute-start(bf16[128,768]{1,0:T(8,128)(2,1)S(1)} %fusion.10), channel_id=1, source_target_pairs={{0,4},{2,6},{4,0},{6,2},{8,12},{10,14},{12,8},{14,10},{1,5},{3,7},... | collective-permute-start | bytes 589832 | tf_op jit(solution)/shard_map/ppermute | solution.py:91
  66.2 0.9 %copy-start.4 = (bf16[8,1,64,128]{3,2,1,0:T(8,128)(2,1)S(1)}, bf16[8,1,64,128]{3,2,1,0:T(8,128)(2,1)}, u32[]{:S(2)}) copy-start(bf16[8,1,64,128]{3,2,1,0:T(8,128)(2,1)} %get-tuple-element.30) | copy-start | bytes 393220
  68.5 6.4 %copy-start.3 = (bf16[8,1,64,128]{3,2,1,0:T(8,128)(2,1)S(1)}, bf16[8,1,64,128]{3,2,1,0:T(8,128)(2,1)}, u32[]{:S(2)}) copy-start(bf16[8,1,64,128]{3,2,1,0:T(8,128)(2,1)} %get-tuple-element.29) | copy-start | bytes 393220
  69.4 14.1 %all-to-all-start.1 = ((bf16[8,2,64,128]{3,2,1,0:T(8,128)(2,1)}), bf16[8,2,64,128]{3,2,1,0:T(8,128)(2,1)S(1)}, u32[]{:S(2)}, u32[]{:S(2)}) async-start(bf16[8,2,64,128]{3,2,1,0:T(8,128)(2,1)} %select_add_fusion), calls=%async_computation.1 | async-start | bytes 524288 | tf_op jit(solution)/shard_map/all_to_all | solution.py:168
  84.4 0.8 copy-start.1

commit v2 on v0

v2 whole, which is shorter than its diff:
```python
import functools
import math

import jax
import jax.numpy as jnp
from jax import lax
from jax.experimental import pallas as pl
from jax.experimental.pallas import tpu as pltpu
from jax.sharding import PartitionSpec as P

PERMUTE_LIMIT = 4
ANY = pl.BlockSpec(memory_space=pl.ANY)
SCALARS = pl.BlockSpec(memory_space=pltpu.SMEM)
VECTORS = pl.BlockSpec(memory_space=pltpu.VMEM)
PARAMS = pltpu.CompilerParams(vmem_limit_bytes=32 * 1024 * 1024)


def crossed(size, distance):
    return [(rank, rank ^ distance) for rank in range(size)]


def rotary_tables(positions, head_size):
    half_size = head_size // 2
    index_f = jnp.arange(half_size).astype(jnp.float32)
    inverse = jnp.exp(-(2.0 * index_f / head_size) * jnp.log(500000.0))
    angles = positions[:, None] * inverse[None, :]
    cosine, sine = jnp.cos(angles), jnp.sin(angles)
    return jnp.concatenate([cosine, cosine], axis=1), jnp.concatenate([-sine, sine], axis=1)


def turn(values, cosine, sine):
    return values * cosine + pltpu.roll(values, values.shape[-1] // 2, axis=1) * sine


def product_kernel(count, place, *refs):
    direct = jnp.concatenate([ref[...] for ref in refs[:count]], axis=0)
    passed = jnp.concatenate([ref[...] for ref in refs[count : 2 * count]], axis=0)
    own_weight, other_weight = refs[2 * count : 2 * count + 2]
    outs = refs[2 * count + 2 :]
    own_first = (place[0] % 2) == place[1]
    for_own = jnp.where(own_first, direct, passed)
    for_other = jnp.where(own_first, passed, direct)
    result = jnp.dot(for_own, own_weight[...], preferred_element_type=jnp.float32) + jnp.dot(
        for_other, other_weight[...], preferred_element_type=jnp.float32
    )
    rows = outs[0].shape[0]
    for index, out in enumerate(outs):
        out[...] = result[index * rows : (index + 1) * rows].astype(out.dtype)


def products(place, direct, passed, own_weight, other_weight):
    count = len(direct)
    rows, columns = direct[0].shape[0], own_weight.shape[1]
    depth = 2 * own_weight.shape[0]
    return pl.pallas_call(
        functools.partial(product_kernel, count),
        out_shape=[
            jax.ShapeDtypeStruct((rows, columns), jnp.bfloat16 if index else jnp.float32)
            for index in range(count)
        ],
        in_specs=[SCALARS] + [VECTORS] * (2 * count + 2),
        out_specs=[VECTORS] * count,
        compiler_params=PARAMS,
        cost_estimate=pl.CostEstimate(
            flops=2 * count * rows * columns * depth,
            bytes_accessed=2 * depth * (columns + count * rows) + 2 * count * rows * columns,
            transcendentals=0,
        ),
        name="products",
    )(place, *direct, *passed, own_weight, other_weight)


def project(tokens, gain, wqkv, place, ranks, head_size):
    me, core = place[0], place[1]
    rows = wqkv.shape[0]
    span = 2 * rows
    members = ranks // 2
    member = me // 2
    token_rows = tokens.shape[0]
    wide = tokens.astype(jnp.float32)
    row_scale = lax.rsqrt(jnp.mean(wide * wide, axis=-1, keepdims=True) + 1e-05)
    kv_weight = wqkv[:, 0, -2:].reshape(rows, -1)
    q_weight = wqkv[:, 0, :-2].reshape(rows, -1)
    kv_other = lax.ppermute(kv_weight, "dp", crossed(ranks, 1))
    q_other = lax.ppermute(q_weight, "dp", crossed(ranks, 1))

    if members <= PERMUTE_LIMIT:
        def half_for(target, which):
            begin = target * span + which * rows
            piece = lax.dynamic_slice(tokens, (0, begin), (token_rows, rows))
            scale = lax.dynamic_slice(gain, (begin,), (rows,))
            return (piece.astype(jnp.float32) * row_scale * scale).astype(jnp.bfloat16)

        order = [2, 3, 1] if members == 4 else list(range(1, members))
        direct = [
            lax.ppermute(half_for(member ^ step, core), "dp", crossed(ranks, 2 * step))
            for step in order
        ]
        passed = [lax.ppermute(piece, "tp", crossed(2, 1)) for piece in direct]
        direct = [half_for(member, core)] + direct
        passed = [half_for(member, 1 - core)] + passed
        results = []
        for own_weight, other_weight in ((kv_weight, kv_other), (q_weight, q_other)):
            own, *parts = products(place, direct, passed, own_weight, other_weight)
            results.append(
                (
                    own,
                    [
                        lax.ppermute(part, "dp", crossed(ranks, 2 * step))
                        for step, part in zip(order, parts)
                    ],
                )
            )
        return results

    groups = [[2 * index + side for index in range(members)] for side in range(2)]
    normed = (wide * row_scale * gain).astype(jnp.bfloat16)
    blocks = normed.reshape(token_rows, members, span).transpose(1, 0, 2)
    blocks = lax.all_to_all(
        blocks, "dp", split_axis=0, concat_axis=0, axis_index_groups=groups, tiled=True
    ).reshape(members * token_rows, span)
    side = me % 2
    weight = jnp.concatenate([kv_weight, q_weight], axis=1)
    other = jnp.concatenate([kv_other, q_other], axis=1)
    parts = jnp.dot(
        lax.dynamic_slice(blocks, (0, side * rows), (blocks.shape[0], rows)),
        weight,
        preferred_element_type=jnp.float32,
    ) + jnp.dot(
        lax.dynamic_slice(blocks, (0, (1 - side) * rows), (blocks.shape[0], rows)),
        other,
        preferred_element_type=jnp.float32,
    )
    parts = lax.all_to_all(
        parts.astype(jnp.bfloat16).reshape(members, token_rows, -1),
        "dp",
        split_axis=0,
        concat_axis=0,
        axis_index_groups=groups,
        tiled=True,
    )
    total = jnp.sum(parts.astype(jnp.float32), axis=0)
    return [(total[:, : 2 * head_size], []), (total[:, 2 * head_size :], [])]


def info_tables(info, ranks):
    pair = jnp.concatenate([info, lax.ppermute(info, "dp", crossed(ranks, 1))], axis=0)
    members = ranks // 2
    if members <= PERMUTE_LIMIT:
        return [pair] + [
            lax.ppermute(pair, "dp", crossed(ranks, 2 * step)) for step in range(1, members)
        ]
    distance = 2
    while distance < ranks:
        pair = jnp.concatenate([pair, lax.ppermute(pair, "dp", crossed(ranks, distance))], axis=0)
        distance *= 2
    return [pair]


def each_rank(tables, me, visit):
    base = 0
    for table in tables:
        count = table.shape[0]
        if count <= 8:
            for row in range(count):
                visit(table, row, me ^ (base + row))
        else:
            def step(row, carry, table=table, base=base):
                visit(table, row, me ^ (base + row))
                return carry

            lax.fori_loop(0, count, step, 0)
        base += count


def pick_kernel(tables_count, prefix, place, *refs):
    tables = refs[:tables_count]
    pool, chosen, semaphore = refs[tables_count:]
    me = place[0]

    def asked(table, row):
        slot = jnp.int32(-1)
        for page in range(prefix):
            slot = jnp.where(table[row, page] == me, table[row, prefix + page], slot)
        return slot

    def visit(act, table, row, rank):
        slot = asked(table, row)

        @pl.when(slot >= 0)
        def _():
            act(pltpu.make_async_copy(pool.at[slot], chosen.at[rank], semaphore.at[rank]))

    each_rank(tables, me, functools.partial(visit, lambda copy: copy.start()))
    each_rank(tables, me, functools.partial(visit, lambda copy: copy.wait()))


def pick_pages(place, tables, pool, ranks, prefix):
    return pl.pallas_call(
        functools.partial(pick_kernel, len(tables), prefix),
        out_shape=jax.ShapeDtypeStruct((ranks,) + pool.shape[1:], pool.dtype),
        in_specs=[SCALARS] * (1 + len(tables)) + [ANY],
        out_specs=ANY,
        scratch_shapes=[pltpu.SemaphoreType.DMA((ranks,))],
        compiler_params=PARAMS,
        name="pick_pages",
    )(place, *tables, pool)


def land_kernel(tables_count, prefix, new_pages, place, *refs):
    tables = refs[:tables_count]
    incoming, _, pool, semaphore = refs[tables_count:]
    me = place[0]

    def target(table, row):
        slot = jnp.int32(-1)
        for page in range(new_pages):
            home = table[row, 2 * prefix + page]
            slot = jnp.where(home == me, table[row, 2 * prefix + new_pages + page], slot)
        return slot

    def visit(act, table, row, rank):
        slot = target(table, row)

        @pl.when(slot >= 0)
        def _():
            act(pltpu.make_async_copy(incoming.at[rank], pool.at[slot], semaphore.at[rank]))

    each_rank(tables, me, functools.partial(visit, lambda copy: copy.start()))
    each_rank(tables, me, functools.partial(visit, lambda copy: copy.wait()))


def land_pages(place, tables, incoming, pool, prefix, new_pages):
    ranks = incoming.shape[0]
    return pl.pallas_call(
        functools.partial(land_kernel, len(tables), prefix, new_pages),
        out_shape=jax.ShapeDtypeStruct(pool.shape, pool.dtype),
        in_specs=[SCALARS] * (1 + len(tables)) + [ANY, ANY],
        out_specs=ANY,
        scratch_shapes=[pltpu.SemaphoreType.DMA((ranks,))],
        input_output_aliases={len(tables) + 2: 0},
        compiler_params=PARAMS,
        name="land_pages",
    )(place, *tables, incoming, pool)


def fresh_kernel(pieces, homes, own, *refs):
    parts = refs[:pieces]
    cosine, sine, keys, values, outgoing, pages, semaphore = refs[pieces:]
    total = own[...]
    for part in parts:
        total = total + part[...].astype(jnp.float32)
    head_size = keys.shape[1]
    keys[...] = turn(total[:, :head_size], cosine[...], sine[...]).astype(keys.dtype)
    values[...] = total[:, head_size:].astype(values.dtype)
    count, _, page_rows, _ = pages.shape
    copies = []
    for page in range(count):
        span = pl.ds(page * page_rows, page_rows)
        pages[page, 0] = keys[span, :]
        pages[page, 1] = values[span, :]
        copies.append(
            pltpu.make_async_copy(
                pages.at[page], outgoing.at[homes[0, page]], semaphore.at[page]
            )
        )
        copies[-1].start()
    for copy in copies:
        copy.wait()


def fresh_pages(homes, own, parts, cosine, sine, ranks, page_rows):
    token_rows, head_size = cosine.shape
    count = homes.shape[1]
    shape = jax.ShapeDtypeStruct((token_rows, head_size), jnp.bfloat16)
    return pl.pallas_call(
        functools.partial(fresh_kernel, len(parts)),
        out_shape=[
            shape,
            shape,
            jax.ShapeDtypeStruct((ranks, 2, page_rows, head_size), jnp.bfloat16),
        ],
        in_specs=[SCALARS] + [VECTORS] * (len(parts) + 3),
        out_specs=[VECTORS, VECTORS, ANY],
        scratch_shapes=[
            pltpu.VMEM((count, 2, page_rows, head_size), jnp.bfloat16),
            pltpu.SemaphoreType.DMA((count,)),
        ],
        compiler_params=PARAMS,
        name="fresh_pages",
    )(homes, own, *parts, cosine, sine)


def attend_kernel(pieces, together, pages_count, owners, own, *refs):
    parts = refs[:pieces]
    cosine, sine, keys_new, values_new, replies, out, keys, values = refs[pieces:]
    token_rows, head_size = keys_new.shape
    page_rows = replies.shape[2]
    prefix = owners.shape[1]
    group = own.shape[1] // head_size
    count = pages_count[0]
    scale = 1.0 / math.sqrt(head_size)
    for page in range(prefix):
        live = page < count
        source = jnp.where(live, owners[0, page], 0)
        span = pl.ds(page * page_rows, page_rows)
        keys[span, :] = replies[source, 0]
        values[span, :] = jnp.where(live, replies[source, 1], jnp.zeros_like(replies[source, 1]))
    keys[prefix * page_rows :, :] = keys_new[...]
    values[prefix * page_rows :, :] = values_new[...]
    total_rows = keys.shape[0]
    shape = (together * token_rows, total_rows)
    row = lax.broadcasted_iota(jnp.int32, shape, 0) % token_rows
    column = lax.broadcasted_iota(jnp.int32, shape, 1)
    new_column = column - prefix * page_rows
    allowed = (column < count * page_rows) | ((new_column >= 0) & (new_column <= row))
    for first in range(0, group, together):
        queries = []
        for member in range(first, first + together):
            lanes = pl.ds(member * head_size, head_size)
            total = own[:, lanes]
            for part in parts:
                total = total + part[:, lanes].astype(jnp.float32)
            queries.append(turn(total, cosine[...], sine[...]).astype(jnp.bfloat16))
        queries = jnp.concatenate(queries, axis=0)
        scores = (
            lax.dot_general(
                queries, keys[...], (((1,), (1,)), ((), ())), preferred_element_type=jnp.float32
            )
            * scale
        )
        scores = jnp.where(allowed, scores, -1e30)
        largest = jnp.max(scores, axis=1, keepdims=True)
        weights = jnp.exp(scores - largest)
        totals = jnp.sum(weights, axis=1, keepdims=True)
        summed = jnp.dot(
            weights.astype(jnp.bfloat16), values[...], preferred_element_type=jnp.float32
        )
        result = (summed / totals).astype(out.dtype)
        for index in range(together):
            out[:, pl.ds((first + index) * head_size, head_size)] = result[
                index * token_rows : (index + 1) * token_rows
            ]


def attend(pages_count, owners, own, parts, cosine, sine, keys_new, values_new, replies):
    token_rows, head_size = cosine.shape
    group = own.shape[1] // head_size
    total_rows = owners.shape[1] * replies.shape[2] + token_rows
    together = group if total_rows <= 1024 else 1
    return pl.pallas_call(
        functools.partial(attend_kernel, len(parts), together),
        out_shape=jax.ShapeDtypeStruct((token_rows, group * head_size), jnp.bfloat16),
        in_specs=[SCALARS] * 2 + [VECTORS] * (len(parts) + 6),
        out_specs=VECTORS,
        scratch_shapes=[pltpu.VMEM((total_rows, head_size), jnp.bfloat16)] * 2,
        compiler_params=PARAMS,
        cost_estimate=pl.CostEstimate(
            flops=4 * token_rows * group * head_size * total_rows,
            bytes_accessed=2 * replies.size + 4 * own.size,
            transcendentals=token_rows * group * total_rows,
        ),
        name="attend",
    )(pages_count, owners, own, *parts, cosine, sine, keys_new, values_new, replies)


def local(tokens, pool, pages_count, owners, slots, homes, home_slots, norm_attn, wqkv):
    ranks = lax.axis_size("dp")
    place = jnp.stack([lax.axis_index("dp"), lax.axis_index("tp")]).astype(jnp.int32)
    token_rows = tokens.shape[0]
    head_size = wqkv.shape[3]
    page_rows = pool.shape[2]
    prefix = owners.shape[1]
    new_pages = homes.shape[1]

    listed = jnp.arange(prefix, dtype=jnp.int32) < pages_count[0]
    info = jnp.concatenate([jnp.where(listed, owners, -1), slots, homes, home_slots], axis=1)
    tables = info_tables(info, ranks)
    (kv_own, kv_parts), (q_own, q_parts) = project(
        tokens, norm_attn, wqkv, place, ranks, head_size
    )

    chosen = pick_pages(place, tables, pool, ranks, prefix)
    replies = lax.all_to_all(chosen, "dp", split_axis=0, concat_axis=0, tiled=True)

    positions = (pages_count[0] * page_rows + jnp.arange(token_rows, dtype=jnp.int32)).astype(
        jnp.float32
    )
    cosine, sine = rotary_tables(positions, head_size)
    keys_new, values_new, outgoing = fresh_pages(
        homes, kv_own, kv_parts, cosine, sine, ranks, page_rows
    )
    incoming = lax.all_to_all(outgoing, "dp", split_axis=0, concat_axis=0, tiled=True)
    pool_out = land_pages(place, tables, incoming, pool, prefix, new_pages)
    attended = attend(
        pages_count, owners, q_own, q_parts, cosine, sine, keys_new, values_new, replies
    )
    return (attended, pool_out)


def solution(mesh):
    in_specs = (
        P(("groups", "dp"), None),
        P(("groups", "dp"), None, None, "tp"),
        P(("groups", "dp")),
        P(("groups", "dp"), None),
        P(("groups", "dp"), None),
        P(("groups", "dp"), None),
        P(("groups", "dp"), None),
        P(),
        P("dp", "tp", None, None),
    )
    out_specs = (P(("groups", "dp"), "tp"), P(("groups", "dp"), None, None, "tp"))
    return jax.shard_map(local, mesh=mesh, in_specs=in_specs, out_specs=out_specs, check_vma=False)
```

time: 153 us -> 75.7 us (0.49)
  waiting for transfers between devices: 99.9 us -> 25.9 us
  starting transfers between devices: 17.4 us -> 35.3 us
  between operations: 15 us -> 1.52 us
  Pallas kernels: 0 us -> 7.96 us
  matrix products: 7.53 us -> 0 us
  local copies, waits for them, and re-layouts: 10.1 us -> 2.73 us
    all_gather x1 -> x0, waiting for transfers between devices: 66.3 us -> none  [local(): lax.all_gather(wqkv, 'dp', axis=0, tiled=True)]
    ppermute x0 -> x18, waiting for transfers between devices: none -> 25.9 us  [the longest x6 13.8 us: project(): lax.ppermute(part, 'dp', crossed(ranks, 2 * step))]
    ppermute x0 -> x18, starting transfers between devices: none -> 25.8 us  [the longest x6 7.99 us: project(): lax.ppermute(part, 'dp', crossed(ranks, 2 * step))]
    all_to_all x1, waiting for transfers between devices: 16.1 us -> 0.01 us  [local(): lax.all_to_all(chosen, 'dp', split_axis=0, concat_axis=0, tiled=True)]
    all_to_all x2 -> x0, starting transfers between devices: 10.5 us -> none  [the longest x1 7.25 us: local(): lax.all_to_all(wanted[:, None], 'dp', split_axis=0, concat_axis=0, tiled=...]
    all_to_all x2 -> x0, waiting for transfers between devices: 10.1 us -> none  [the longest x1 5.26 us: local(): lax.all_to_all(wanted[:, None], 'dp', split_axis=0, concat_axis=0, tiled=...]
    pallas_call x0 -> x6, Pallas kernels: none -> 7.96 us  [the longest x2 2.22 us: products(): pl.pallas_call(functools.partial(product_kernel, count), out_shape=[jax.S...]
    dot_general x10 -> x0, matrix products: 7.53 us -> none  [the longest x1 4.65 us: row_adder(): jnp.dot(left, shard_piece.reshape(count_rows, -1), preferred_element_type...]
  transfers between devices with their start and end apart: 5 -> 20, of which waited for: 5 -> 11; matrix products, arithmetic and copies ran while one was open for 3% -> 2% of each run, Pallas kernels for 0% -> 9%
where the time goes in v2:
time: 75.7 us; the launch traced here: 75.3 us
  starting transfers between devices  35.3 us (47%)
  waiting for transfers between devices  25.9 us (34%)
  Pallas kernels  7.96 us (11%)
  local copies, waits for them, and re-layouts  2.73 us (4%)
  other arithmetic  1.82 us (2%)
  between operations  1.52 us (2%)
    ppermute x6, waiting for transfers between devices, project(): lax.ppermute(part, 'dp', crossed(ranks, 2 * step))  13.8 us
    ppermute x1, waiting for transfers between devices, project(): kv_other = lax.ppermute(kv_weight, 'dp', crossed(ranks, 1))  9.13 us
    ppermute x6, starting transfers between devices, project(): lax.ppermute(part, 'dp', crossed(ranks, 2 * step))  7.99 us
    ppermute x3, starting transfers between devices, info_tables(): lax.ppermute(pair, 'dp', crossed(ranks, 2 * step))  7.03 us
    ppermute x3, starting transfers between devices, project(): lax.ppermute(half_for(member ^ step, core), 'dp', crossed(ranks, 2 * step))  5.62 us
    all_to_all x1, starting transfers between devices, local(): lax.all_to_all(chosen, 'dp', split_axis=0, concat_axis=0, tiled=True)  4.8 us
    all_to_all x1, starting transfers between devices, local(): lax.all_to_all(outgoing, 'dp', split_axis=0, concat_axis=0, tiled=True)  4.73 us
    pallas_call x2, Pallas kernels, products(): pl.pallas_call(functools.partial(product_kernel, count), out_shape=[jax.S...  2.22 us
  transfers between devices with their start and end apart: 20, of which 11 were waited for; matrix products, arithmetic and copies ran while one was open for 2% of the time, Pallas kernels for 9%

profile of v2, /device:TPU:0, one launch (start us, length us, event | category | flops | bytes accessed | tf_op | source)
XLA Modules:
  0.0 75.3 jit_solution(8234996564677103328)
XLA Ops:
  0.6 0.0 copy-start.3
  0.6 0.0 copy-start.4
  0.6 1.1 %copy.23.refs_4_.refs_5_ = bf16[16,2,64,128]{3,2,1,0:T(8,128)(2,1)S(1)} copy(bf16[16,2,64,128]{3,2,1,0:T(8,128)(2,1)} %param.10) | data formatting | bytes 1048576
  1.8 0.2 copy-done.3
  2.0 0.3 multiply_reduce_fusion
  2.3 0.0 copy-done.4
  2.4 0.1 fusion.1
  2.5 0.9 %multiply_convert_fusion = (bf16[128,512]{1,0:T(8,128)(2,1)S(1)}, bf16[128,512]{1,0:T(8,128)(2,1)S(1)}, bf16[128,512]{1,0:T(8,128)(2,1)}, bf16[128,512]{1,0:T(8,128)(2,1)S(1)}, bf16[128,512]{1,0:T(8,128)(2,1)S(1)}) fusion(f32[512]{0:T(512)S(1)} %get-tuple-element.29, bf16[128,4096]{1,0:T(8,128)(2,1)S(1)} %copy-done.3, s32[]{:T(128)S(6)} %select_n.34, ...), kind=kLoop, calls=%fused_computation.3 | loop fusion | flops 1310720 | bytes 1321492 | tf_op jit(solution)/shard_map/convert_element_type | solution.py:92
  3.3 4.0 %collective-permute-start = (bf16[128,512]{1,0:T(8,128)(2,1)}, bf16[128,512]{1,0:T(8,128)(2,1)S(1)}, u32[]{:S(2)}, u32[]{:S(2)}) collective-permute-start(bf16[128,512]{1,0:T(8,128)(2,1)} %get-tuple-element.26), channel_id=1, source_target_pairs={{0,8},{2,10},{4,12},{6,14},{8,0},{10,2},{12,4},{14,6},{1,9},{3,11}... | collective-permute-start | bytes 393224 | tf_op jit(solution)/shard_map/ppermute | solution.py:96
  7.4 1.3 %collective-permute-start.1 = (bf16[128,512]{1,0:T(8,128)(2,1)S(1)}, bf16[128,512]{1,0:T(8,128)(2,1)S(1)}, u32[]{:S(2)}, u32[]{:S(2)}) collective-permute-start(bf16[128,512]{1,0:T(8,128)(2,1)S(1)} %get-tuple-element.25), channel_id=1, source_target_pairs={{0,12},{2,14},{4,8},{6,10},{8,4},{10,6},{12,0},{14,2},{1,13},{3,15... | collective-permute-start | bytes 393224 | tf_op jit(solution)/shard_map/ppermute | solution.py:96
  8.7 0.2 collective-permute-start.2
  9.6 0.0 copy-done.2
  9.6 0.1 pad_add_fusion.2
  9.7 1.5 %collective-permute-start.14 = (s32[1,12]{1,0:T(1,128)S(1)}, s32[1,12]{1,0:T(1,128)S(1)}, u32[]{:S(2)}, u32[]{:S(2)}) collective-permute-start(s32[1,12]{1,0:T(1,128)S(1)} %pad_add_fusion.2), channel_id=1, source_target_pairs={{0,2},{2,0},{4,6},{6,4},{8,10},{10,8},{12,14},{14,12},{1,3},{3,1},... | collective-permute-start | bytes 152 | tf_op jit(solution)/shard_map/ppermute | solution.py:147
  11.2 0.4 copy.12
  11.7 0.1 copy.18
  11.7 0.4 slice-done.1
  12.2 0.3 copy.13
  12.5 0.1 pad_add_fusion.1.place
  12.6 0.7 collective-permute-done.14
  13.3 0.1 pad_add_fusion.refs_0_
  13.4 1.8 %collective-permute-start.15 = (s32[2,12]{1,0:T(2,128)S(1)}, s32[2,12]{1,0:T(2,128)S(1)}, u32[]{:S(2)}, u32[]{:S(2)}) collective-permute-start(s32[2,12]{1,0:T(2,128)S(1)} %pad_add_fusion.refs_0_), channel_id=1, source_target_pairs={{0,4},{2,6},{4,0},{6,2},{8,12},{10,14},{12,8},{14,10},{1,5},{3,7},... | collective-permute-start | bytes 296 | tf_op jit(solution)/shard_map/ppermute | solution.py:151
  15.2 1.7 %collective-permute-start.16 = (s32[2,12]{1,0:T(2,128)S(1)}, s32[2,12]{1,0:T(2,128)S(1)}, u32[]{:S(2)}, u32[]{:S(2)}) collective-permute-start(s32[2,12]{1,0:T(2,128)S(1)} %pad_add_fusion.refs_0_), channel_id=1, source_target_pairs={{0,8},{2,10},{4,12},{6,14},{8,0},{10,2},{12,4},{14,6},{1,9},{3,11}... | collective-permute-start | bytes 296 | tf_op jit(solution)/shard_map/ppermute | solution.py:151
  16.8 1.1 %collective-permute-done.15.refs_1_ = s32[2,12]{1,0:T(2,128)S(1)} collective-permute-done((s32[2,12]{1,0:T(2,128)S(1)}, s32[2,12]{1,0:T(2,128)S(1)}, u32[]{:S(2)}, u32[]{:S(2)}) %collective-permute-start.15) | collective-permute-done | bytes 128 | tf_op jit(solution)/shard_map/ppermute | solution.py:151
  17.9 3.5 %collective-permute-start.17 = (s32[2,12]{1,0:T(2,128)S(1)}, s32[2,12]{1,0:T(2,128)S(1)}, u32[]{:S(2)}, u32[]{:S(2)}) collective-permute-start(s32[2,12]{1,0:T(2,128)S(1)} %pad_add_fusion.refs_0_), channel_id=1, source_target_pairs={{0,12},{2,14},{4,8},{6,10},{8,4},{10,6},{12,0},{14,2},{1,13},{3,15... | collective-permute-start | bytes 296 | tf_op jit(solution)/shard_map/ppermute | solution.py:151
  21.4 0.0 collective-permute-done.16.refs_2_
  21.4 1.5 %collective-permute-start.6 = (bf16[512,512]{1,0:T(8,128)(2,1)S(1)}, bf16[512,512]{1,0:T(8,128)(2,1)S(1)}, u32[]{:S(2)}, u32[]{:S(2)}) collective-permute-start(bf16[512,512]{1,0:T(8,128)(2,1)S(1)} %bitcast.17), channel_id=1, source_target_pairs={{0,2},{2,0},{4,6},{6,4},{8,10},{10,8},{12,14},{14,12},{1,3},{3,1},... | collective-permute-start | bytes 1572872 | tf_op jit(solution)/shard_map/ppermute | solution.py:85
  22.9 0.3 collective-permute-done.17.refs_3_
  23.3 1.5 %collective-permute-start.10 = (bf16[512,256]{1,0:T(8,128)(2,1)S(1)}, bf16[512,256]{1,0:T(8,128)(2,1)S(1)}, u32[]{:S(2)}, u32[]{:S(2)}) collective-permute-start(bf16[512,256]{1,0:T(8,128)(2,1)S(1)} %bitcast.19), channel_id=1, source_target_pairs={{0,2},{2,0},{4,6},{6,4},{8,10},{10,8},{12,14},{14,12},{1,3},{3,1},... | collective-permute-start | bytes 786440 | tf_op jit(solution)/shard_map/ppermute | solution.py:84
  24.8 1.3 %pick_pages.1 = bf16[8,2,64,128]{3,2,1,0:T(8,128)(2,1)} custom-call(s32[2]{0:T(128)S(1)} %pad_add_fusion.1.place, s32[2,12]{1,0:T(2,128)S(1)} %pad_add_fusion.refs_0_, s32[2,12]{1,0:T(2,128)S(1)} %collective-permute-done.15.refs_1_, s32[2,12]{1,0:T(2,128)S(1)} %collective-permute-done.16.refs_2_, s32[2,12]{1,0:T(2,128)S(1)} %collective-permute-done.17.refs_3_, ...), custom_call_target="tpu_custom_call" | custom-call | tf_op jit(solution)/shard_map/pick_pages/pallas_call | solution.py:199
  26.2 4.8 %all-to-all-start = ((bf16[8,2,64,128]{3,2,1,0:T(8,128)(2,1)}), bf16[8,2,64,128]{3,2,1,0:T(8,128)(2,1)S(1)}, u32[]{:S(2)}, u32[]{:S(2)}) async-start(bf16[8,2,64,128]{3,2,1,0:T(8,128)(2,1)} %pick_pages.1), calls=%async_computation | async-start | bytes 524288 | tf_op jit(solution)/shard_map/all_to_all | solution.py:384
  31.0 0.0 collective-permute-done.refs_1_
  31.0 0.1 collective-permute-start.3
  31.1 0.0 collective-permute-done.1.refs_2_
  31.1 0.5 collective-permute-start.4
  31.6 0.0 collective-permute-done.2.refs_3_
  31.6 0.1 collective-permute-start.5
  31.6 0.3 fusion
  32.0 0.4 collective-permute-done.3.refs_5_
  32.4 0.2 collective-permute-done.4.refs_6_
  32.6 0.3 collective-permute-done.5.refs_7_
  32.9 9.1 %collective-permute-done.10.refs_9_ = bf16[512,256]{1,0:T(8,128)(2,1)S(1)} collective-permute-done((bf16[512,256]{1,0:T(8,128)(2,1)S(1)}, bf16[512,256]{1,0:T(8,128)(2,1)S(1)}, u32[]{:S(2)}, u32[]{:S(2)}) %collective-permute-start.10) | collective-permute-done | bytes 262176 | tf_op jit(solution)/shard_map/ppermute | solution.py:84
  42.0 1.0 %products.3 = (f32[128,256]{1,0:T(8,128)S(1)}, bf16[128,256]{1,0:T(8,128)(2,1)S(1)}, bf16[128,256]{1,0:T(8,128)(2,1)S(1)}, bf16[128,256]{1,0:T(8,128)(2,1)S(1)}) custom-call(s32[2]{0:T(128)S(1)} %pad_add_fusion.1.place, bf16[128,512]{1,0:T(8,128)(2,1)S(1)} %get-tuple-element.27.refs_0_, bf16[128,512]{1,0:T(8,128)(2,1)S(1)} %collective-permute-done.refs_1_, ...), custom_call_target="tpu_custom_call" | custom-call | flops 268435456 | bytes 1835008 | tf_op jit(solution)/shard_map/products/pallas_call | solution.py:55
  43.0 0.1 collective-permute-start.11
  43.1 2.8 %collective-permute-start.12 = (bf16[128,256]{1,0:T(8,128)(2,1)S(1)}, bf16[128,256]{1,0:T(8,128)(2,1)S(1)}, u32[]{:S(2)}, u32[]{:S(2)}) collective-permute-start(bf16[128,256]{1,0:T(8,128)(2,1)S(1)} %get-tuple-element.19), channel_id=1, source_target_pairs={{0,12},{2,14},{4,8},{6,10},{8,4},{10,6},{12,0},{14,2},{1,13},{3,15... | collective-permute-start | bytes 196616 | tf_op jit(solution)/shard_map/ppermute | solution.py:109
  45.9 0.7 collective-permute-start.13
  46.6 0.1 pad_maximum_fusion
  46.7 2.3 %collective-permute-done.11.refs_0_ = bf16[128,256]{1,0:T(8,128)(2,1)S(1)} collective-permute-done((bf16[128,256]{1,0:T(8,128)(2,1)S(1)}, bf16[128,256]{1,0:T(8,128)(2,1)S(1)}, u32[]{:S(2)}, u32[]{:S(2)}) %collective-permute-start.11) | collective-permute-done | bytes 65568 | tf_op jit(solution)/shard_map/ppermute | solution.py:109
  49.0 0.5 collective-permute-done.12.refs_1_
  49.5 0.7 collective-permute-done.13.refs_2_
  50.2 1.3 %fresh_pages.1 = (bf16[128,128]{1,0:T(8,128)(2,1)S(1)}, bf16[128,128]{1,0:T(8,128)(2,1)S(1)}, bf16[8,2,64,128]{3,2,1,0:T(8,128)(2,1)}) custom-call(s32[1,2]{1,0:T(1,128)S(1)} %copy-done.1, f32[128,256]{1,0:T(8,128)S(1)} %get-tuple-element.17.own, bf16[128,256]{1,0:T(8,128)(2,1)S(1)} %collective-permute-done.11.refs_0_, ...), custom_call_target="tpu_custom_call" | custom-call | tf_op jit(solution)/shard_map/fresh_pages/pallas_call | solution.py:276
  51.4 0.0 all-to-all-done.refs_7_
  51.4 4.7 %all-to-all-start.1 = ((bf16[8,2,64,128]{3,2,1,0:T(8,128)(2,1)}), bf16[8,2,64,128]{3,2,1,0:T(8,128)(2,1)S(1)}, u32[]{:S(2)}, u32[]{:S(2)}) async-start(bf16[8,2,64,128]{3,2,1,0:T(8,128)(2,1)} %get-tuple-element.23), calls=%async_computation.1 | async-start | bytes 524288 | tf_op jit(solution)/shard_map/all_to_all | solution.py:393
  56.2 0.0 collective-permute-done.6.refs_9_
  56.2 1.2 %products.2 = (f32[128,512]{1,0:T(8,128)S(1)}, bf16[128,512]{1,0:T(8,128)(2,1)S(1)}, bf16[128,512]{1,0:T(8,128)(2,1)S(1)}, bf16[128,512]{1,0:T(8,128)(2,1)S(1)}) custom-call(s32[2]{0:T(128)S(1)} %pad_add_fusion.1.place, bf16[128,512]{1,0:T(8,128)(2,1)S(1)} %get-tuple-element.27.refs_0_, bf16[128,512]{1,0:T(8,128)(2,1)S(1)} %collective-permute-done.refs_1_, ...), custom_call_target="tpu_custom_call" | custom-call | flops 536870912 | bytes 2621440 | tf_op jit(solution)/shard_map/products/pallas_call | solution.py:55
  57.4 3.0 %collective-permute-start.7 = (bf16[128,512]{1,0:T(8,128)(2,1)S(1)}, bf16[128,512]{1,0:T(8,128)(2,1)S(1)}, u32[]{:S(2)}, u32[]{:S(2)}) collective-permute-start(bf16[128,512]{1,0:T(8,128)(2,1)S(1)} %get-tuple-element.14), channel_id=1, source_target_pairs={{0,8},{2,10},{4,12},{6,14},{8,0},{10,2},{12,4},{14,6},{1,9},{3,11}... | collective-permute-start | bytes 393224 | tf_op jit(solution)/shard_map/ppermute | solution.py:109
  60.4 1.5 %collective-permute-start.8 = (bf16[128,512]{1,0:T(8,128)(2,1)S(1)}, bf16[128,512]{1,0:T(8,128)(2,1)S(1)}, u32[]{:S(2)}, u32[]{:S(2)}) collective-permute-start(bf16[128,512]{1,0:T(8,128)(2,1)S(1)} %get-tuple-element.15), channel_id=1, source_target_pairs={{0,12},{2,14},{4,8},{6,10},{8,4},{10,6},{12,0},{14,2},{1,13},{3,15... | collective-permute-start | bytes 393224 | tf_op jit(solution)/shard_map/ppermute | solution.py:109
  61.9 0.0 collective-permute-start.9
  61.9 10.3 %collective-permute-done.7.refs_0_ = bf16[128,512]{1,0:T(8,128)(2,1)S(1)} collective-permute-done((bf16[128,512]{1,0:T(8,128)(2,1)S(1)}, bf16[128,512]{1,0:T(8,128)(2,1)S(1)}, u32[]{:S(2)}, u32[]{:S(2)}) %collective-permute-start.7) | collective-permute-done | bytes 131104 | tf_op jit(solution)/shard_map/ppermute | solution.py:109
  72.2 0.0 collective-permute-done.8.refs_1_
  72.2 0.0 collective-permute-done.9.refs_2_
  72.2 1.8 %attend.1 = bf16[128,512]{1,0:T(8,128)(2,1)} custom-call(s32[1]{0:T(128)} %copy.22.pages_count, s32[1,4]{1,0:T(1,128)S(1)} %copy-done.2, f32[128,512]{1,0:T(8,128)S(1)} %get-tuple-element.13.own, bf16[128,512]{1,0:T(8,128)(2,1)S(1)} %collective-permute-done.7.refs_0_, bf16[128,512]{1,0:T(8,128)(2,1)S(1)} %collective-permute-done.8.refs_1_, ...), custom_call_target="tpu_custom_call" | custom-call | flops 100663296 | bytes 524288 | tf_op jit(solution)/shard_map/attend/pallas_call | solution.py:351
  74.0 0.0 all-to-all-done.1.refs_4_
  74.0 1.3 %land_pages.1 = bf16[16,2,64,128]{3,2,1,0:T(8,128)(2,1)} custom-call(s32[2]{0:T(128)S(1)} %pad_add_fusion.1.place, s32[2,12]{1,0:T(2,128)S(1)} %pad_add_fusion.refs_0_, s32[2,12]{1,0:T(2,128)S(1)} %collective-permute-done.15.refs_1_, s32[2,12]{1,0:T(2,128)S(1)} %collective-permute-done.16.refs_2_, ...), custom_call_target="tpu_custom_call", output_to_operand_aliasing={{}: (6, {})} | custom-call | tf_op jit(solution)/shard_map/land_pages/pallas_call | solution.py:235
  (17 shorter events, 0.1 us)
Async XLA Ops:
  0.6 1.4 %copy-start.3 = (bf16[128,4096]{1,0:T(8,128)(2,1)S(1)}, bf16[128,4096]{1,0:T(8,128)(2,1)}, u32[]{:S(2)}) copy-start(bf16[128,4096]{1,0:T(8,128)(2,1)} %param.9) | copy-start | bytes 3145732
  0.6 1.7 %copy-start.4 = (f32[4096]{0:T(1024)S(1)}, f32[4096]{0:T(1024)}, u32[]{:S(2)}) copy-start(f32[4096]{0:T(1024)} %param.16) | copy-start | bytes 49156
  1.8 23.0 %copy-start = (bf16[16,2,64,128]{3,2,1,0:T(8,128)(2,1)}, bf16[16,2,64,128]{3,2,1,0:T(8,128)(2,1)S(1)}, u32[]{:S(2)}) copy-start(bf16[16,2,64,128]{3,2,1,0:T(8,128)(2,1)S(1)} %copy.23.refs_4_.refs_5_) | copy-start | bytes 1572868
  2.0 7.6 %copy-start.2 = (s32[1,4]{1,0:T(1,128)S(1)}, s32[1,4]{1,0:T(1,128)}, u32[]{:S(2)}) copy-start(s32[1,4]{1,0:T(1,128)} %owners.1) | copy-start | bytes 52
  2.0 7.6 %copy-start.1 = (s32[1,2]{1,0:T(1,128)S(1)}, s32[1,2]{1,0:T(1,128)}, u32[]{:S(2)}) copy-start(s32[1,2]{1,0:T(1,128)} %homes.1) | copy-start | bytes 28
  2.0 7.6 %copy-start.5 = (s32[1,2]{1,0:T(1,128)S(1)}, s32[1,2]{1,0:T(1,128)}, u32[]{:S(2)}) copy-start(s32[1,2]{1,0:T(1,128)} %param.15) | copy-start | bytes 28
  2.0 7.6 %copy-start.6 = (s32[1,4]{1,0:T(1,128)S(1)}, s32[1,4]{1,0:T(1,128)}, u32[]{:S(2)}) copy-start(s32[1,4]{1,0:T(1,128)} %param.13) | copy-start | bytes 52
  3.3 7.9 %slice-start = ((bf16[512,1,6,128]{3,0,2,1:T(8,128)(2,1)}), bf16[512,1,4,128]{3,0,2,1:T(8,128)(2,1)S(1)}, s32[]{:S(2)}) async-start(bf16[512,1,6,128]{3,0,2,1:T(8,128)(2,1)} %param.17), calls=%async_computation.2 | async-start | bytes 1048576 | tf_op jit(solution)/shard_map/slice | solution.py:83
  3.3 27.6 %collective-permute-start = (bf16[128,512]{1,0:T(8,128)(2,1)}, bf16[128,512]{1,0:T(8,128)(2,1)S(1)}, u32[]{:S(2)}, u32[]{:S(2)}) collective-permute-start(bf16[128,512]{1,0:T(8,128)(2,1)} %get-tuple-element.26), channel_id=1, source_target_pairs={{0,8},{2,10},{4,12},{6,14},{8,0},{10,2},{12,4},{14,6},{1,9},{3,11}... | collective-permute-start | bytes 393224 | tf_op jit(solution)/shard_map/ppermute | solution.py:96
  7.4 23.7 %collective-permute-start.1 = (bf16[128,512]{1,0:T(8,128)(2,1)S(1)}, bf16[128,512]{1,0:T(8,128)(2,1)S(1)}, u32[]{:S(2)}, u32[]{:S(2)}) collective-permute-start(bf16[128,512]{1,0:T(8,128)(2,1)S(1)} %get-tuple-element.25), channel_id=1, source_target_pairs={{0,12},{2,14},{4,8},{6,10},{8,4},{10,6},{12,0},{14,2},{1,13},{3,15... | collective-permute-start | bytes 393224 | tf_op jit(solution)/shard_map/ppermute | solution.py:96
  8.7 22.8 %collective-permute-start.2 = (bf16[128,512]{1,0:T(8,128)(2,1)S(1)}, bf16[128,512]{1,0:T(8,128)(2,1)S(1)}, u32[]{:S(2)}, u32[]{:S(2)}) collective-permute-start(bf16[128,512]{1,0:T(8,128)(2,1)S(1)} %get-tuple-element.28), channel_id=1, source_target_pairs={{0,4},{2,6},{4,0},{6,2},{8,12},{10,14},{12,8},{14,10},{1,5},{3,7},... | collective-permute-start | bytes 393224 | tf_op jit(solution)/shard_map/ppermute | solution.py:96
  9.7 3.5 %collective-permute-start.14 = (s32[1,12]{1,0:T(1,128)S(1)}, s32[1,12]{1,0:T(1,128)S(1)}, u32[]{:S(2)}, u32[]{:S(2)}) collective-permute-start(s32[1,12]{1,0:T(1,128)S(1)} %pad_add_fusion.2), channel_id=1, source_target_pairs={{0,2},{2,0},{4,6},{6,4},{8,10},{10,8},{12,14},{14,12},{1,3},{3,1},... | collective-permute-start | bytes 152 | tf_op jit(solution)/shard_map/ppermute | solution.py:147
  11.2 1.0 %slice-start.1 = ((bf16[512,1,6,128]{3,0,2,1:T(8,128)(2,1)}), bf16[512,1,2,128]{3,0,2,1:T(8,128)(2,1)S(1)}, s32[]{:S(2)}) async-start(bf16[512,1,6,128]{3,0,2,1:T(8,128)(2,1)} %param.17), calls=%async_computation.3 | async-start | bytes 524288 | tf_op jit(solution)/shard_map/slice | solution.py:82
  13.4 4.5 %collective-permute-start.15 = (s32[2,12]{1,0:T(2,128)S(1)}, s32[2,12]{1,0:T(2,128)S(1)}, u32[]{:S(2)}, u32[]{:S(2)}) collective-permute-start(s32[2,12]{1,0:T(2,128)S(1)} %pad_add_fusion.refs_0_), channel_id=1, source_target_pairs={{0,4},{2,6},{4,0},{6,2},{8,12},{10,14},{12,8},{14,10},{1,5},{3,7},... | collective-permute-start | bytes 296 | tf_op jit(solution)/shard_map/ppermute | solution.py:151
  15.2 6.3 %collective-permute-start.16 = (s32[2,12]{1,0:T(2,128)S(1)}, s32[2,12]{1,0:T(2,128)S(1)}, u32[]{:S(2)}, u32[]{:S(2)}) collective-permute-start(s32[2,12]{1,0:T(2,128)S(1)} %pad_add_fusion.refs_0_), channel_id=1, source_target_pairs={{0,8},{2,10},{4,12},{6,14},{8,0},{10,2},{12,4},{14,6},{1,9},{3,11}... | collective-permute-start | bytes 296 | tf_op jit(solution)/shard_map/ppermute | solution.py:151
  17.9 5.4 %collective-permute-start.17 = (s32[2,12]{1,0:T(2,128)S(1)}, s32[2,12]{1,0:T(2,128)S(1)}, u32[]{:S(2)}, u32[]{:S(2)}) collective-permute-start(s32[2,12]{1,0:T(2,128)S(1)} %pad_add_fusion.refs_0_), channel_id=1, source_target_pairs={{0,12},{2,14},{4,8},{6,10},{8,4},{10,6},{12,0},{14,2},{1,13},{3,15... | collective-permute-start | bytes 296 | tf_op jit(solution)/shard_map/ppermute | solution.py:151
  21.4 34.7 %collective-permute-start.6 = (bf16[512,512]{1,0:T(8,128)(2,1)S(1)}, bf16[512,512]{1,0:T(8,128)(2,1)S(1)}, u32[]{:S(2)}, u32[]{:S(2)}) collective-permute-start(bf16[512,512]{1,0:T(8,128)(2,1)S(1)} %bitcast.17), channel_id=1, source_target_pairs={{0,2},{2,0},{4,6},{6,4},{8,10},{10,8},{12,14},{14,12},{1,3},{3,1},... | collective-permute-start | bytes 1572872 | tf_op jit(solution)/shard_map/ppermute | solution.py:85
  23.3 18.8 %collective-permute-start.10 = (bf16[512,256]{1,0:T(8,128)(2,1)S(1)}, bf16[512,256]{1,0:T(8,128)(2,1)S(1)}, u32[]{:S(2)}, u32[]{:S(2)}) collective-permute-start(bf16[512,256]{1,0:T(8,128)(2,1)S(1)} %bitcast.19), channel_id=1, source_target_pairs={{0,2},{2,0},{4,6},{6,4},{8,10},{10,8},{12,14},{14,12},{1,3},{3,1},... | collective-permute-start | bytes 786440 | tf_op jit(solution)/shard_map/ppermute | solution.py:84
  26.2 25.3 %all-to-all-start = ((bf16[8,2,64,128]{3,2,1,0:T(8,128)(2,1)}), bf16[8,2,64,128]{3,2,1,0:T(8,128)(2,1)S(1)}, u32[]{:S(2)}, u32[]{:S(2)}) async-start(bf16[8,2,64,128]{3,2,1,0:T(8,128)(2,1)} %pick_pages.1), calls=%async_computation | async-start | bytes 524288 | tf_op jit(solution)/shard_map/all_to_all | solution.py:384
  31.0 1.4 %collective-permute-start.3 = (bf16[128,512]{1,0:T(8,128)(2,1)S(1)}, bf16[128,512]{1,0:T(8,128)(2,1)S(1)}, u32[]{:S(2)}, u32[]{:S(2)}) collective-permute-start(bf16[128,512]{1,0:T(8,128)(2,1)S(1)} %collective-permute-done.refs_1_), channel_id=1, source_target_pairs={{0,1},{1,0},{2,3},{3,2},{4,5},{5,4},{6,7},{7,6},{8,9},{9,8},{10,11... | collective-permute-start | bytes 393224 | tf_op jit(solution)/shard_map/ppermute | solution.py:99
  31.1 1.5 %collective-permute-start.4 = (bf16[128,512]{1,0:T(8,128)(2,1)S(1)}, bf16[128,512]{1,0:T(8,128)(2,1)S(1)}, u32[]{:S(2)}, u32[]{:S(2)}) collective-permute-start(bf16[128,512]{1,0:T(8,128)(2,1)S(1)} %collective-permute-done.1.refs_2_), channel_id=1, source_target_pairs={{0,1},{1,0},{2,3},{3,2},{4,5},{5,4},{6,7},{7,6},{8,9},{9,8},{10,11... | collective-permute-start | bytes 393224 | tf_op jit(solution)/shard_map/ppermute | solution.py:99
  31.6 1.3 %collective-permute-start.5 = (bf16[128,512]{1,0:T(8,128)(2,1)S(1)}, bf16[128,512]{1,0:T(8,128)(2,1)S(1)}, u32[]{:S(2)}, u32[]{:S(2)}) collective-permute-start(bf16[128,512]{1,0:T(8,128)(2,1)S(1)} %collective-permute-done.2.refs_3_), channel_id=1, source_target_pairs={{0,1},{1,0},{2,3},{3,2},{4,5},{5,4},{6,7},{7,6},{8,9},{9,8},{10,11... | collective-permute-start | bytes 393224 | tf_op jit(solution)/shard_map/ppermute | solution.py:99
  43.0 6.0 %collective-permute-start.11 = (bf16[128,256]{1,0:T(8,128)(2,1)S(1)}, bf16[128,256]{1,0:T(8,128)(2,1)S(1)}, u32[]{:S(2)}, u32[]{:S(2)}) collective-permute-start(bf16[128,256]{1,0:T(8,128)(2,1)S(1)} %get-tuple-element.18), channel_id=1, source_target_pairs={{0,8},{2,10},{4,12},{6,14},{8,0},{10,2},{12,4},{14,6},{1,9},{3,11}... | collective-permute-start | bytes 196616 | tf_op jit(solution)/shard_map/ppermute | solution.py:109
  43.1 6.4 %collective-permute-start.12 = (bf16[128,256]{1,0:T(8,128)(2,1)S(1)}, bf16[128,256]{1,0:T(8,128)(2,1)S(1)}, u32[]{:S(2)}, u32[]{:S(2)}) collective-permute-start(bf16[128,256]{1,0:T(8,128)(2,1)S(1)} %get-tuple-element.19), channel_id=1, source_target_pairs={{0,12},{2,14},{4,8},{6,10},{8,4},{10,6},{12,0},{14,2},{1,13},{3,15... | collective-permute-start | bytes 196616 | tf_op jit(solution)/shard_map/ppermute | solution.py:109
  45.9 4.3 %collective-permute-start.13 = (bf16[128,256]{1,0:T(8,128)(2,1)S(1)}, bf16[128,256]{1,0:T(8,128)(2,1)S(1)}, u32[]{:S(2)}, u32[]{:S(2)}) collective-permute-start(bf16[128,256]{1,0:T(8,128)(2,1)S(1)} %get-tuple-element.20), channel_id=1, source_target_pairs={{0,4},{2,6},{4,0},{6,2},{8,12},{10,14},{12,8},{14,10},{1,5},{3,7},... | collective-permute-start | bytes 196616 | tf_op jit(solution)/shard_map/ppermute | solution.py:109
  51.4 22.5 %all-to-all-start.1 = ((bf16[8,2,64,128]{3,2,1,0:T(8,128)(2,1)}), bf16[8,2,64,128]{3,2,1,0:T(8,128)(2,1)S(1)}, u32[]{:S(2)}, u32[]{:S(2)}) async-start(bf16[8,2,64,128]{3,2,1,0:T(8,128)(2,1)} %get-tuple-element.23), calls=%async_computation.1 | async-start | bytes 524288 | tf_op jit(solution)/shard_map/all_to_all | solution.py:393
  57.4 14.7 %collective-permute-start.7 = (bf16[128,512]{1,0:T(8,128)(2,1)S(1)}, bf16[128,512]{1,0:T(8,128)(2,1)S(1)}, u32[]{:S(2)}, u32[]{:S(2)}) collective-permute-start(bf16[128,512]{1,0:T(8,128)(2,1)S(1)} %get-tuple-element.14), channel_id=1, source_target_pairs={{0,8},{2,10},{4,12},{6,14},{8,0},{10,2},{12,4},{14,6},{1,9},{3,11}... | collective-permute-start | bytes 393224 | tf_op jit(solution)/shard_map/ppermute | solution.py:109
  60.4 11.7 %collective-permute-start.8 = (bf16[128,512]{1,0:T(8,128)(2,1)S(1)}, bf16[128,512]{1,0:T(8,128)(2,1)S(1)}, u32[]{:S(2)}, u32[]{:S(2)}) collective-permute-start(bf16[128,512]{1,0:T(8,128)(2,1)S(1)} %get-tuple-element.15), channel_id=1, source_target_pairs={{0,12},{2,14},{4,8},{6,10},{8,4},{10,6},{12,0},{14,2},{1,13},{3,15... | collective-permute-start | bytes 393224 | tf_op jit(solution)/shard_map/ppermute | solution.py:109
  61.9 10.3 %collective-permute-start.9 = (bf16[128,512]{1,0:T(8,128)(2,1)S(1)}, bf16[128,512]{1,0:T(8,128)(2,1)S(1)}, u32[]{:S(2)}, u32[]{:S(2)}) collective-permute-start(bf16[128,512]{1,0:T(8,128)(2,1)S(1)} %get-tuple-element.16), channel_id=1, source_target_pairs={{0,4},{2,6},{4,0},{6,2},{8,12},{10,14},{12,8},{14,10},{1,5},{3,7},... | collective-permute-start | bytes 393224 | tf_op jit(solution)/shard_map/ppermute | solution.py:109

commit v3 on v2

--- a/solution.py
+++ b/solution.py
@@ -32,7 +32,7 @@
     return values * cosine + pltpu.roll(values, values.shape[-1] // 2, axis=1) * sine
 
 
-def product_kernel(count, place, *refs):
+def product_kernel(count, columns, place, *refs):
     direct = jnp.concatenate([ref[...] for ref in refs[:count]], axis=0)
     passed = jnp.concatenate([ref[...] for ref in refs[count : 2 * count]], axis=0)
     own_weight, other_weight = refs[2 * count : 2 * count + 2]
@@ -40,20 +40,20 @@
     own_first = (place[0] % 2) == place[1]
     for_own = jnp.where(own_first, direct, passed)
     for_other = jnp.where(own_first, passed, direct)
-    result = jnp.dot(for_own, own_weight[...], preferred_element_type=jnp.float32) + jnp.dot(
-        for_other, other_weight[...], preferred_element_type=jnp.float32
-    )
+    result = jnp.dot(
+        for_own, own_weight[:, columns], preferred_element_type=jnp.float32
+    ) + jnp.dot(for_other, other_weight[:, columns], preferred_element_type=jnp.float32)
     rows = outs[0].shape[0]
     for index, out in enumerate(outs):
         out[...] = result[index * rows : (index + 1) * rows].astype(out.dtype)
 
 
-def products(place, direct, passed, own_weight, other_weight):
+def products(place, direct, passed, own_weight, other_weight, begin, columns):
     count = len(direct)
-    rows, columns = direct[0].shape[0], own_weight.shape[1]
+    rows = direct[0].shape[0]
     depth = 2 * own_weight.shape[0]
     return pl.pallas_call(
-        functools.partial(product_kernel, count),
+        functools.partial(product_kernel, count, slice(begin, begin + columns)),
         out_shape=[
             jax.ShapeDtypeStruct((rows, columns), jnp.bfloat16 if index else jnp.float32)
             for index in range(count)
@@ -70,19 +70,17 @@
     )(place, *direct, *passed, own_weight, other_weight)
 
 
-def project(tokens, gain, wqkv, place, ranks, head_size):
+def project(tokens, gain, weight, other, tables, place, ranks, head_size):
     me, core = place[0], place[1]
-    rows = wqkv.shape[0]
+    rows = weight.shape[0]
     span = 2 * rows
     members = ranks // 2
     member = me // 2
     token_rows = tokens.shape[0]
     wide = tokens.astype(jnp.float32)
     row_scale = lax.rsqrt(jnp.mean(wide * wide, axis=-1, keepdims=True) + 1e-05)
-    kv_weight = wqkv[:, 0, -2:].reshape(rows, -1)
-    q_weight = wqkv[:, 0, :-2].reshape(rows, -1)
-    kv_other = lax.ppermute(kv_weight, "dp", crossed(ranks, 1))
-    q_other = lax.ppermute(q_weight, "dp", crossed(ranks, 1))
+    kv_columns = 2 * head_size
+    q_columns = weight.shape[1] - kv_columns
 
     if members <= PERMUTE_LIMIT:
         def half_for(target, which):
@@ -92,16 +90,18 @@
             return (piece.astype(jnp.float32) * row_scale * scale).astype(jnp.bfloat16)
 
         order = [2, 3, 1] if members == 4 else list(range(1, members))
+        pieces = [half_for(member ^ step, core) for step in order]
+        pieces, _ = lax.optimization_barrier((pieces, tables))
         direct = [
-            lax.ppermute(half_for(member ^ step, core), "dp", crossed(ranks, 2 * step))
-            for step in order
+            lax.ppermute(piece, "dp", crossed(ranks, 2 * step))
+            for step, piece in zip(order, pieces)
         ]
         passed = [lax.ppermute(piece, "tp", crossed(2, 1)) for piece in direct]
         direct = [half_for(member, core)] + direct
         passed = [half_for(member, 1 - core)] + passed
         results = []
-        for own_weight, other_weight in ((kv_weight, kv_other), (q_weight, q_other)):
-            own, *parts = products(place, direct, passed, own_weight, other_weight)
+        for begin, columns in ((q_columns, kv_columns), (0, q_columns)):
+            own, *parts = products(place, direct, passed, weight, other, begin, columns)
             results.append(
                 (
                     own,
@@ -120,8 +120,6 @@
         blocks, "dp", split_axis=0, concat_axis=0, axis_index_groups=groups, tiled=True
     ).reshape(members * token_rows, span)
     side = me % 2
-    weight = jnp.concatenate([kv_weight, q_weight], axis=1)
-    other = jnp.concatenate([kv_other, q_other], axis=1)
     parts = jnp.dot(
         lax.dynamic_slice(blocks, (0, side * rows), (blocks.shape[0], rows)),
         weight,
@@ -140,11 +138,11 @@
         tiled=True,
     )
     total = jnp.sum(parts.astype(jnp.float32), axis=0)
-    return [(total[:, : 2 * head_size], []), (total[:, 2 * head_size :], [])]
-
-
-def info_tables(info, ranks):
-    pair = jnp.concatenate([info, lax.ppermute(info, "dp", crossed(ranks, 1))], axis=0)
+    return [(total[:, q_columns:], []), (total[:, :q_columns], [])]
+
+
+def info_tables(info, near, ranks):
+    pair = jnp.concatenate([info, near], axis=0)
     members = ranks // 2
     if members <= PERMUTE_LIMIT:
         return [pair] + [
@@ -203,6 +201,7 @@
         out_specs=ANY,
         scratch_shapes=[pltpu.SemaphoreType.DMA((ranks,))],
         compiler_params=PARAMS,
+        cost_estimate=pl.CostEstimate(flops=0, bytes_accessed=4 * ranks * pool[0].size, transcendentals=0),
         name="pick_pages",
     )(place, *tables, pool)
 
@@ -240,6 +239,7 @@
         scratch_shapes=[pltpu.SemaphoreType.DMA((ranks,))],
         input_output_aliases={len(tables) + 2: 0},
         compiler_params=PARAMS,
+        cost_estimate=pl.CostEstimate(flops=0, bytes_accessed=8 * pool[0].size, transcendentals=0),
         name="land_pages",
     )(place, *tables, incoming, pool)
 
@@ -287,6 +287,7 @@
             pltpu.SemaphoreType.DMA((count,)),
         ],
         compiler_params=PARAMS,
+        cost_estimate=pl.CostEstimate(flops=0, bytes_accessed=16 * token_rows * head_size, transcendentals=0),
         name="fresh_pages",
     )(homes, own, *parts, cosine, sine)
 
@@ -375,9 +376,12 @@
 
     listed = jnp.arange(prefix, dtype=jnp.int32) < pages_count[0]
     info = jnp.concatenate([jnp.where(listed, owners, -1), slots, homes, home_slots], axis=1)
-    tables = info_tables(info, ranks)
+    near = lax.ppermute(info, "dp", crossed(ranks, 1))
+    weight, near = lax.optimization_barrier((wqkv.reshape(wqkv.shape[0], -1), near))
+    other = lax.ppermute(weight, "dp", crossed(ranks, 1))
+    tables = info_tables(info, near, ranks)
     (kv_own, kv_parts), (q_own, q_parts) = project(
-        tokens, norm_attn, wqkv, place, ranks, head_size
+        tokens, norm_attn, weight, other, tables, place, ranks, head_size
     )
 
     chosen = pick_pages(place, tables, pool, ranks, prefix)

time: 75.7 us -> 72.9 us (0.963)
  starting transfers between devices: 35.3 us -> 30.1 us
  other arithmetic: 1.82 us -> 3.63 us
    ppermute x6 -> x5, waiting for transfers between devices: 9.82 us -> 1.74 us  [the longest x3 1.74 us: project(): lax.ppermute(piece, 'dp', crossed(ranks, 2 * step))]
    ppermute x6, waiting for transfers between devices: 13.8 us -> 18.5 us  [project(): lax.ppermute(part, 'dp', crossed(ranks, 2 * step))]
    ppermute x3, waiting for transfers between devices: 1.39 us -> 5.15 us  [info_tables(): lax.ppermute(pair, 'dp', crossed(ranks, 2 * step))]
    ppermute x3, starting transfers between devices: 7.03 us -> 4.39 us  [info_tables(): lax.ppermute(pair, 'dp', crossed(ranks, 2 * step))]
    ppermute x6 -> x5, starting transfers between devices: 10.2 us -> 7.61 us  [the longest x3 3.49 us: project(): lax.ppermute(piece, 'dp', crossed(ranks, 2 * step))]
    ppermute x6, starting transfers between devices: 7.99 us -> 10.4 us  [project(): lax.ppermute(part, 'dp', crossed(ranks, 2 * step))]
    all_to_all x1, starting transfers between devices: 4.8 us -> 3.42 us  [local(): lax.all_to_all(chosen, 'dp', split_axis=0, concat_axis=0, tiled=True)]
    slice x6 -> x0, local copies, waits for them, and re-layouts: 1.13 us -> none  [the longest x3 0.72 us: project(): kv_weight = wqkv[:, 0, -2:].reshape(rows, -1)]
  transfers between devices with their start and end apart: 20 -> 19, of which waited for: 11 -> 9; matrix products, arithmetic and copies ran while one was open for 2% -> 6% of each run, Pallas kernels for 9% -> 9%
where the time goes in v3:
time: 72.9 us; the launch traced here: 72.5 us
  starting transfers between devices  30.1 us (41%)
  waiting for transfers between devices  26.4 us (36%)
  Pallas kernels  7.97 us (11%)
  other arithmetic  3.63 us (5%)
  local copies, waits for them, and re-layouts  2.88 us (4%)
  between operations  1.58 us (2%)
    ppermute x6, waiting for transfers between devices, project(): lax.ppermute(part, 'dp', crossed(ranks, 2 * step))  18.5 us
    ppermute x6, starting transfers between devices, project(): lax.ppermute(part, 'dp', crossed(ranks, 2 * step))  10.4 us
    ppermute x3, waiting for transfers between devices, info_tables(): lax.ppermute(pair, 'dp', crossed(ranks, 2 * step))  5.15 us
    ppermute x3, starting transfers between devices, info_tables(): lax.ppermute(pair, 'dp', crossed(ranks, 2 * step))  4.39 us
    all_to_all x1, starting transfers between devices, local(): lax.all_to_all(outgoing, 'dp', split_axis=0, concat_axis=0, tiled=True)  3.72 us
    ppermute x3, starting transfers between devices, project(): lax.ppermute(piece, 'dp', crossed(ranks, 2 * step))  3.49 us
    all_to_all x1, starting transfers between devices, local(): lax.all_to_all(chosen, 'dp', split_axis=0, concat_axis=0, tiled=True)  3.42 us
    ppermute x1, starting transfers between devices, local(): near = lax.ppermute(info, 'dp', crossed(ranks, 1))  2.94 us
  transfers between devices with their start and end apart: 19, of which 9 were waited for; matrix products, arithmetic and copies ran while one was open for 6% of the time, Pallas kernels for 9%

profile of v3, /device:TPU:0, one launch (start us, length us, event | category | flops | bytes accessed | tf_op | source)
XLA Modules:
  0.0 72.5 jit_solution(10703365373882112924)
XLA Ops:
  0.6 0.0 copy-start.6
  0.7 0.0 copy-start.1
  0.7 0.0 copy-start.8
  0.7 1.2 %copy.20.refs_4_.refs_5_ = bf16[16,2,64,128]{3,2,1,0:T(8,128)(2,1)S(1)} copy(bf16[16,2,64,128]{3,2,1,0:T(8,128)(2,1)} %param.10) | data formatting | bytes 1048576
  2.6 0.1 pad_add_fusion.2
  2.7 0.4 copy-done.10
  3.1 2.9 %collective-permute-start = (s32[1,12]{1,0:T(1,128)S(1)}, s32[1,12]{1,0:T(1,128)S(1)}, u32[]{:S(2)}, u32[]{:S(2)}) collective-permute-start(s32[1,12]{1,0:T(1,128)S(1)} %pad_add_fusion.2), channel_id=1, source_target_pairs={{0,2},{2,0},{4,6},{6,4},{8,10},{10,8},{12,14},{14,12},{1,3},{3,1},... | collective-permute-start | bytes 152 | tf_op jit(solution)/shard_map/ppermute | solution.py:379
  6.0 0.5 multiply_exponential_fusion
  6.5 0.3 multiply_reduce_fusion
  6.8 0.0 copy-start.5
  6.8 0.6 add_rsqrt_fusion
  7.4 0.3 copy.13
  7.7 0.7 fusion.1
  8.4 0.0 collective-permute-done
  8.4 0.3 copy.15.refs_8_
  8.7 0.0 copy-start.7
  8.7 0.0 copy-start.9
  8.7 1.2 %collective-permute-start.10 = (bf16[512,768]{1,0:T(8,128)(2,1)S(1)}, bf16[512,768]{1,0:T(8,128)(2,1)S(1)}, u32[]{:S(2)}, u32[]{:S(2)}) collective-permute-start(bf16[512,768]{1,0:T(8,128)(2,1)S(1)} %copy.15.refs_8_), channel_id=1, source_target_pairs={{0,2},{2,0},{4,6},{6,4},{8,10},{10,8},{12,14},{14,12},{1,3},{3,1},... | collective-permute-start | bytes 2359304 | tf_op jit(solution)/shard_map/ppermute | solution.py:381
  9.9 1.6 %multiply_convert_fusion = (bf16[128,512]{1,0:T(8,128)(2,1)S(1)}, bf16[128,512]{1,0:T(8,128)(2,1)}, bf16[128,512]{1,0:T(8,128)(2,1)}, bf16[128,512]{1,0:T(8,128)(2,1)S(1)}, bf16[128,512]{1,0:T(8,128)(2,1)S(1)}) fusion(f32[512]{0:T(512)S(1)} %get-tuple-element.39, bf16[128,4096]{1,0:T(8,128)(2,1)S(1)} %copy-done.3, s32[]{:T(128)S(6)} %select_n.35, ...), kind=kLoop, calls=%fused_computation.1 | loop fusion | flops 1310720 | bytes 1321492 | tf_op jit(solution)/shard_map/convert_element_type | solution.py:90
  11.6 0.1 pad_add_fusion.refs_0_
  11.6 1.6 %collective-permute-start.1 = (s32[2,12]{1,0:T(2,128)S(1)}, s32[2,12]{1,0:T(2,128)S(1)}, u32[]{:S(2)}, u32[]{:S(2)}) collective-permute-start(s32[2,12]{1,0:T(2,128)S(1)} %pad_add_fusion.refs_0_), channel_id=1, source_target_pairs={{0,4},{2,6},{4,0},{6,2},{8,12},{10,14},{12,8},{14,10},{1,5},{3,7},... | collective-permute-start | bytes 296 | tf_op jit(solution)/shard_map/ppermute | solution.py:149
  13.2 2.6 %collective-permute-start.2 = (s32[2,12]{1,0:T(2,128)S(1)}, s32[2,12]{1,0:T(2,128)S(1)}, u32[]{:S(2)}, u32[]{:S(2)}) collective-permute-start(s32[2,12]{1,0:T(2,128)S(1)} %pad_add_fusion.refs_0_), channel_id=1, source_target_pairs={{0,8},{2,10},{4,12},{6,14},{8,0},{10,2},{12,4},{14,6},{1,9},{3,11}... | collective-permute-start | bytes 296 | tf_op jit(solution)/shard_map/ppermute | solution.py:149
  15.8 0.2 collective-permute-start.3
  16.0 0.0 collective-permute-done.1.refs_1_
  16.0 1.7 %collective-permute-done.2.refs_2_ = s32[2,12]{1,0:T(2,128)S(1)} collective-permute-done((s32[2,12]{1,0:T(2,128)S(1)}, s32[2,12]{1,0:T(2,128)S(1)}, u32[]{:S(2)}, u32[]{:S(2)}) %collective-permute-start.2) | collective-permute-done | bytes 128 | tf_op jit(solution)/shard_map/ppermute | solution.py:149
  17.7 3.5 %collective-permute-done.3.refs_3_ = s32[2,12]{1,0:T(2,128)S(1)} collective-permute-done((s32[2,12]{1,0:T(2,128)S(1)}, s32[2,12]{1,0:T(2,128)S(1)}, u32[]{:S(2)}, u32[]{:S(2)}) %collective-permute-start.3) | collective-permute-done | bytes 128 | tf_op jit(solution)/shard_map/ppermute | solution.py:149
  21.2 0.0 collective-permute-start.4
  21.2 1.0 %collective-permute-start.5 = (bf16[128,512]{1,0:T(8,128)(2,1)}, bf16[128,512]{1,0:T(8,128)(2,1)S(1)}, u32[]{:S(2)}, u32[]{:S(2)}) collective-permute-start(bf16[128,512]{1,0:T(8,128)(2,1)} %get-tuple-element.20), channel_id=1, source_target_pairs={{0,12},{2,14},{4,8},{6,10},{8,4},{10,6},{12,0},{14,2},{1,13},{3,15... | collective-permute-start | bytes 393224 | tf_op jit(solution)/shard_map/ppermute | solution.py:96
  22.2 2.5 %collective-permute-start.6 = (bf16[128,512]{1,0:T(8,128)(2,1)S(1)}, bf16[128,512]{1,0:T(8,128)(2,1)S(1)}, u32[]{:S(2)}, u32[]{:S(2)}) collective-permute-start(bf16[128,512]{1,0:T(8,128)(2,1)S(1)} %get-tuple-element.21), channel_id=1, source_target_pairs={{0,4},{2,6},{4,0},{6,2},{8,12},{10,14},{12,8},{14,10},{1,5},{3,7},... | collective-permute-start | bytes 393224 | tf_op jit(solution)/shard_map/ppermute | solution.py:96
  24.7 0.1 pad_add_fusion.1.place
  24.7 1.3 %pick_pages.1 = bf16[8,2,64,128]{3,2,1,0:T(8,128)(2,1)} custom-call(s32[2]{0:T(128)S(1)} %pad_add_fusion.1.place, s32[2,12]{1,0:T(2,128)S(1)} %pad_add_fusion.refs_0_, s32[2,12]{1,0:T(2,128)S(1)} %collective-permute-done.1.refs_1_, s32[2,12]{1,0:T(2,128)S(1)} %collective-permute-done.2.refs_2_, s32[2,12]{1,0:T(2,128)S(1)} %collective-permute-done.3.refs_3_, ...), custom_call_target="tpu_custom_call" | custom-call | bytes 524288 | tf_op jit(solution)/shard_map/pick_pages/pallas_call | solution.py:197
  26.1 3.4 %all-to-all-start = ((bf16[8,2,64,128]{3,2,1,0:T(8,128)(2,1)}), bf16[8,2,64,128]{3,2,1,0:T(8,128)(2,1)S(1)}, u32[]{:S(2)}, u32[]{:S(2)}) async-start(bf16[8,2,64,128]{3,2,1,0:T(8,128)(2,1)} %pick_pages.1), calls=%async_computation | async-start | bytes 524288 | tf_op jit(solution)/shard_map/all_to_all | solution.py:388
  29.5 1.1 %collective-permute-done.4.refs_1_ = bf16[128,512]{1,0:T(8,128)(2,1)S(1)} collective-permute-done((bf16[128,512]{1,0:T(8,128)(2,1)}, bf16[128,512]{1,0:T(8,128)(2,1)S(1)}, u32[]{:S(2)}, u32[]{:S(2)}) %collective-permute-start.4) | collective-permute-done | bytes 131104 | tf_op jit(solution)/shard_map/ppermute | solution.py:96
  30.6 0.0 collective-permute-start.7
  30.6 0.0 collective-permute-done.5.refs_2_
  30.6 0.5 collective-permute-start.8
  31.1 0.7 collective-permute-done.6.refs_3_
  31.8 0.0 collective-permute-start.9
  31.8 0.3 fusion
  32.1 0.0 collective-permute-done.7.refs_5_
  32.1 0.0 collective-permute-done.8.refs_6_
  32.1 1.0 %collective-permute-done.9.refs_7_ = bf16[128,512]{1,0:T(8,128)(2,1)S(1)} collective-permute-done((bf16[128,512]{1,0:T(8,128)(2,1)S(1)}, bf16[128,512]{1,0:T(8,128)(2,1)S(1)}, u32[]{:S(2)}, u32[]{:S(2)}) %collective-permute-start.9) | collective-permute-done | bytes 131104 | tf_op jit(solution)/shard_map/ppermute | solution.py:99
  33.1 0.0 collective-permute-done.10.refs_9_
  33.1 1.0 %products.3 = (f32[128,256]{1,0:T(8,128)S(1)}, bf16[128,256]{1,0:T(8,128)(2,1)S(1)}, bf16[128,256]{1,0:T(8,128)(2,1)S(1)}, bf16[128,256]{1,0:T(8,128)(2,1)S(1)}) custom-call(s32[2]{0:T(128)S(1)} %pad_add_fusion.1.place, bf16[128,512]{1,0:T(8,128)(2,1)S(1)} %get-tuple-element.37.refs_0_, bf16[128,512]{1,0:T(8,128)(2,1)S(1)} %collective-permute-done.4.refs_1_, ...), custom_call_target="tpu_custom_call" | custom-call | flops 268435456 | bytes 1835008 | tf_op jit(solution)/shard_map/products/pallas_call | solution.py:55
  34.1 5.0 %collective-permute-start.14 = (bf16[128,256]{1,0:T(8,128)(2,1)S(1)}, bf16[128,256]{1,0:T(8,128)(2,1)S(1)}, u32[]{:S(2)}, u32[]{:S(2)}) collective-permute-start(bf16[128,256]{1,0:T(8,128)(2,1)S(1)} %get-tuple-element.28), channel_id=1, source_target_pairs={{0,8},{2,10},{4,12},{6,14},{8,0},{10,2},{12,4},{14,6},{1,9},{3,11}... | collective-permute-start | bytes 196616 | tf_op jit(solution)/shard_map/ppermute | solution.py:109
  39.1 1.0 %collective-permute-start.15 = (bf16[128,256]{1,0:T(8,128)(2,1)S(1)}, bf16[128,256]{1,0:T(8,128)(2,1)S(1)}, u32[]{:S(2)}, u32[]{:S(2)}) collective-permute-start(bf16[128,256]{1,0:T(8,128)(2,1)S(1)} %get-tuple-element.29), channel_id=1, source_target_pairs={{0,12},{2,14},{4,8},{6,10},{8,4},{10,6},{12,0},{14,2},{1,13},{3,15... | collective-permute-start | bytes 196616 | tf_op jit(solution)/shard_map/ppermute | solution.py:109
  40.1 0.0 collective-permute-start.16
  40.1 0.1 pad_maximum_fusion
  40.2 3.2 %collective-permute-done.14.refs_0_ = bf16[128,256]{1,0:T(8,128)(2,1)S(1)} collective-permute-done((bf16[128,256]{1,0:T(8,128)(2,1)S(1)}, bf16[128,256]{1,0:T(8,128)(2,1)S(1)}, u32[]{:S(2)}, u32[]{:S(2)}) %collective-permute-start.14) | collective-permute-done | bytes 65568 | tf_op jit(solution)/shard_map/ppermute | solution.py:109
  43.4 2.3 %collective-permute-done.15.refs_1_ = bf16[128,256]{1,0:T(8,128)(2,1)S(1)} collective-permute-done((bf16[128,256]{1,0:T(8,128)(2,1)S(1)}, bf16[128,256]{1,0:T(8,128)(2,1)S(1)}, u32[]{:S(2)}, u32[]{:S(2)}) %collective-permute-start.15) | collective-permute-done | bytes 65568 | tf_op jit(solution)/shard_map/ppermute | solution.py:109
  45.7 0.2 collective-permute-done.16.refs_2_
  45.9 1.3 %fresh_pages.1 = (bf16[128,128]{1,0:T(8,128)(2,1)S(1)}, bf16[128,128]{1,0:T(8,128)(2,1)S(1)}, bf16[8,2,64,128]{3,2,1,0:T(8,128)(2,1)}) custom-call(s32[1,2]{1,0:T(1,128)S(1)} %copy-done.1, f32[128,256]{1,0:T(8,128)S(1)} %get-tuple-element.27.own, bf16[128,256]{1,0:T(8,128)(2,1)S(1)} %collective-permute-done.14.refs_0_, ...), custom_call_target="tpu_custom_call" | custom-call | bytes 262144 | tf_op jit(solution)/shard_map/fresh_pages/pallas_call | solution.py:276
  47.2 0.0 all-to-all-done.refs_7_
  47.2 3.7 %all-to-all-start.1 = ((bf16[8,2,64,128]{3,2,1,0:T(8,128)(2,1)}), bf16[8,2,64,128]{3,2,1,0:T(8,128)(2,1)S(1)}, u32[]{:S(2)}, u32[]{:S(2)}) async-start(bf16[8,2,64,128]{3,2,1,0:T(8,128)(2,1)} %get-tuple-element.33), calls=%async_computation.1 | async-start | bytes 524288 | tf_op jit(solution)/shard_map/all_to_all | solution.py:397
  50.9 1.3 %products.2 = (f32[128,512]{1,0:T(8,128)S(1)}, bf16[128,512]{1,0:T(8,128)(2,1)S(1)}, bf16[128,512]{1,0:T(8,128)(2,1)S(1)}, bf16[128,512]{1,0:T(8,128)(2,1)S(1)}) custom-call(s32[2]{0:T(128)S(1)} %pad_add_fusion.1.place, bf16[128,512]{1,0:T(8,128)(2,1)S(1)} %get-tuple-element.37.refs_0_, bf16[128,512]{1,0:T(8,128)(2,1)S(1)} %collective-permute-done.4.refs_1_, ...), custom_call_target="tpu_custom_call" | custom-call | flops 536870912 | bytes 2621440 | tf_op jit(solution)/shard_map/products/pallas_call | solution.py:55
  52.1 3.0 %collective-permute-start.11 = (bf16[128,512]{1,0:T(8,128)(2,1)S(1)}, bf16[128,512]{1,0:T(8,128)(2,1)S(1)}, u32[]{:S(2)}, u32[]{:S(2)}) collective-permute-start(bf16[128,512]{1,0:T(8,128)(2,1)S(1)} %get-tuple-element.24), channel_id=1, source_target_pairs={{0,8},{2,10},{4,12},{6,14},{8,0},{10,2},{12,4},{14,6},{1,9},{3,11}... | collective-permute-start | bytes 393224 | tf_op jit(solution)/shard_map/ppermute | solution.py:109
  55.1 1.5 %collective-permute-start.12 = (bf16[128,512]{1,0:T(8,128)(2,1)S(1)}, bf16[128,512]{1,0:T(8,128)(2,1)S(1)}, u32[]{:S(2)}, u32[]{:S(2)}) collective-permute-start(bf16[128,512]{1,0:T(8,128)(2,1)S(1)} %get-tuple-element.25), channel_id=1, source_target_pairs={{0,12},{2,14},{4,8},{6,10},{8,4},{10,6},{12,0},{14,2},{1,13},{3,15... | collective-permute-start | bytes 393224 | tf_op jit(solution)/shard_map/ppermute | solution.py:109
  56.6 0.0 collective-permute-start.13
  56.6 12.8 %collective-permute-done.11.refs_0_ = bf16[128,512]{1,0:T(8,128)(2,1)S(1)} collective-permute-done((bf16[128,512]{1,0:T(8,128)(2,1)S(1)}, bf16[128,512]{1,0:T(8,128)(2,1)S(1)}, u32[]{:S(2)}, u32[]{:S(2)}) %collective-permute-start.11) | collective-permute-done | bytes 131104 | tf_op jit(solution)/shard_map/ppermute | solution.py:109
  69.4 0.0 collective-permute-done.12.refs_1_
  69.4 0.0 collective-permute-done.13.refs_2_
  69.4 1.8 %attend.1 = bf16[128,512]{1,0:T(8,128)(2,1)} custom-call(s32[1]{0:T(128)} %copy.19.pages_count, s32[1,4]{1,0:T(1,128)S(1)} %copy-done.2, f32[128,512]{1,0:T(8,128)S(1)} %get-tuple-element.23.own, bf16[128,512]{1,0:T(8,128)(2,1)S(1)} %collective-permute-done.11.refs_0_, bf16[128,512]{1,0:T(8,128)(2,1)S(1)} %collective-permute-done.12.refs_1_, ...), custom_call_target="tpu_custom_call" | custom-call | flops 100663296 | bytes 524288 | tf_op jit(solution)/shard_map/attend/pallas_call | solution.py:352
  71.2 0.0 all-to-all-done.1.refs_4_
  71.2 1.3 %land_pages.1 = bf16[16,2,64,128]{3,2,1,0:T(8,128)(2,1)} custom-call(s32[2]{0:T(128)S(1)} %pad_add_fusion.1.place, s32[2,12]{1,0:T(2,128)S(1)} %pad_add_fusion.refs_0_, s32[2,12]{1,0:T(2,128)S(1)} %collective-permute-done.1.refs_1_, s32[2,12]{1,0:T(2,128)S(1)} %collective-permute-done.2.refs_2_, ...), custom_call_target="tpu_custom_call", output_to_operand_aliasing={{}: (6, {})} | custom-call | bytes 131072 | tf_op jit(solution)/shard_map/land_pages/pallas_call | solution.py:234
  (25 shorter events, 0.1 us)
Async XLA Ops:
  0.6 1.9 %copy-start.2 = (s32[1,4]{1,0:T(1,128)S(1)}, s32[1,4]{1,0:T(1,128)}, u32[]{:S(2)}) copy-start(s32[1,4]{1,0:T(1,128)} %owners.1) | copy-start | bytes 52
  0.6 1.9 %copy-start.6 = (s32[1,2]{1,0:T(1,128)S(1)}, s32[1,2]{1,0:T(1,128)}, u32[]{:S(2)}) copy-start(s32[1,2]{1,0:T(1,128)} %param.15) | copy-start | bytes 28
  0.7 1.9 %copy-start.1 = (s32[1,2]{1,0:T(1,128)S(1)}, s32[1,2]{1,0:T(1,128)}, u32[]{:S(2)}) copy-start(s32[1,2]{1,0:T(1,128)} %homes.1) | copy-start | bytes 28
  0.7 1.9 %copy-start.8 = (s32[1,4]{1,0:T(1,128)S(1)}, s32[1,4]{1,0:T(1,128)}, u32[]{:S(2)}) copy-start(s32[1,4]{1,0:T(1,128)} %param.13) | copy-start | bytes 52
  0.7 5.9 %copy-start.3 = (bf16[128,4096]{1,0:T(8,128)(2,1)S(1)}, bf16[128,4096]{1,0:T(8,128)(2,1)}, u32[]{:S(2)}) copy-start(bf16[128,4096]{1,0:T(8,128)(2,1)} %param.9) | copy-start | bytes 3145732
  0.7 6.7 %copy-start.4 = (bf16[512,1,6,128]{3,0,2,1:T(8,128)(2,1)S(1)}, bf16[512,1,6,128]{3,0,2,1:T(8,128)(2,1)}, u32[]{:S(2)}) copy-start(bf16[512,1,6,128]{3,0,2,1:T(8,128)(2,1)} %param.17) | copy-start | bytes 2359300
  1.9 22.9 %copy-start = (bf16[16,2,64,128]{3,2,1,0:T(8,128)(2,1)}, bf16[16,2,64,128]{3,2,1,0:T(8,128)(2,1)S(1)}, u32[]{:S(2)}) copy-start(bf16[16,2,64,128]{3,2,1,0:T(8,128)(2,1)S(1)} %copy.20.refs_4_.refs_5_) | copy-start | bytes 1572868
  2.6 0.5 copy-start.10
  3.1 5.4 %collective-permute-start = (s32[1,12]{1,0:T(1,128)S(1)}, s32[1,12]{1,0:T(1,128)S(1)}, u32[]{:S(2)}, u32[]{:S(2)}) collective-permute-start(s32[1,12]{1,0:T(1,128)S(1)} %pad_add_fusion.2), channel_id=1, source_target_pairs={{0,2},{2,0},{4,6},{6,4},{8,10},{10,8},{12,14},{14,12},{1,3},{3,1},... | collective-permute-start | bytes 152 | tf_op jit(solution)/shard_map/ppermute | solution.py:379
  6.8 0.9 %copy-start.5 = (f32[4096]{0:T(1024)S(1)}, f32[4096]{0:T(1024)}, u32[]{:S(2)}) copy-start(f32[4096]{0:T(1024)} %param.16) | copy-start | bytes 49156
  8.4 1.5 %copy-start.13 = (s32[1,12]{1,0:T(1,128)}, s32[1,12]{1,0:T(1,128)S(1)}, u32[]{:S(2)}) copy-start(s32[1,12]{1,0:T(1,128)S(1)} %collective-permute-done) | copy-start | bytes 148
  8.7 2.8 %copy-start.7 = (s32[1,2]{1,0:T(1,128)S(1)}, s32[1,2]{1,0:T(1,128)}, u32[]{:S(2)}) copy-start(s32[1,2]{1,0:T(1,128)} %param.15) | copy-start | bytes 28
  8.7 2.8 %copy-start.9 = (s32[1,4]{1,0:T(1,128)S(1)}, s32[1,4]{1,0:T(1,128)}, u32[]{:S(2)}) copy-start(s32[1,4]{1,0:T(1,128)} %param.13) | copy-start | bytes 52
  8.7 2.8 %copy-start.11 = (s32[1,4]{1,0:T(1,128)S(1)}, s32[1,4]{1,0:T(1,128)}, u32[]{:S(2)}) copy-start(s32[1,4]{1,0:T(1,128)} %copy-done.10) | copy-start | bytes 52
  8.7 24.4 %collective-permute-start.10 = (bf16[512,768]{1,0:T(8,128)(2,1)S(1)}, bf16[512,768]{1,0:T(8,128)(2,1)S(1)}, u32[]{:S(2)}, u32[]{:S(2)}) collective-permute-start(bf16[512,768]{1,0:T(8,128)(2,1)S(1)} %copy.15.refs_8_), channel_id=1, source_target_pairs={{0,2},{2,0},{4,6},{6,4},{8,10},{10,8},{12,14},{14,12},{1,3},{3,1},... | collective-permute-start | bytes 2359304 | tf_op jit(solution)/shard_map/ppermute | solution.py:381
  9.9 1.6 %copy-start.14 = (s32[1,12]{1,0:T(1,128)S(1)}, s32[1,12]{1,0:T(1,128)}, u32[]{:S(2)}) copy-start(s32[1,12]{1,0:T(1,128)} %copy-done.13) | copy-start | bytes 148
  11.5 20.2 %copy-start.12 = (f32[64]{0:T(128)S(1)}, f32[64]{0:T(128)}, u32[]{:S(2)}) copy-start(f32[64]{0:T(128)} %multiply_exponential_fusion) | copy-start | bytes 772
  11.6 4.4 %collective-permute-start.1 = (s32[2,12]{1,0:T(2,128)S(1)}, s32[2,12]{1,0:T(2,128)S(1)}, u32[]{:S(2)}, u32[]{:S(2)}) collective-permute-start(s32[2,12]{1,0:T(2,128)S(1)} %pad_add_fusion.refs_0_), channel_id=1, source_target_pairs={{0,4},{2,6},{4,0},{6,2},{8,12},{10,14},{12,8},{14,10},{1,5},{3,7},... | collective-permute-start | bytes 296 | tf_op jit(solution)/shard_map/ppermute | solution.py:149
  13.2 4.5 %collective-permute-start.2 = (s32[2,12]{1,0:T(2,128)S(1)}, s32[2,12]{1,0:T(2,128)S(1)}, u32[]{:S(2)}, u32[]{:S(2)}) collective-permute-start(s32[2,12]{1,0:T(2,128)S(1)} %pad_add_fusion.refs_0_), channel_id=1, source_target_pairs={{0,8},{2,10},{4,12},{6,14},{8,0},{10,2},{12,4},{14,6},{1,9},{3,11}... | collective-permute-start | bytes 296 | tf_op jit(solution)/shard_map/ppermute | solution.py:149
  15.8 5.4 %collective-permute-start.3 = (s32[2,12]{1,0:T(2,128)S(1)}, s32[2,12]{1,0:T(2,128)S(1)}, u32[]{:S(2)}, u32[]{:S(2)}) collective-permute-start(s32[2,12]{1,0:T(2,128)S(1)} %pad_add_fusion.refs_0_), channel_id=1, source_target_pairs={{0,12},{2,14},{4,8},{6,10},{8,4},{10,6},{12,0},{14,2},{1,13},{3,15... | collective-permute-start | bytes 296 | tf_op jit(solution)/shard_map/ppermute | solution.py:149
  21.2 9.4 %collective-permute-start.4 = (bf16[128,512]{1,0:T(8,128)(2,1)}, bf16[128,512]{1,0:T(8,128)(2,1)S(1)}, u32[]{:S(2)}, u32[]{:S(2)}) collective-permute-start(bf16[128,512]{1,0:T(8,128)(2,1)} %get-tuple-element.19), channel_id=1, source_target_pairs={{0,8},{2,10},{4,12},{6,14},{8,0},{10,2},{12,4},{14,6},{1,9},{3,11}... | collective-permute-start | bytes 393224 | tf_op jit(solution)/shard_map/ppermute | solution.py:96
  21.2 9.4 %collective-permute-start.5 = (bf16[128,512]{1,0:T(8,128)(2,1)}, bf16[128,512]{1,0:T(8,128)(2,1)S(1)}, u32[]{:S(2)}, u32[]{:S(2)}) collective-permute-start(bf16[128,512]{1,0:T(8,128)(2,1)} %get-tuple-element.20), channel_id=1, source_target_pairs={{0,12},{2,14},{4,8},{6,10},{8,4},{10,6},{12,0},{14,2},{1,13},{3,15... | collective-permute-start | bytes 393224 | tf_op jit(solution)/shard_map/ppermute | solution.py:96
  22.2 9.6 %collective-permute-start.6 = (bf16[128,512]{1,0:T(8,128)(2,1)S(1)}, bf16[128,512]{1,0:T(8,128)(2,1)S(1)}, u32[]{:S(2)}, u32[]{:S(2)}) collective-permute-start(bf16[128,512]{1,0:T(8,128)(2,1)S(1)} %get-tuple-element.21), channel_id=1, source_target_pairs={{0,4},{2,6},{4,0},{6,2},{8,12},{10,14},{12,8},{14,10},{1,5},{3,7},... | collective-permute-start | bytes 393224 | tf_op jit(solution)/shard_map/ppermute | solution.py:96
  26.1 21.1 %all-to-all-start = ((bf16[8,2,64,128]{3,2,1,0:T(8,128)(2,1)}), bf16[8,2,64,128]{3,2,1,0:T(8,128)(2,1)S(1)}, u32[]{:S(2)}, u32[]{:S(2)}) async-start(bf16[8,2,64,128]{3,2,1,0:T(8,128)(2,1)} %pick_pages.1), calls=%async_computation | async-start | bytes 524288 | tf_op jit(solution)/shard_map/all_to_all | solution.py:388
  30.6 1.5 %collective-permute-start.7 = (bf16[128,512]{1,0:T(8,128)(2,1)S(1)}, bf16[128,512]{1,0:T(8,128)(2,1)S(1)}, u32[]{:S(2)}, u32[]{:S(2)}) collective-permute-start(bf16[128,512]{1,0:T(8,128)(2,1)S(1)} %collective-permute-done.4.refs_1_), channel_id=1, source_target_pairs={{0,1},{1,0},{2,3},{3,2},{4,5},{5,4},{6,7},{7,6},{8,9},{9,8},{10,11... | collective-permute-start | bytes 393224 | tf_op jit(solution)/shard_map/ppermute | solution.py:99
  30.6 1.5 %collective-permute-start.8 = (bf16[128,512]{1,0:T(8,128)(2,1)S(1)}, bf16[128,512]{1,0:T(8,128)(2,1)S(1)}, u32[]{:S(2)}, u32[]{:S(2)}) collective-permute-start(bf16[128,512]{1,0:T(8,128)(2,1)S(1)} %collective-permute-done.5.refs_2_), channel_id=1, source_target_pairs={{0,1},{1,0},{2,3},{3,2},{4,5},{5,4},{6,7},{7,6},{8,9},{9,8},{10,11... | collective-permute-start | bytes 393224 | tf_op jit(solution)/shard_map/ppermute | solution.py:99
  31.8 1.3 %collective-permute-start.9 = (bf16[128,512]{1,0:T(8,128)(2,1)S(1)}, bf16[128,512]{1,0:T(8,128)(2,1)S(1)}, u32[]{:S(2)}, u32[]{:S(2)}) collective-permute-start(bf16[128,512]{1,0:T(8,128)(2,1)S(1)} %collective-permute-done.6.refs_3_), channel_id=1, source_target_pairs={{0,1},{1,0},{2,3},{3,2},{4,5},{5,4},{6,7},{7,6},{8,9},{9,8},{10,11... | collective-permute-start | bytes 393224 | tf_op jit(solution)/shard_map/ppermute | solution.py:99
  34.1 9.3 %collective-permute-start.14 = (bf16[128,256]{1,0:T(8,128)(2,1)S(1)}, bf16[128,256]{1,0:T(8,128)(2,1)S(1)}, u32[]{:S(2)}, u32[]{:S(2)}) collective-permute-start(bf16[128,256]{1,0:T(8,128)(2,1)S(1)} %get-tuple-element.28), channel_id=1, source_target_pairs={{0,8},{2,10},{4,12},{6,14},{8,0},{10,2},{12,4},{14,6},{1,9},{3,11}... | collective-permute-start | bytes 196616 | tf_op jit(solution)/shard_map/ppermute | solution.py:109
  39.1 6.6 %collective-permute-start.15 = (bf16[128,256]{1,0:T(8,128)(2,1)S(1)}, bf16[128,256]{1,0:T(8,128)(2,1)S(1)}, u32[]{:S(2)}, u32[]{:S(2)}) collective-permute-start(bf16[128,256]{1,0:T(8,128)(2,1)S(1)} %get-tuple-element.29), channel_id=1, source_target_pairs={{0,12},{2,14},{4,8},{6,10},{8,4},{10,6},{12,0},{14,2},{1,13},{3,15... | collective-permute-start | bytes 196616 | tf_op jit(solution)/shard_map/ppermute | solution.py:109
  40.1 5.8 %collective-permute-start.16 = (bf16[128,256]{1,0:T(8,128)(2,1)S(1)}, bf16[128,256]{1,0:T(8,128)(2,1)S(1)}, u32[]{:S(2)}, u32[]{:S(2)}) collective-permute-start(bf16[128,256]{1,0:T(8,128)(2,1)S(1)} %get-tuple-element.30), channel_id=1, source_target_pairs={{0,4},{2,6},{4,0},{6,2},{8,12},{10,14},{12,8},{14,10},{1,5},{3,7},... | collective-permute-start | bytes 196616 | tf_op jit(solution)/shard_map/ppermute | solution.py:109
  47.2 24.0 %all-to-all-start.1 = ((bf16[8,2,64,128]{3,2,1,0:T(8,128)(2,1)}), bf16[8,2,64,128]{3,2,1,0:T(8,128)(2,1)S(1)}, u32[]{:S(2)}, u32[]{:S(2)}) async-start(bf16[8,2,64,128]{3,2,1,0:T(8,128)(2,1)} %get-tuple-element.33), calls=%async_computation.1 | async-start | bytes 524288 | tf_op jit(solution)/shard_map/all_to_all | solution.py:397
  52.1 17.2 %collective-permute-start.11 = (bf16[128,512]{1,0:T(8,128)(2,1)S(1)}, bf16[128,512]{1,0:T(8,128)(2,1)S(1)}, u32[]{:S(2)}, u32[]{:S(2)}) collective-permute-start(bf16[128,512]{1,0:T(8,128)(2,1)S(1)} %get-tuple-element.24), channel_id=1, source_target_pairs={{0,8},{2,10},{4,12},{6,14},{8,0},{10,2},{12,4},{14,6},{1,9},{3,11}... | collective-permute-start | bytes 393224 | tf_op jit(solution)/shard_map/ppermute | solution.py:109
  55.1 14.2 %collective-permute-start.12 = (bf16[128,512]{1,0:T(8,128)(2,1)S(1)}, bf16[128,512]{1,0:T(8,128)(2,1)S(1)}, u32[]{:S(2)}, u32[]{:S(2)}) collective-permute-start(bf16[128,512]{1,0:T(8,128)(2,1)S(1)} %get-tuple-element.25), channel_id=1, source_target_pairs={{0,12},{2,14},{4,8},{6,10},{8,4},{10,6},{12,0},{14,2},{1,13},{3,15... | collective-permute-start | bytes 393224 | tf_op jit(solution)/shard_map/ppermute | solution.py:109
  56.6 12.8 %collective-permute-start.13 = (bf16[128,512]{1,0:T(8,128)(2,1)S(1)}, bf16[128,512]{1,0:T(8,128)(2,1)S(1)}, u32[]{:S(2)}, u32[]{:S(2)}) collective-permute-start(bf16[128,512]{1,0:T(8,128)(2,1)S(1)} %get-tuple-element.26), channel_id=1, source_target_pairs={{0,4},{2,6},{4,0},{6,2},{8,12},{10,14},{12,8},{14,10},{1,5},{3,7},... | collective-permute-start | bytes 393224 | tf_op jit(solution)/shard_map/ppermute | solution.py:109

commit v4 on v2

v4 whole, which is shorter than its diff:
```python
import functools
import math

import jax
import jax.numpy as jnp
from jax import lax
from jax.experimental import pallas as pl
from jax.experimental.pallas import tpu as pltpu
from jax.sharding import PartitionSpec as P

ANY = pl.BlockSpec(memory_space=pl.ANY)
SCALARS = pl.BlockSpec(memory_space=pltpu.SMEM)
VECTORS = pl.BlockSpec(memory_space=pltpu.VMEM)
PARAMS = pltpu.CompilerParams(vmem_limit_bytes=32 * 1024 * 1024)


def crossed(size, distance):
    return [(rank, rank ^ distance) for rank in range(size)]


def rotary_tables(positions, head_size):
    half_size = head_size // 2
    index_f = jnp.arange(half_size).astype(jnp.float32)
    inverse = jnp.exp(-(2.0 * index_f / head_size) * jnp.log(500000.0))
    angles = positions[:, None] * inverse[None, :]
    cosine, sine = jnp.cos(angles), jnp.sin(angles)
    return jnp.concatenate([cosine, cosine], axis=1), jnp.concatenate([-sine, sine], axis=1)


def turn(values, cosine, sine):
    return values * cosine + pltpu.roll(values, values.shape[-1] // 2, axis=1) * sine


def product_kernel(place, *refs):
    direct = jnp.concatenate([ref[...] for ref in refs[:4]], axis=0)
    passed = jnp.concatenate([ref[...] for ref in refs[4:8]], axis=0)
    own_weight, other_weight, kept, leaving = refs[8:]
    own_first = (place[0] % 2) == place[1]
    for_own = jnp.where(own_first, direct, passed)
    for_other = jnp.where(own_first, passed, direct)
    result = jnp.dot(for_own, own_weight[...], preferred_element_type=jnp.float32) + jnp.dot(
        for_other, other_weight[...], preferred_element_type=jnp.float32
    )
    rows = kept.shape[0] // 2
    kept[:rows] = result[:rows]
    kept[rows:] = result[2 * rows : 3 * rows]
    leaving[:rows] = result[rows : 2 * rows].astype(leaving.dtype)
    leaving[rows:] = result[3 * rows :].astype(leaving.dtype)


def products(place, direct, passed, own_weight, other_weight):
    rows, columns = direct[0].shape[0], own_weight.shape[1]
    depth = 2 * own_weight.shape[0]
    return pl.pallas_call(
        product_kernel,
        out_shape=[
            jax.ShapeDtypeStruct((2 * rows, columns), jnp.float32),
            jax.ShapeDtypeStruct((2 * rows, columns), jnp.bfloat16),
        ],
        in_specs=[SCALARS] + [VECTORS] * 10,
        out_specs=[VECTORS] * 2,
        compiler_params=PARAMS,
        cost_estimate=pl.CostEstimate(
            flops=8 * rows * columns * depth,
            bytes_accessed=2 * depth * (columns + 4 * rows) + 12 * rows * columns,
            transcendentals=0,
        ),
        name="products",
    )(place, *direct, *passed, own_weight, other_weight)


def fold_kernel(kept, arrived, far):
    rows = far.shape[0]
    far[...] = (kept[rows:] + arrived[rows:].astype(jnp.float32)).astype(far.dtype)


def fold(kept, arrived):
    rows, columns = kept.shape[0] // 2, kept.shape[1]
    return pl.pallas_call(
        fold_kernel,
        out_shape=jax.ShapeDtypeStruct((rows, columns), jnp.bfloat16),
        in_specs=[VECTORS] * 2,
        out_specs=VECTORS,
        compiler_params=PARAMS,
        cost_estimate=pl.CostEstimate(
            flops=rows * columns, bytes_accessed=10 * rows * columns, transcendentals=0
        ),
        name="fold",
    )(kept, arrived)


def project(tokens, gain, wqkv, place, ranks):
    me, core = place[0], place[1]
    rows = wqkv.shape[0]
    span = 2 * rows
    members = ranks // 2
    member = me // 2
    token_rows = tokens.shape[0]
    wide = tokens.astype(jnp.float32)
    row_scale = lax.rsqrt(jnp.mean(wide * wide, axis=-1, keepdims=True) + 1e-05)

    def near(weight):
        return lax.ppermute(weight, "dp", crossed(ranks, 1))

    if members == 4:
        def half_for(target, which):
            begin = target * span + which * rows
            piece = lax.dynamic_slice(tokens, (0, begin), (token_rows, rows))
            scale = lax.dynamic_slice(gain, (begin,), (rows,))
            return (piece.astype(jnp.float32) * row_scale * scale).astype(jnp.bfloat16)

        pieces = [half_for(member ^ step, core) for step in range(1, 4)]
        pieces, wqkv = lax.optimization_barrier((pieces, wqkv))
        direct = [None] * 3
        for step in (2, 3, 1):
            direct[step - 1] = lax.ppermute(pieces[step - 1], "dp", crossed(ranks, 2 * step))
        passed = [lax.ppermute(piece, "tp", crossed(2, 1)) for piece in direct]
        direct = [half_for(member, core)] + direct
        passed = [half_for(member, 1 - core)] + passed
        kv_weight = wqkv[:, 0, -2:].reshape(rows, -1)
        q_weight = wqkv[:, 0, :-2].reshape(rows, -1)
        results = []
        for weight in (kv_weight, q_weight):
            kept, leaving = products(place, direct, passed, weight, near(weight))
            arrived = lax.ppermute(leaving, "dp", crossed(ranks, 2))
            far = lax.ppermute(fold(kept, arrived), "dp", crossed(ranks, 4))
            results.append([kept, arrived, far])
        return results

    groups = [[2 * index + side for index in range(members)] for side in range(2)]
    normed = (wide * row_scale * gain).astype(jnp.bfloat16)
    blocks = normed.reshape(token_rows, members, span).transpose(1, 0, 2)
    blocks = lax.all_to_all(
        blocks, "dp", split_axis=0, concat_axis=0, axis_index_groups=groups, tiled=True
    ).reshape(members * token_rows, span)
    side = me % 2
    weight = wqkv.reshape(rows, -1)
    parts = jnp.dot(
        lax.dynamic_slice(blocks, (0, side * rows), (blocks.shape[0], rows)),
        weight,
        preferred_element_type=jnp.float32,
    ) + jnp.dot(
        lax.dynamic_slice(blocks, (0, (1 - side) * rows), (blocks.shape[0], rows)),
        near(weight),
        preferred_element_type=jnp.float32,
    )
    parts = lax.all_to_all(
        parts.astype(jnp.bfloat16).reshape(members, token_rows, -1),
        "dp",
        split_axis=0,
        concat_axis=0,
        axis_index_groups=groups,
        tiled=True,
    )
    total = jnp.sum(parts.astype(jnp.float32), axis=0)
    q_columns = weight.shape[1] - 2 * wqkv.shape[3]
    return [[total[:, q_columns:]], [total[:, :q_columns]]]


def each_rank(ranks, visit):
    if ranks <= 8:
        for rank in range(ranks):
            visit(rank)
    else:
        def step(rank, carry):
            visit(rank)
            return carry

        lax.fori_loop(0, ranks, step, 0)


def pick_kernel(table, pool, chosen, semaphore):
    ranks = chosen.shape[0]

    def visit(act, rank):
        @pl.when(table[rank, 0] >= 0)
        def _():
            act(pltpu.make_async_copy(pool.at[table[rank, 0]], chosen.at[rank], semaphore.at[rank]))

    each_rank(ranks, functools.partial(visit, lambda copy: copy.start()))
    each_rank(ranks, functools.partial(visit, lambda copy: copy.wait()))


def pick_pages(table, pool):
    ranks = table.shape[0]
    return pl.pallas_call(
        pick_kernel,
        out_shape=jax.ShapeDtypeStruct((ranks,) + pool.shape[1:], pool.dtype),
        in_specs=[SCALARS, ANY],
        out_specs=ANY,
        scratch_shapes=[pltpu.SemaphoreType.DMA((ranks,))],
        compiler_params=PARAMS,
        cost_estimate=pl.CostEstimate(
            flops=0, bytes_accessed=4 * ranks * pool[0].size, transcendentals=0
        ),
        name="pick_pages",
    )(table, pool)


def land_kernel(table, incoming, _, pool, semaphore):
    ranks = incoming.shape[0]

    def visit(act, rank):
        @pl.when(table[rank, 1] >= 0)
        def _():
            act(pltpu.make_async_copy(incoming.at[rank], pool.at[table[rank, 1]], semaphore.at[rank]))

    each_rank(ranks, functools.partial(visit, lambda copy: copy.start()))
    each_rank(ranks, functools.partial(visit, lambda copy: copy.wait()))


def land_pages(table, incoming, pool):
    ranks = incoming.shape[0]
    return pl.pallas_call(
        land_kernel,
        out_shape=jax.ShapeDtypeStruct(pool.shape, pool.dtype),
        in_specs=[SCALARS, ANY, ANY],
        out_specs=ANY,
        scratch_shapes=[pltpu.SemaphoreType.DMA((ranks,))],
        input_output_aliases={2: 0},
        compiler_params=PARAMS,
        cost_estimate=pl.CostEstimate(
            flops=0, bytes_accessed=8 * pool[0].size, transcendentals=0
        ),
        name="land_pages",
    )(table, incoming, pool)


def fresh_kernel(pieces, homes, *refs):
    parts = refs[:pieces]
    cosine, sine, keys, values, outgoing, pages, semaphore = refs[pieces:]
    token_rows, head_size = keys.shape
    total = sum(part[:token_rows].astype(jnp.float32) for part in parts)
    keys[...] = turn(total[:, :head_size], cosine[...], sine[...]).astype(keys.dtype)
    values[...] = total[:, head_size:].astype(values.dtype)
    count, _, page_rows, _ = pages.shape
    copies = []
    for page in range(count):
        span = pl.ds(page * page_rows, page_rows)
        pages[page, 0] = keys[span, :]
        pages[page, 1] = values[span, :]
        copies.append(
            pltpu.make_async_copy(
                pages.at[page], outgoing.at[homes[0, page]], semaphore.at[page]
            )
        )
        copies[-1].start()
    for copy in copies:
        copy.wait()


def fresh_pages(homes, parts, cosine, sine, ranks, page_rows):
    token_rows, head_size = cosine.shape
    count = homes.shape[1]
    shape = jax.ShapeDtypeStruct((token_rows, head_size), jnp.bfloat16)
    return pl.pallas_call(
        functools.partial(fresh_kernel, len(parts)),
        out_shape=[
            shape,
            shape,
            jax.ShapeDtypeStruct((ranks, 2, page_rows, head_size), jnp.bfloat16),
        ],
        in_specs=[SCALARS] + [VECTORS] * (len(parts) + 2),
        out_specs=[VECTORS, VECTORS, ANY],
        scratch_shapes=[
            pltpu.VMEM((count, 2, page_rows, head_size), jnp.bfloat16),
            pltpu.SemaphoreType.DMA((count,)),
        ],
        compiler_params=PARAMS,
        cost_estimate=pl.CostEstimate(flops=0, bytes_accessed=16 * token_rows * head_size, transcendentals=0),
        name="fresh_pages",
    )(homes, *parts, cosine, sine)


def attend_kernel(pieces, together, pages_count, owners, *refs):
    parts = refs[:pieces]
    cosine, sine, keys_new, values_new, replies, out, keys, values = refs[pieces:]
    token_rows, head_size = keys_new.shape
    page_rows = replies.shape[2]
    prefix = owners.shape[1]
    group = out.shape[1] // head_size
    count = pages_count[0]
    scale = 1.0 / math.sqrt(head_size)
    for page in range(prefix):
        live = page < count
        source = jnp.where(live, owners[0, page], 0)
        span = pl.ds(page * page_rows, page_rows)
        keys[span, :] = replies[source, 0]
        values[span, :] = jnp.where(live, replies[source, 1], jnp.zeros_like(replies[source, 1]))
    keys[prefix * page_rows :, :] = keys_new[...]
    values[prefix * page_rows :, :] = values_new[...]
    total_rows = keys.shape[0]
    shape = (together * token_rows, total_rows)
    row = lax.broadcasted_iota(jnp.int32, shape, 0) % token_rows
    column = lax.broadcasted_iota(jnp.int32, shape, 1)
    new_column = column - prefix * page_rows
    allowed = (column < count * page_rows) | ((new_column >= 0) & (new_column <= row))
    for first in range(0, group, together):
        queries = []
        for member in range(first, first + together):
            lanes = pl.ds(member * head_size, head_size)
            total = sum(part[:token_rows, lanes].astype(jnp.float32) for part in parts)
            queries.append(turn(total, cosine[...], sine[...]).astype(jnp.bfloat16))
        queries = jnp.concatenate(queries, axis=0)
        scores = (
            lax.dot_general(
                queries, keys[...], (((1,), (1,)), ((), ())), preferred_element_type=jnp.float32
            )
            * scale
        )
        scores = jnp.where(allowed, scores, -1e30)
        largest = jnp.max(scores, axis=1, keepdims=True)
        weights = jnp.exp(scores - largest)
        totals = jnp.sum(weights, axis=1, keepdims=True)
        summed = jnp.dot(
            weights.astype(jnp.bfloat16), values[...], preferred_element_type=jnp.float32
        )
        result = (summed / totals).astype(out.dtype)
        for index in range(together):
            out[:, pl.ds((first + index) * head_size, head_size)] = result[
                index * token_rows : (index + 1) * token_rows
            ]


def attend(pages_count, owners, parts, cosine, sine, keys_new, values_new, replies):
    token_rows, head_size = cosine.shape
    group = parts[0].shape[1] // head_size
    total_rows = owners.shape[1] * replies.shape[2] + token_rows
    together = group if total_rows <= 1024 else 1
    return pl.pallas_call(
        functools.partial(attend_kernel, len(parts), together),
        out_shape=jax.ShapeDtypeStruct((token_rows, group * head_size), jnp.bfloat16),
        in_specs=[SCALARS] * 2 + [VECTORS] * (len(parts) + 5),
        out_specs=VECTORS,
        scratch_shapes=[pltpu.VMEM((total_rows, head_size), jnp.bfloat16)] * 2,
        compiler_params=PARAMS,
        cost_estimate=pl.CostEstimate(
            flops=4 * token_rows * group * head_size * total_rows,
            bytes_accessed=2 * replies.size + 4 * parts[0].size,
            transcendentals=token_rows * group * total_rows,
        ),
        name="attend",
    )(pages_count, owners, *parts, cosine, sine, keys_new, values_new, replies)


def local(tokens, pool, pages_count, owners, slots, homes, home_slots, norm_attn, wqkv):
    ranks = lax.axis_size("dp")
    place = jnp.stack([lax.axis_index("dp"), lax.axis_index("tp")]).astype(jnp.int32)
    token_rows = tokens.shape[0]
    head_size = wqkv.shape[3]
    page_rows = pool.shape[2]
    prefix = owners.shape[1]

    lanes = jnp.arange(ranks, dtype=jnp.int32)
    listed = jnp.arange(prefix, dtype=jnp.int32) < pages_count[0]
    asks = (owners[0][None, :] == lanes[:, None]) & listed[None, :]
    lands = homes[0][None, :] == lanes[:, None]
    wanted = jnp.max(jnp.where(asks, slots, -1), axis=1)
    replaced = jnp.max(jnp.where(lands, home_slots, -1), axis=1)
    table = lax.all_to_all(
        jnp.stack([wanted, replaced], axis=1), "dp", split_axis=0, concat_axis=0, tiled=True
    )
    kv_parts, q_parts = project(tokens, norm_attn, wqkv, place, ranks)
    replies = lax.all_to_all(
        pick_pages(table, pool), "dp", split_axis=0, concat_axis=0, tiled=True
    )

    positions = (pages_count[0] * page_rows + jnp.arange(token_rows, dtype=jnp.int32)).astype(
        jnp.float32
    )
    cosine, sine = rotary_tables(positions, head_size)
    keys_new, values_new, outgoing = fresh_pages(
        homes, kv_parts, cosine, sine, ranks, page_rows
    )
    incoming = lax.all_to_all(outgoing, "dp", split_axis=0, concat_axis=0, tiled=True)
    pool_out = land_pages(table, incoming, pool)
    attended = attend(
        pages_count, owners, q_parts, cosine, sine, keys_new, values_new, replies
    )
    return (attended, pool_out)


def solution(mesh):
    in_specs = (
        P(("groups", "dp"), None),
        P(("groups", "dp"), None, None, "tp"),
        P(("groups", "dp")),
        P(("groups", "dp"), None),
        P(("groups", "dp"), None),
        P(("groups", "dp"), None),
        P(("groups", "dp"), None),
        P(),
        P("dp", "tp", None, None),
    )
    out_specs = (P(("groups", "dp"), "tp"), P(("groups", "dp"), None, None, "tp"))
    return jax.shard_map(local, mesh=mesh, in_specs=in_specs, out_specs=out_specs, check_vma=False)
```

time: 75.7 us -> 75.4 us (level)
  starting transfers between devices: 35.3 us -> 33.3 us
  waiting for transfers between devices: 25.9 us -> 27.5 us
    ppermute x15 -> x9, starting transfers between devices: 25.2 us -> 16.5 us  [the longest x3 5.68 us: project(): lax.ppermute(pieces[step - 1], 'dp', crossed(ranks, 2 * step))]
    all_to_all x1 -> x2, waiting for transfers between devices: 0.01 us -> 7.73 us  [the longest x1 7.73 us: local(): lax.all_to_all(jnp.stack([wanted, replaced], axis=1), 'dp', split_axis=0,...]
    all_to_all x1 -> x2, starting transfers between devices: 4.8 us -> 11.3 us  [the longest x1 5.7 us: local(): lax.all_to_all(pick_pages(table, pool), 'dp', split_axis=0, concat_axis=0...]
    ppermute x15 -> x9, waiting for transfers between devices: 25 us -> 19.8 us  [the longest x2 11.5 us: project(): arrived = lax.ppermute(leaving, 'dp', crossed(ranks, 2))]
    ppermute x3, waiting for transfers between devices: 0.95 us -> 0.01 us  [project(): passed = [lax.ppermute(piece, 'tp', crossed(2, 1)) for piece in direct]]
    pallas_call x4 -> x6, Pallas kernels: 4.87 us -> 4.95 us  [the longest x2 2.23 us: products(): pl.pallas_call(product_kernel, out_shape=[jax.ShapeDtypeStruct((2 * rows,...]
    unnamed x17 -> x19, local copies, waits for them, and re-layouts: 1.5 us -> 1.52 us
  transfers between devices with their start and end apart: 20 -> 15, of which waited for: 11 -> 5; matrix products, arithmetic and copies ran while one was open for 2% -> 4% of each run, Pallas kernels for 9% -> 9%
where the time goes in v4:
time: 75.4 us; the launch traced here: 75 us
  starting transfers between devices  33.3 us (44%)
  waiting for transfers between devices  27.5 us (36%)
  Pallas kernels  8.03 us (11%)
  local copies, waits for them, and re-layouts  2.98 us (4%)
  other arithmetic  1.67 us (2%)
  between operations  1.55 us (2%)
    ppermute x2, waiting for transfers between devices, project(): arrived = lax.ppermute(leaving, 'dp', crossed(ranks, 2))  11.5 us
    ppermute x2, waiting for transfers between devices, project(): far = lax.ppermute(fold(kept, arrived), 'dp', crossed(ranks, 4))  8.31 us
    all_to_all x1, waiting for transfers between devices, local(): lax.all_to_all(jnp.stack([wanted, replaced], axis=1), 'dp', split_axis=0,...  7.73 us
    all_to_all x1, starting transfers between devices, local(): lax.all_to_all(pick_pages(table, pool), 'dp', split_axis=0, concat_axis=0...  5.7 us
    ppermute x3, starting transfers between devices, project(): lax.ppermute(pieces[step - 1], 'dp', crossed(ranks, 2 * step))  5.68 us
    all_to_all x1, starting transfers between devices, local(): lax.all_to_all(jnp.stack([wanted, replaced], axis=1), 'dp', split_axis=0,...  5.6 us
    all_to_all x1, starting transfers between devices, local(): lax.all_to_all(outgoing, 'dp', split_axis=0, concat_axis=0, tiled=True)  4.91 us
    ppermute x2, starting transfers between devices, project(): arrived = lax.ppermute(leaving, 'dp', crossed(ranks, 2))  4.17 us
  transfers between devices with their start and end apart: 15, of which 5 were waited for; matrix products, arithmetic and copies ran while one was open for 4% of the time, Pallas kernels for 9%

profile of v4, /device:TPU:0, one launch (start us, length us, event | category | flops | bytes accessed | tf_op | source)
XLA Modules:
  0.0 75.0 jit_solution(8680085289563589079)
XLA Ops:
  0.6 0.0 copy-start.3
  0.6 0.0 copy-start.4
  0.6 1.1 %copy.38.pool._ = bf16[16,2,64,128]{3,2,1,0:T(8,128)(2,1)S(1)} copy(bf16[16,2,64,128]{3,2,1,0:T(8,128)(2,1)} %param.10) | data formatting | bytes 1048576
  1.8 0.2 copy-done.3
  2.0 0.3 multiply_reduce_fusion
  2.3 0.0 copy-done.4
  2.3 0.1 fusion.3
  2.4 0.2 multiply_convert_fusion
  2.7 3.1 %collective-permute-start = (bf16[128,512]{1,0:T(8,128)(2,1)S(1)}, bf16[128,512]{1,0:T(8,128)(2,1)S(1)}, u32[]{:S(2)}, u32[]{:S(2)}) collective-permute-start(bf16[128,512]{1,0:T(8,128)(2,1)S(1)} %get-tuple-element.13), channel_id=1, source_target_pairs={{0,4},{2,6},{4,0},{6,2},{8,12},{10,14},{12,8},{14,10},{1,5},{3,7},... | collective-permute-start | bytes 393224 | tf_op jit(solution)/shard_map/ppermute | solution.py:116
  5.8 2.6 %collective-permute-start.1 = (bf16[128,512]{1,0:T(8,128)(2,1)S(1)}, bf16[128,512]{1,0:T(8,128)(2,1)S(1)}, u32[]{:S(2)}, u32[]{:S(2)}) collective-permute-start(bf16[128,512]{1,0:T(8,128)(2,1)S(1)} %get-tuple-element.14), channel_id=1, source_target_pairs={{0,8},{2,10},{4,12},{6,14},{8,0},{10,2},{12,4},{14,6},{1,9},{3,11}... | collective-permute-start | bytes 393224 | tf_op jit(solution)/shard_map/ppermute | solution.py:116
  8.3 0.0 collective-permute-start.2
  8.3 0.0 slice-done
  8.4 0.4 copy.22
  8.8 0.0 slice-start.1
  8.8 0.1 copy.33
  8.9 0.0 copy-start.2
  8.9 0.0 copy-start.7
  8.9 0.0 copy-start.1
  8.9 0.0 copy-start.6
  8.9 1.8 %collective-permute-start.6 = (bf16[512,512]{1,0:T(8,128)(2,1)S(1)}, bf16[512,512]{1,0:T(8,128)(2,1)S(1)}, u32[]{:S(2)}, u32[]{:S(2)}) collective-permute-start(bf16[512,512]{1,0:T(8,128)(2,1)S(1)} %bitcast.26), channel_id=1, source_target_pairs={{0,2},{2,0},{4,6},{6,4},{8,10},{10,8},{12,14},{14,12},{1,3},{3,1},... | collective-permute-start | bytes 1572872 | tf_op jit(solution)/shard_map/ppermute | solution.py:103
  10.7 0.0 slice-done.1
  10.7 0.3 copy.23
  11.0 0.8 %collective-permute-start.9 = (bf16[512,256]{1,0:T(8,128)(2,1)S(1)}, bf16[512,256]{1,0:T(8,128)(2,1)S(1)}, u32[]{:S(2)}, u32[]{:S(2)}) collective-permute-start(bf16[512,256]{1,0:T(8,128)(2,1)S(1)} %bitcast.28), channel_id=1, source_target_pairs={{0,2},{2,0},{4,6},{6,4},{8,10},{10,8},{12,14},{14,12},{1,3},{3,1},... | collective-permute-start | bytes 786440 | tf_op jit(solution)/shard_map/ppermute | solution.py:103
  12.5 0.0 copy-done.2
  12.5 0.0 copy-done.7
  12.5 0.1 fusion.2
  12.6 0.1 select_reduce_fusion
  12.7 0.7 copy.24
  13.4 5.6 %all-to-all-start = ((s32[8,1,2]{2,1,0:T(1,128)}), s32[8,1,2]{2,1,0:T(1,128)S(1)}, u32[]{:S(2)}, u32[]{:S(2)}) async-start(s32[8,1,2]{2,1,0:T(1,128)} %copy.24), calls=%async_computation | async-start | bytes 8192 | tf_op jit(solution)/shard_map/all_to_all | solution.py:360
  19.0 0.5 multiply_exponential_fusion
  19.5 0.0 collective-permute-done.refs_1_
  19.5 0.0 collective-permute-start.3
  19.5 0.0 collective-permute-done.1.refs_2_
  19.5 0.5 collective-permute-start.4
  20.0 0.0 collective-permute-done.2.refs_3_
  20.0 0.1 collective-permute-start.5
  20.1 7.7 %all-to-all-done = s32[8,1,2]{2,1,0:T(1,128)S(1)} async-done(((s32[8,1,2]{2,1,0:T(1,128)}), s32[8,1,2]{2,1,0:T(1,128)S(1)}, u32[]{:S(2)}, u32[]{:S(2)}) %all-to-all-start) | async-done | bytes 96 | tf_op jit(solution)/shard_map/all_to_all | solution.py:360
  27.8 0.0 copy-done
  27.8 1.4 %pick_pages.1 = bf16[8,2,64,128]{3,2,1,0:T(8,128)(2,1)} custom-call(s32[8,2]{1,0:T(8,128)S(1)} %bitcast.30, bf16[16,2,64,128]{3,2,1,0:T(8,128)(2,1)S(1)} %copy.38.pool._), custom_call_target="tpu_custom_call" | custom-call | bytes 524288 | tf_op jit(solution)/shard_map/pick_pages/pallas_call | solution.py:186
  29.2 5.7 %all-to-all-start.1 = ((bf16[8,2,64,128]{3,2,1,0:T(8,128)(2,1)}), bf16[8,2,64,128]{3,2,1,0:T(8,128)(2,1)S(1)}, u32[]{:S(2)}, u32[]{:S(2)}) async-start(bf16[8,2,64,128]{3,2,1,0:T(8,128)(2,1)} %pick_pages.1), calls=%async_computation.1 | async-start | bytes 524288 | tf_op jit(solution)/shard_map/all_to_all | solution.py:364
  34.9 0.1 pad_add_fusion.place
  35.0 0.0 collective-permute-done.3.refs_5_
  35.0 0.0 collective-permute-done.4.refs_6_
  35.0 0.0 collective-permute-done.5.refs_7_
  35.0 0.0 collective-permute-done.9.refs_9_
  35.0 1.0 %products.3 = (f32[256,256]{1,0:T(8,128)S(1)}, bf16[256,256]{1,0:T(8,128)(2,1)S(1)}) custom-call(s32[2]{0:T(128)S(1)} %pad_add_fusion.place, bf16[128,512]{1,0:T(8,128)(2,1)S(1)} %get-tuple-element.27.refs_0_, bf16[128,512]{1,0:T(8,128)(2,1)S(1)} %collective-permute-done.refs_1_, bf16[128,512]{1,0:T(8,128)(2,1)S(1)} %collective-permute-done.1.refs_2_, ...), custom_call_target="tpu_custom_call" | custom-call | flops 268435456 | bytes 1966080 | tf_op jit(solution)/shard_map/products/pallas_call | solution.py:54
  36.0 2.1 %collective-permute-start.10 = (bf16[256,256]{1,0:T(8,128)(2,1)S(1)}, bf16[256,256]{1,0:T(8,128)(2,1)S(1)}, u32[]{:S(2)}, u32[]{:S(2)}) collective-permute-start(bf16[256,256]{1,0:T(8,128)(2,1)S(1)} %get-tuple-element.20), channel_id=1, source_target_pairs={{0,4},{2,6},{4,0},{6,2},{8,12},{10,14},{12,8},{14,10},{1,5},{3,7},... | collective-permute-start | bytes 393224 | tf_op jit(solution)/shard_map/ppermute | solution.py:125
  38.1 0.3 fusion
  38.4 4.3 %collective-permute-done.10.arrived.refs_1_ = bf16[256,256]{1,0:T(8,128)(2,1)S(1)} collective-permute-done((bf16[256,256]{1,0:T(8,128)(2,1)S(1)}, bf16[256,256]{1,0:T(8,128)(2,1)S(1)}, u32[]{:S(2)}, u32[]{:S(2)}) %collective-permute-start.10) | collective-permute-done | bytes 131104 | tf_op jit(solution)/shard_map/ppermute | solution.py:125
  42.7 2.2 %collective-permute-start.11 = (bf16[128,256]{1,0:T(8,128)(2,1)S(1)}, bf16[128,256]{1,0:T(8,128)(2,1)S(1)}, u32[]{:S(2)}, u32[]{:S(2)}) collective-permute-start(bf16[128,256]{1,0:T(8,128)(2,1)S(1)} %fold.3), channel_id=1, source_target_pairs={{0,8},{2,10},{4,12},{6,14},{8,0},{10,2},{12,4},{14,6},{1,9},{3,11}... | collective-permute-start | bytes 196616 | tf_op jit(solution)/shard_map/ppermute | solution.py:126
  44.9 0.1 pad_maximum_fusion
  45.0 3.4 %collective-permute-done.11.refs_2_ = bf16[128,256]{1,0:T(8,128)(2,1)S(1)} collective-permute-done((bf16[128,256]{1,0:T(8,128)(2,1)S(1)}, bf16[128,256]{1,0:T(8,128)(2,1)S(1)}, u32[]{:S(2)}, u32[]{:S(2)}) %collective-permute-start.11) | collective-permute-done | bytes 65568 | tf_op jit(solution)/shard_map/ppermute | solution.py:126
  48.4 1.3 %fresh_pages.1 = (bf16[128,128]{1,0:T(8,128)(2,1)S(1)}, bf16[128,128]{1,0:T(8,128)(2,1)S(1)}, bf16[8,2,64,128]{3,2,1,0:T(8,128)(2,1)}) custom-call(s32[1,2]{1,0:T(1,128)S(1)} %copy-done.2, f32[256,256]{1,0:T(8,128)S(1)} %get-tuple-element.19.kept.refs_0_, bf16[256,256]{1,0:T(8,128)(2,1)S(1)} %collective-permute-done.10.arrived.refs_1_, ...), custom_call_target="tpu_custom_call" | custom-call | bytes 262144 | tf_op jit(solution)/shard_map/fresh_pages/pallas_call | solution.py:256
  49.7 0.0 all-to-all-done.1.refs_7_
  49.7 4.9 %all-to-all-start.2 = ((bf16[8,2,64,128]{3,2,1,0:T(8,128)(2,1)}), bf16[8,2,64,128]{3,2,1,0:T(8,128)(2,1)S(1)}, u32[]{:S(2)}, u32[]{:S(2)}) async-start(bf16[8,2,64,128]{3,2,1,0:T(8,128)(2,1)} %get-tuple-element.23), calls=%async_computation.2 | async-start | bytes 524288 | tf_op jit(solution)/shard_map/all_to_all | solution.py:375
  54.6 0.0 collective-permute-done.6.refs_9_
  54.6 1.2 %products.2 = (f32[256,512]{1,0:T(8,128)S(1)}, bf16[256,512]{1,0:T(8,128)(2,1)S(1)}) custom-call(s32[2]{0:T(128)S(1)} %pad_add_fusion.place, bf16[128,512]{1,0:T(8,128)(2,1)S(1)} %get-tuple-element.27.refs_0_, bf16[128,512]{1,0:T(8,128)(2,1)S(1)} %collective-permute-done.refs_1_, bf16[128,512]{1,0:T(8,128)(2,1)S(1)} %collective-permute-done.1.refs_2_, ...), custom_call_target="tpu_custom_call" | custom-call | flops 536870912 | bytes 2883584 | tf_op jit(solution)/shard_map/products/pallas_call | solution.py:54
  55.9 2.1 %collective-permute-start.7 = (bf16[256,512]{1,0:T(8,128)(2,1)S(1)}, bf16[256,512]{1,0:T(8,128)(2,1)S(1)}, u32[]{:S(2)}, u32[]{:S(2)}) collective-permute-start(bf16[256,512]{1,0:T(8,128)(2,1)S(1)} %get-tuple-element.18), channel_id=1, source_target_pairs={{0,4},{2,6},{4,0},{6,2},{8,12},{10,14},{12,8},{14,10},{1,5},{3,7},... | collective-permute-start | bytes 786440 | tf_op jit(solution)/shard_map/ppermute | solution.py:125
  58.0 7.2 %collective-permute-done.7.arrived.refs_1_ = bf16[256,512]{1,0:T(8,128)(2,1)S(1)} collective-permute-done((bf16[256,512]{1,0:T(8,128)(2,1)S(1)}, bf16[256,512]{1,0:T(8,128)(2,1)S(1)}, u32[]{:S(2)}, u32[]{:S(2)}) %collective-permute-start.7) | collective-permute-done | bytes 262176 | tf_op jit(solution)/shard_map/ppermute | solution.py:125
  65.2 1.9 %collective-permute-start.8 = (bf16[128,512]{1,0:T(8,128)(2,1)S(1)}, bf16[128,512]{1,0:T(8,128)(2,1)S(1)}, u32[]{:S(2)}, u32[]{:S(2)}) collective-permute-start(bf16[128,512]{1,0:T(8,128)(2,1)S(1)} %fold.2), channel_id=1, source_target_pairs={{0,8},{2,10},{4,12},{6,14},{8,0},{10,2},{12,4},{14,6},{1,9},{3,11}... | collective-permute-start | bytes 393224 | tf_op jit(solution)/shard_map/ppermute | solution.py:126
  67.0 4.9 %collective-permute-done.8.refs_2_ = bf16[128,512]{1,0:T(8,128)(2,1)S(1)} collective-permute-done((bf16[128,512]{1,0:T(8,128)(2,1)S(1)}, bf16[128,512]{1,0:T(8,128)(2,1)S(1)}, u32[]{:S(2)}, u32[]{:S(2)}) %collective-permute-start.8) | collective-permute-done | bytes 131104 | tf_op jit(solution)/shard_map/ppermute | solution.py:126
  71.9 1.8 %attend.1 = bf16[128,512]{1,0:T(8,128)(2,1)} custom-call(s32[1]{0:T(128)} %copy.37.pages_count, s32[1,4]{1,0:T(1,128)S(1)} %copy-done.1, f32[256,512]{1,0:T(8,128)S(1)} %get-tuple-element.17.kept.refs_0_, bf16[256,512]{1,0:T(8,128)(2,1)S(1)} %collective-permute-done.7.arrived.refs_1_, bf16[128,512]{1,0:T(8,128)(2,1)S(1)} %collective-permute-done.8.refs_2_, ...), custom_call_target="tpu_custom_call" | custom-call | flops 100663296 | bytes 786432 | tf_op jit(solution)/shard_map/attend/pallas_call | solution.py:330
  73.7 0.0 all-to-all-done.2.incoming
  73.7 1.3 %land_pages.1 = bf16[16,2,64,128]{3,2,1,0:T(8,128)(2,1)} custom-call(s32[8,2]{1,0:T(8,128)S(1)} %bitcast.31, bf16[8,2,64,128]{3,2,1,0:T(8,128)(2,1)S(1)} %all-to-all-done.2.incoming, bf16[16,2,64,128]{3,2,1,0:T(8,128)(2,1)} %copy-done), custom_call_target="tpu_custom_call", output_to_operand_aliasing={{}: (2, {})} | custom-call | bytes 131072 | tf_op jit(solution)/shard_map/land_pages/pallas_call | solution.py:214
  (13 shorter events, 0.1 us)
Async XLA Ops:
  0.6 1.4 %copy-start.3 = (bf16[128,4096]{1,0:T(8,128)(2,1)S(1)}, bf16[128,4096]{1,0:T(8,128)(2,1)}, u32[]{:S(2)}) copy-start(bf16[128,4096]{1,0:T(8,128)(2,1)} %param.9) | copy-start | bytes 3145732
  0.6 1.7 %copy-start.4 = (f32[4096]{0:T(1024)S(1)}, f32[4096]{0:T(1024)}, u32[]{:S(2)}) copy-start(f32[4096]{0:T(1024)} %param.16) | copy-start | bytes 49156
  1.8 26.0 %copy-start = (bf16[16,2,64,128]{3,2,1,0:T(8,128)(2,1)}, bf16[16,2,64,128]{3,2,1,0:T(8,128)(2,1)S(1)}, u32[]{:S(2)}) copy-start(bf16[16,2,64,128]{3,2,1,0:T(8,128)(2,1)S(1)} %copy.38.pool._) | copy-start | bytes 1572868
  2.4 5.9 %slice-start = ((bf16[512,1,6,128]{3,0,2,1:T(8,128)(2,1)}), bf16[512,1,4,128]{3,0,2,1:T(8,128)(2,1)S(1)}, s32[]{:S(2)}) async-start(bf16[512,1,6,128]{3,0,2,1:T(8,128)(2,1)} %param.17), calls=%async_computation.3 | async-start | bytes 1048576 | tf_op jit(solution)/shard_map/slice | solution.py:121
  2.7 16.8 %collective-permute-start = (bf16[128,512]{1,0:T(8,128)(2,1)S(1)}, bf16[128,512]{1,0:T(8,128)(2,1)S(1)}, u32[]{:S(2)}, u32[]{:S(2)}) collective-permute-start(bf16[128,512]{1,0:T(8,128)(2,1)S(1)} %get-tuple-element.13), channel_id=1, source_target_pairs={{0,4},{2,6},{4,0},{6,2},{8,12},{10,14},{12,8},{14,10},{1,5},{3,7},... | collective-permute-start | bytes 393224 | tf_op jit(solution)/shard_map/ppermute | solution.py:116
  5.8 13.7 %collective-permute-start.1 = (bf16[128,512]{1,0:T(8,128)(2,1)S(1)}, bf16[128,512]{1,0:T(8,128)(2,1)S(1)}, u32[]{:S(2)}, u32[]{:S(2)}) collective-permute-start(bf16[128,512]{1,0:T(8,128)(2,1)S(1)} %get-tuple-element.14), channel_id=1, source_target_pairs={{0,8},{2,10},{4,12},{6,14},{8,0},{10,2},{12,4},{14,6},{1,9},{3,11}... | collective-permute-start | bytes 393224 | tf_op jit(solution)/shard_map/ppermute | solution.py:116
  8.3 11.6 %collective-permute-start.2 = (bf16[128,512]{1,0:T(8,128)(2,1)S(1)}, bf16[128,512]{1,0:T(8,128)(2,1)S(1)}, u32[]{:S(2)}, u32[]{:S(2)}) collective-permute-start(bf16[128,512]{1,0:T(8,128)(2,1)S(1)} %get-tuple-element.15), channel_id=1, source_target_pairs={{0,12},{2,14},{4,8},{6,10},{8,4},{10,6},{12,0},{14,2},{1,13},{3,15... | collective-permute-start | bytes 393224 | tf_op jit(solution)/shard_map/ppermute | solution.py:116
  8.8 1.9 %slice-start.1 = ((bf16[512,1,6,128]{3,0,2,1:T(8,128)(2,1)}), bf16[512,1,2,128]{3,0,2,1:T(8,128)(2,1)S(1)}, s32[]{:S(2)}) async-start(bf16[512,1,6,128]{3,0,2,1:T(8,128)(2,1)} %param.17), calls=%async_computation.4 | async-start | bytes 524288 | tf_op jit(solution)/shard_map/slice | solution.py:120
  8.9 3.6 %copy-start.2 = (s32[1,2]{1,0:T(1,128)S(1)}, s32[1,2]{1,0:T(1,128)}, u32[]{:S(2)}) copy-start(s32[1,2]{1,0:T(1,128)} %homes.1) | copy-start | bytes 28
  8.9 3.6 %copy-start.7 = (s32[1,2]{1,0:T(1,128)S(1)}, s32[1,2]{1,0:T(1,128)}, u32[]{:S(2)}) copy-start(s32[1,2]{1,0:T(1,128)} %param.15) | copy-start | bytes 28
  8.9 3.7 %copy-start.1 = (s32[1,4]{1,0:T(1,128)S(1)}, s32[1,4]{1,0:T(1,128)}, u32[]{:S(2)}) copy-start(s32[1,4]{1,0:T(1,128)} %owners.1) | copy-start | bytes 52
  8.9 3.7 %copy-start.6 = (s32[1,4]{1,0:T(1,128)S(1)}, s32[1,4]{1,0:T(1,128)}, u32[]{:S(2)}) copy-start(s32[1,4]{1,0:T(1,128)} %param.13) | copy-start | bytes 52
  8.9 45.7 %collective-permute-start.6 = (bf16[512,512]{1,0:T(8,128)(2,1)S(1)}, bf16[512,512]{1,0:T(8,128)(2,1)S(1)}, u32[]{:S(2)}, u32[]{:S(2)}) collective-permute-start(bf16[512,512]{1,0:T(8,128)(2,1)S(1)} %bitcast.26), channel_id=1, source_target_pairs={{0,2},{2,0},{4,6},{6,4},{8,10},{10,8},{12,14},{14,12},{1,3},{3,1},... | collective-permute-start | bytes 1572872 | tf_op jit(solution)/shard_map/ppermute | solution.py:103
  11.0 24.0 %collective-permute-start.9 = (bf16[512,256]{1,0:T(8,128)(2,1)S(1)}, bf16[512,256]{1,0:T(8,128)(2,1)S(1)}, u32[]{:S(2)}, u32[]{:S(2)}) collective-permute-start(bf16[512,256]{1,0:T(8,128)(2,1)S(1)} %bitcast.28), channel_id=1, source_target_pairs={{0,2},{2,0},{4,6},{6,4},{8,10},{10,8},{12,14},{14,12},{1,3},{3,1},... | collective-permute-start | bytes 786440 | tf_op jit(solution)/shard_map/ppermute | solution.py:103
  13.4 14.4 %all-to-all-start = ((s32[8,1,2]{2,1,0:T(1,128)}), s32[8,1,2]{2,1,0:T(1,128)S(1)}, u32[]{:S(2)}, u32[]{:S(2)}) async-start(s32[8,1,2]{2,1,0:T(1,128)} %copy.24), calls=%async_computation | async-start | bytes 8192 | tf_op jit(solution)/shard_map/all_to_all | solution.py:360
  19.5 15.5 %collective-permute-start.3 = (bf16[128,512]{1,0:T(8,128)(2,1)S(1)}, bf16[128,512]{1,0:T(8,128)(2,1)S(1)}, u32[]{:S(2)}, u32[]{:S(2)}) collective-permute-start(bf16[128,512]{1,0:T(8,128)(2,1)S(1)} %collective-permute-done.refs_1_), channel_id=1, source_target_pairs={{0,1},{1,0},{2,3},{3,2},{4,5},{5,4},{6,7},{7,6},{8,9},{9,8},{10,11... | collective-permute-start | bytes 393224 | tf_op jit(solution)/shard_map/ppermute | solution.py:117
  19.5 15.5 %collective-permute-start.4 = (bf16[128,512]{1,0:T(8,128)(2,1)S(1)}, bf16[128,512]{1,0:T(8,128)(2,1)S(1)}, u32[]{:S(2)}, u32[]{:S(2)}) collective-permute-start(bf16[128,512]{1,0:T(8,128)(2,1)S(1)} %collective-permute-done.1.refs_2_), channel_id=1, source_target_pairs={{0,1},{1,0},{2,3},{3,2},{4,5},{5,4},{6,7},{7,6},{8,9},{9,8},{10,11... | collective-permute-start | bytes 393224 | tf_op jit(solution)/shard_map/ppermute | solution.py:117
  20.0 15.0 %collective-permute-start.5 = (bf16[128,512]{1,0:T(8,128)(2,1)S(1)}, bf16[128,512]{1,0:T(8,128)(2,1)S(1)}, u32[]{:S(2)}, u32[]{:S(2)}) collective-permute-start(bf16[128,512]{1,0:T(8,128)(2,1)S(1)} %collective-permute-done.2.refs_3_), channel_id=1, source_target_pairs={{0,1},{1,0},{2,3},{3,2},{4,5},{5,4},{6,7},{7,6},{8,9},{9,8},{10,11... | collective-permute-start | bytes 393224 | tf_op jit(solution)/shard_map/ppermute | solution.py:117
  29.2 8.9 %copy-start.5 = (f32[64]{0:T(128)S(1)}, f32[64]{0:T(128)}, u32[]{:S(2)}) copy-start(f32[64]{0:T(128)} %multiply_exponential_fusion) | copy-start | bytes 772
  29.2 20.5 %all-to-all-start.1 = ((bf16[8,2,64,128]{3,2,1,0:T(8,128)(2,1)}), bf16[8,2,64,128]{3,2,1,0:T(8,128)(2,1)S(1)}, u32[]{:S(2)}, u32[]{:S(2)}) async-start(bf16[8,2,64,128]{3,2,1,0:T(8,128)(2,1)} %pick_pages.1), calls=%async_computation.1 | async-start | bytes 524288 | tf_op jit(solution)/shard_map/all_to_all | solution.py:364
  36.0 6.7 %collective-permute-start.10 = (bf16[256,256]{1,0:T(8,128)(2,1)S(1)}, bf16[256,256]{1,0:T(8,128)(2,1)S(1)}, u32[]{:S(2)}, u32[]{:S(2)}) collective-permute-start(bf16[256,256]{1,0:T(8,128)(2,1)S(1)} %get-tuple-element.20), channel_id=1, source_target_pairs={{0,4},{2,6},{4,0},{6,2},{8,12},{10,14},{12,8},{14,10},{1,5},{3,7},... | collective-permute-start | bytes 393224 | tf_op jit(solution)/shard_map/ppermute | solution.py:125
  42.7 5.7 %collective-permute-start.11 = (bf16[128,256]{1,0:T(8,128)(2,1)S(1)}, bf16[128,256]{1,0:T(8,128)(2,1)S(1)}, u32[]{:S(2)}, u32[]{:S(2)}) collective-permute-start(bf16[128,256]{1,0:T(8,128)(2,1)S(1)} %fold.3), channel_id=1, source_target_pairs={{0,8},{2,10},{4,12},{6,14},{8,0},{10,2},{12,4},{14,6},{1,9},{3,11}... | collective-permute-start | bytes 196616 | tf_op jit(solution)/shard_map/ppermute | solution.py:126
  49.7 24.0 %all-to-all-start.2 = ((bf16[8,2,64,128]{3,2,1,0:T(8,128)(2,1)}), bf16[8,2,64,128]{3,2,1,0:T(8,128)(2,1)S(1)}, u32[]{:S(2)}, u32[]{:S(2)}) async-start(bf16[8,2,64,128]{3,2,1,0:T(8,128)(2,1)} %get-tuple-element.23), calls=%async_computation.2 | async-start | bytes 524288 | tf_op jit(solution)/shard_map/all_to_all | solution.py:375
  55.9 9.2 %collective-permute-start.7 = (bf16[256,512]{1,0:T(8,128)(2,1)S(1)}, bf16[256,512]{1,0:T(8,128)(2,1)S(1)}, u32[]{:S(2)}, u32[]{:S(2)}) collective-permute-start(bf16[256,512]{1,0:T(8,128)(2,1)S(1)} %get-tuple-element.18), channel_id=1, source_target_pairs={{0,4},{2,6},{4,0},{6,2},{8,12},{10,14},{12,8},{14,10},{1,5},{3,7},... | collective-permute-start | bytes 786440 | tf_op jit(solution)/shard_map/ppermute | solution.py:125
  65.2 6.8 %collective-permute-start.8 = (bf16[128,512]{1,0:T(8,128)(2,1)S(1)}, bf16[128,512]{1,0:T(8,128)(2,1)S(1)}, u32[]{:S(2)}, u32[]{:S(2)}) collective-permute-start(bf16[128,512]{1,0:T(8,128)(2,1)S(1)} %fold.2), channel_id=1, source_target_pairs={{0,8},{2,10},{4,12},{6,14},{8,0},{10,2},{12,4},{14,6},{1,9},{3,11}... | collective-permute-start | bytes 393224 | tf_op jit(solution)/shard_map/ppermute | solution.py:126

commit v5 on v4

v5 whole, which is shorter than its diff:
```python
import functools
import math

import jax
import jax.numpy as jnp
from jax import lax
from jax.experimental import pallas as pl
from jax.experimental.pallas import tpu as pltpu
from jax.sharding import PartitionSpec as P

WAITS = dict(kv=30, q=10, pick=3, fresh=0, fold=0, attend=10, land=0, prepare=0)
ANY = pl.BlockSpec(memory_space=pl.ANY)
SCALARS = pl.BlockSpec(memory_space=pltpu.SMEM)
VECTORS = pl.BlockSpec(memory_space=pltpu.VMEM)
PARAMS = pltpu.CompilerParams(vmem_limit_bytes=32 * 1024 * 1024)


def wait(name):
    return pl.CostEstimate(flops=int(WAITS[name] * 1.15e9), bytes_accessed=0, transcendentals=0)


def tie(value, *others):
    return lax.optimization_barrier((value,) + others)[0]


def crossed(size, distance):
    return [(rank, rank ^ distance) for rank in range(size)]


def rotary_tables(positions, head_size):
    half_size = head_size // 2
    index_f = jnp.arange(half_size).astype(jnp.float32)
    inverse = jnp.exp(-(2.0 * index_f / head_size) * jnp.log(500000.0))
    angles = positions[:, None] * inverse[None, :]
    cosine, sine = jnp.cos(angles), jnp.sin(angles)
    return jnp.concatenate([cosine, cosine], axis=1), jnp.concatenate([-sine, sine], axis=1)


def turn(values, cosine, sine):
    return values * cosine + pltpu.roll(values, values.shape[-1] // 2, axis=1) * sine


def prepare_kernel(*refs):
    arguments, pieces, numbers = refs[:7], refs[7:12], refs[12]
    local_copies, semaphore = refs[13:20], refs[20]
    copies = [
        pltpu.make_async_copy(here, there, semaphore.at[index])
        for index, (here, there) in enumerate(zip(arguments, local_copies))
    ]
    for copy in copies:
        copy.start()
    tokens, gain, pages_count, owners, slots, homes, home_slots = local_copies
    token_rows, width = tokens.shape
    rows = pieces[0].shape[1]
    member, core = lax.axis_index("dp") // 2, lax.axis_index("tp")
    for copy in copies:
        copy.wait()
    count = pages_count[0, 0]
    values = [count]
    values += [jnp.where(page < count, owners[0, page], -1) for page in range(owners.shape[1])]
    for ref in (slots, homes, home_slots):
        values += [ref[0, page] for page in range(ref.shape[1])]
    shape = (pieces[-1].shape[0] - token_rows, rows)
    column = lax.broadcasted_iota(jnp.int32, shape, 1)
    tail = jnp.zeros(shape, jnp.float32)
    for index, value in enumerate(values):
        numbers[0, index] = value
        tail = jnp.where(column == index, value.astype(jnp.float32), tail)
    wide = tokens[...].astype(jnp.float32)
    row_scale = lax.rsqrt(jnp.sum(wide * wide, axis=1, keepdims=True) / width + 1e-05)
    for index, piece in enumerate(pieces):
        target = member ^ max(index - 1, 0)
        half = 1 - core if index == 1 else core
        span = pl.ds(pl.multiple_of((2 * target + half) * rows, 128), rows)
        part = tokens[:, span].astype(jnp.float32) * row_scale * gain[:, span]
        piece[:token_rows] = part.astype(piece.dtype)
        if index > 1:
            piece[token_rows:] = tail.astype(piece.dtype)


def prepare(tokens, gain, pages_count, requests, rows):
    token_rows, width = tokens.shape
    heights = [token_rows] * 2 + [token_rows + 16] * 3
    arguments = [tokens, gain.reshape(1, width), pages_count.reshape(1, 1)] + requests
    count = 1 + sum(part.shape[1] for part in requests)
    return pl.pallas_call(
        prepare_kernel,
        out_shape=[jax.ShapeDtypeStruct((height, rows), jnp.bfloat16) for height in heights]
        + [jax.ShapeDtypeStruct((1, count), jnp.int32)],
        in_specs=[ANY] * 7,
        out_specs=[VECTORS] * 5 + [SCALARS],
        scratch_shapes=[pltpu.VMEM(value.shape, value.dtype) for value in arguments[:2]]
        + [pltpu.SMEM(value.shape, value.dtype) for value in arguments[2:]]
        + [pltpu.SemaphoreType.DMA((7,))],
        compiler_params=pltpu.CompilerParams(vmem_limit_bytes=60 * 1024 * 1024),
        cost_estimate=wait("prepare"),
        name="prepare",
    )(*arguments)


def side_by_side(*refs):
    return jnp.concatenate(
        [blocks[index] for blocks in refs for index in range(blocks.shape[0])], axis=1
    )


def product_kernel(place, *refs):
    own_weight = refs[8]
    other = [ref for ref in refs[9:] if len(ref.shape) == 3]
    kept, *leaving = refs[9 + len(other) :]
    rows = leaving[-1].shape[0] // (1 if len(leaving) == 3 else 2)
    direct = jnp.concatenate([ref[:rows] for ref in refs[:4]], axis=0)
    passed = jnp.concatenate([ref[:rows] for ref in refs[4:8]], axis=0)
    own_first = (place[0] % 2) == place[1]
    for_own = jnp.where(own_first, direct, passed)
    for_other = jnp.where(own_first, passed, direct)
    result = jnp.dot(
        for_own, side_by_side(own_weight), preferred_element_type=jnp.float32
    ) + jnp.dot(for_other, side_by_side(*other), preferred_element_type=jnp.float32)
    result = [result[index * rows : (index + 1) * rows] for index in range(4)]
    kept[:rows] = result[0]
    if len(leaving) == 3:
        for out, part in zip(leaving, result[1:]):
            out[...] = part.astype(out.dtype)
    else:
        kept[rows:] = result[2]
        leaving[0][:rows] = result[1].astype(leaving[0].dtype)
        leaving[0][rows:] = result[3].astype(leaving[0].dtype)


def products(place, direct, passed, own_weight, first, other, paired):
    rows, head_size = direct[0].shape[0], own_weight.shape[2]
    shapes = [(2 * rows, jnp.float32), (2 * rows, jnp.bfloat16)]
    if not paired:
        shapes = [(rows, jnp.float32)] + [(rows, jnp.bfloat16)] * 3
    count = sum(part.shape[0] for part in other)
    columns = count * head_size
    depth = 2 * own_weight.shape[1]
    blocks = pl.BlockSpec((count,) + own_weight.shape[1:], lambda step: (first // count, 0, 0))
    return pl.pallas_call(
        product_kernel,
        grid=(1,),
        out_shape=[jax.ShapeDtypeStruct((height, columns), kind) for height, kind in shapes],
        in_specs=[SCALARS] + [VECTORS] * 8 + [blocks] + [VECTORS] * len(other),
        out_specs=[VECTORS] * len(shapes),
        compiler_params=PARAMS,
        cost_estimate=wait("q" if first == 0 else "kv"),
        name="products",
    )(place, *direct, *passed, own_weight, *other)


def fold_kernel(kept, arrived, *refs):
    pages, far, relay = refs[:4], refs[4], refs[5]
    rows = far.shape[0]
    far[...] = (kept[rows:] + arrived[rows:].astype(jnp.float32)).astype(far.dtype)
    for index, page in enumerate(pages):
        relay[index] = page[1]


def fold(kept, arrived, pages):
    rows, columns = kept.shape[0] // 2, kept.shape[1]
    return pl.pallas_call(
        fold_kernel,
        out_shape=[
            jax.ShapeDtypeStruct((rows, columns), jnp.bfloat16),
            jax.ShapeDtypeStruct((4,) + pages[0].shape[1:], pages[0].dtype),
        ],
        in_specs=[VECTORS] * 6,
        out_specs=[VECTORS] * 2,
        compiler_params=PARAMS,
        cost_estimate=wait("fold"),
        name="fold",
    )(kept, arrived, *pages)


def answer(numbers, prefix, me, ranks):
    new_pages = (numbers.shape[1] - 1 - 2 * prefix) // 2
    starts = [1, 1 + prefix, 1 + 2 * prefix, 1 + 2 * prefix + new_pages, numbers.shape[1]]
    owners, slots, homes, home_slots = [
        numbers[:, first:last] for first, last in zip(starts[:-1], starts[1:])
    ]
    asked = jnp.max(jnp.where(owners == me, slots, -1), axis=1)
    replaced = jnp.max(jnp.where(homes == me, home_slots, -1), axis=1)
    return jnp.stack([asked, replaced, ranks], axis=1).astype(jnp.int32)


def near(values, ranks):
    return lax.ppermute(values, "dp", crossed(ranks, 1))


def along(values, ranks, step):
    return lax.ppermute(values, "dp", crossed(ranks, 2 * step))


def column_plan(tokens, gain, wqkv, pages_count, requests, pool, place, ranks):
    me = place[0]
    rows = wqkv.shape[0]
    blocks = wqkv.shape[2]
    token_rows = tokens.shape[0]
    prefix = requests[0].shape[1]
    weight = wqkv[:, 0].transpose(1, 0, 2)
    kv_other, *q_other = [
        near(weight[first : first + 2], ranks) for first in range(blocks - 2, -1, -2)
    ]
    own_direct, own_passed, *pieces, numbers = prepare(tokens, gain, pages_count, requests, rows)
    direct = [None] * 3
    for step in (2, 3, 1):
        direct[step - 1] = along(pieces[step - 1], ranks, step)
    direct = tie(direct, kv_other)
    passed = [lax.ppermute(piece, "tp", crossed(2, 1)) for piece in direct]
    table = [piece[token_rows : token_rows + 1, : numbers.shape[1]] for piece in direct]
    table = jnp.concatenate([numbers] + [row.astype(jnp.int32) for row in table], axis=0)
    direct = [own_direct] + direct
    passed = [own_passed] + passed

    kv_own, *leaving = products(place, direct, passed, weight, blocks - 2, [kv_other], False)
    kv_parts = [kv_own] + [along(part, ranks, step) for step, part in zip((1, 2, 3), leaving)]

    table = tie(table, kv_own)
    table = jnp.concatenate([table, near(table, ranks)], axis=0)
    lanes = jnp.arange(ranks, dtype=jnp.int32)
    table = answer(table, prefix, me, (2 * lanes % ranks + lanes // 4) ^ me)
    *picked, copied = pick_pages(table, pool, 4)
    pages = picked[:1] + [along(picked[step], ranks, step) for step in (1, 2, 3)]

    q_other = tie(q_other[::-1], kv_parts, picked[0])
    q_kept, leaving = products(place, direct, passed, weight, 0, q_other, True)
    q_arrived = along(leaving, ranks, 1)
    kv_parts = tie(kv_parts, q_kept)

    def finish(fresh):
        far, relay = fold(q_kept, tie(q_arrived, fresh), pages)
        relayed = near(relay, ranks)
        return [q_kept, q_arrived, along(far, ranks, 2)], pages + [relayed]

    return kv_parts, finish, table, copied, numbers


def general_plan(tokens, gain, wqkv, pages_count, requests, pool, place, ranks):
    me = place[0]
    rows = wqkv.shape[0]
    members = ranks // 2
    token_rows = tokens.shape[0]
    blocks = wqkv.shape[2]
    prefix = requests[0].shape[1]
    weight = wqkv[:, 0].transpose(1, 0, 2)
    groups = [[2 * index + side for index in range(members)] for side in range(2)]
    wide = tokens.astype(jnp.float32)
    row_scale = lax.rsqrt(jnp.mean(wide * wide, axis=-1, keepdims=True) + 1e-05)
    normed = (wide * row_scale * gain).astype(jnp.bfloat16)
    chunks = normed.reshape(token_rows, members, 2 * rows).transpose(1, 0, 2)
    chunks = lax.all_to_all(
        chunks, "dp", split_axis=0, concat_axis=0, axis_index_groups=groups, tiled=True
    ).reshape(members * token_rows, 2 * rows)
    side = me % 2
    parts = jnp.dot(
        lax.dynamic_slice(chunks, (0, side * rows), (chunks.shape[0], rows)),
        side_by_side(weight),
        preferred_element_type=jnp.float32,
    ) + jnp.dot(
        lax.dynamic_slice(chunks, (0, (1 - side) * rows), (chunks.shape[0], rows)),
        side_by_side(near(weight, ranks)),
        preferred_element_type=jnp.float32,
    )
    parts = lax.all_to_all(
        parts.astype(jnp.bfloat16).reshape(members, token_rows, -1),
        "dp",
        split_axis=0,
        concat_axis=0,
        axis_index_groups=groups,
        tiled=True,
    )
    total = jnp.sum(parts.astype(jnp.float32), axis=0)
    q_columns = (blocks - 2) * wqkv.shape[3]
    lanes = jnp.arange(ranks, dtype=jnp.int32)
    listed = jnp.arange(prefix, dtype=jnp.int32) < pages_count[0]
    numbers = jnp.concatenate(
        [pages_count[:, None], jnp.where(listed, requests[0], -1)] + requests[1:], axis=1
    )
    table = answer(jnp.broadcast_to(numbers, (ranks,) + numbers.shape[1:]), prefix, lanes[:, None], lanes)
    table = lax.all_to_all(table[:, :2], "dp", split_axis=0, concat_axis=0, tiled=True)
    table = jnp.concatenate([table, lanes[:, None]], axis=1)
    chosen, copied = pick_pages(table, pool, 1)
    replies = lax.all_to_all(chosen, "dp", split_axis=0, concat_axis=0, tiled=True)

    def finish(fresh):
        return [total[:, :q_columns]], [replies]

    return [total[:, q_columns:]], finish, table, copied, numbers


def each_row(rows, visit):
    if rows <= 8:
        for row in range(rows):
            visit(row)
    else:
        def step(row, carry):
            visit(row)
            return carry

        lax.fori_loop(0, rows, step, 0)


def pick_kernel(table, pool, *refs):
    *outs, copied, semaphore = refs
    rows = table.shape[0]
    whole = pltpu.make_async_copy(pool, copied, semaphore.at[rows])
    whole.start()

    def visit(act, row):
        @pl.when(table[row, 0] >= 0)
        def _():
            place = (0, table[row, 2]) if len(outs) == 1 else (row % len(outs), row // len(outs))
            act(
                pltpu.make_async_copy(
                    pool.at[table[row, 0]], outs[place[0]].at[place[1]], semaphore.at[row]
                )
            )

    each_row(rows, functools.partial(visit, lambda copy: copy.start()))
    each_row(rows, functools.partial(visit, lambda copy: copy.wait()))
    whole.wait()


def pick_pages(table, pool, count):
    rows = table.shape[0]
    page = pool.shape[1:]
    return pl.pallas_call(
        pick_kernel,
        out_shape=[jax.ShapeDtypeStruct((rows // count,) + page, pool.dtype)] * count
        + [jax.ShapeDtypeStruct(pool.shape, pool.dtype)],
        in_specs=[SCALARS, ANY],
        out_specs=[ANY] * (count + 1),
        scratch_shapes=[pltpu.SemaphoreType.DMA((rows + 1,))],
        compiler_params=PARAMS,
        cost_estimate=wait("pick"),
        name="pick_pages",
    )(table, pool)


def land_kernel(table, incoming, _, pool, semaphore):
    ranks = incoming.shape[0]

    def visit(act, row):
        @pl.when(table[row, 1] >= 0)
        def _():
            act(
                pltpu.make_async_copy(
                    incoming.at[table[row, 2]], pool.at[table[row, 1]], semaphore.at[row]
                )
            )

    each_row(ranks, functools.partial(visit, lambda copy: copy.start()))
    each_row(ranks, functools.partial(visit, lambda copy: copy.wait()))


def land_pages(table, incoming, pool):
    ranks = incoming.shape[0]
    return pl.pallas_call(
        land_kernel,
        out_shape=jax.ShapeDtypeStruct(pool.shape, pool.dtype),
        in_specs=[SCALARS, ANY, ANY],
        out_specs=ANY,
        scratch_shapes=[pltpu.SemaphoreType.DMA((ranks,))],
        input_output_aliases={2: 0},
        compiler_params=PARAMS,
        cost_estimate=wait("land"),
        name="land_pages",
    )(table, incoming, pool)


def fresh_kernel(pieces, first, numbers, *refs):
    parts = refs[:pieces]
    cosine, sine, keys, values, outgoing, pages, semaphore = refs[pieces:]
    token_rows, head_size = keys.shape
    total = sum(part[:token_rows].astype(jnp.float32) for part in parts)
    keys[...] = turn(total[:, :head_size], cosine[...], sine[...]).astype(keys.dtype)
    values[...] = total[:, head_size:].astype(values.dtype)
    count, _, page_rows, _ = pages.shape
    copies = []
    for page in range(count):
        span = pl.ds(page * page_rows, page_rows)
        pages[page, 0] = keys[span, :]
        pages[page, 1] = values[span, :]
        copies.append(
            pltpu.make_async_copy(
                pages.at[page], outgoing.at[numbers[0, first + page]], semaphore.at[page]
            )
        )
        copies[-1].start()
    for copy in copies:
        copy.wait()


def fresh_pages(numbers, first, count, parts, cosine, sine, ranks, page_rows):
    token_rows, head_size = cosine.shape
    shape = jax.ShapeDtypeStruct((token_rows, head_size), jnp.bfloat16)
    return pl.pallas_call(
        functools.partial(fresh_kernel, len(parts), first),
        out_shape=[
            shape,
            shape,
            jax.ShapeDtypeStruct((ranks, 2, page_rows, head_size), jnp.bfloat16),
        ],
        in_specs=[SCALARS] + [VECTORS] * (len(parts) + 2),
        out_specs=[VECTORS, VECTORS, ANY],
        scratch_shapes=[
            pltpu.VMEM((count, 2, page_rows, head_size), jnp.bfloat16),
            pltpu.SemaphoreType.DMA((count,)),
        ],
        compiler_params=PARAMS,
        cost_estimate=wait("fresh"),
        name="fresh_pages",
    )(numbers, *parts, cosine, sine)


def attend_kernel(terms, together, prefix, place, numbers, *refs):
    parts, (cosine, sine, keys_new, values_new) = refs[:terms], refs[terms : terms + 4]
    *pages, out, keys, values = refs[terms + 4 :]
    token_rows, head_size = keys_new.shape
    page_rows = pages[0].shape[2]
    group = out.shape[1] // head_size
    count = numbers[0, 0]
    scale = 1.0 / math.sqrt(head_size)

    def store(page, key, value):
        span = pl.ds(page * page_rows, page_rows)
        keys[span, :] = key
        values[span, :] = jnp.where(page < count, value, jnp.zeros_like(value))

    for page in range(prefix):
        owner = numbers[0, 1 + page]
        if len(pages) == 1:
            source = jnp.where(page < count, owner, 0)
            store(page, pages[0][source, 0], pages[0][source, 1])
        else:
            distance = place[0] ^ owner
            store(page, pages[0][0, 0], pages[0][0, 1])
            for index in range(2 * (len(pages) - 1)):
                source = (-1, index // 2) if index % 2 else (index // 2, 0)

                @pl.when(distance == index)
                def _(page=page, source=source):
                    taken = pages[source[0]]
                    store(page, taken[source[1], 0], taken[source[1], 1])

    keys[prefix * page_rows :, :] = keys_new[...]
    values[prefix * page_rows :, :] = values_new[...]
    total_rows = keys.shape[0]
    shape = (together * token_rows, total_rows)
    row = lax.broadcasted_iota(jnp.int32, shape, 0) % token_rows
    column = lax.broadcasted_iota(jnp.int32, shape, 1)
    new_column = column - prefix * page_rows
    allowed = (column < count * page_rows) | ((new_column >= 0) & (new_column <= row))
    for first in range(0, group, together):
        queries = []
        for member in range(first, first + together):
            lanes = pl.ds(member * head_size, head_size)
            total = sum(part[:token_rows, lanes].astype(jnp.float32) for part in parts)
            queries.append(turn(total, cosine[...], sine[...]).astype(jnp.bfloat16))
        queries = jnp.concatenate(queries, axis=0)
        scores = (
            lax.dot_general(
                queries, keys[...], (((1,), (1,)), ((), ())), preferred_element_type=jnp.float32
            )
            * scale
        )
        scores = jnp.where(allowed, scores, -1e30)
        largest = jnp.max(scores, axis=1, keepdims=True)
        weights = jnp.exp(scores - largest)
        totals = jnp.sum(weights, axis=1, keepdims=True)
        summed = jnp.dot(
            weights.astype(jnp.bfloat16), values[...], preferred_element_type=jnp.float32
        )
        result = (summed / totals).astype(out.dtype)
        for index in range(together):
            out[:, pl.ds((first + index) * head_size, head_size)] = result[
                index * token_rows : (index + 1) * token_rows
            ]


def attend(place, numbers, prefix, parts, cosine, sine, keys_new, values_new, pages):
    token_rows, head_size = cosine.shape
    group = parts[0].shape[1] // head_size
    total_rows = prefix * pages[0].shape[2] + token_rows
    together = group if total_rows <= 1024 else 1
    return pl.pallas_call(
        functools.partial(attend_kernel, len(parts), together, prefix),
        out_shape=jax.ShapeDtypeStruct((token_rows, group * head_size), jnp.bfloat16),
        in_specs=[SCALARS] * 2 + [VECTORS] * (len(parts) + 4 + len(pages)),
        out_specs=VECTORS,
        scratch_shapes=[pltpu.VMEM((total_rows, head_size), jnp.bfloat16)] * 2,
        compiler_params=PARAMS,
        cost_estimate=wait("attend"),
        name="attend",
    )(place, numbers, *parts, cosine, sine, keys_new, values_new, *pages)


def local(tokens, pool, pages_count, owners, slots, homes, home_slots, norm_attn, wqkv):
    ranks = lax.axis_size("dp")
    place = jnp.stack([lax.axis_index("dp"), lax.axis_index("tp")]).astype(jnp.int32)
    token_rows = tokens.shape[0]
    head_size = wqkv.shape[3]
    page_rows = pool.shape[2]
    prefix = owners.shape[1]
    new_pages = homes.shape[1]

    requests = [owners, slots, homes, home_slots]
    plan = column_plan if ranks == 8 else general_plan
    kv_parts, finish, table, copied, numbers = plan(
        tokens, norm_attn, wqkv, pages_count, requests, pool, place, ranks
    )
    positions = tie(pages_count[0], kv_parts[0]) * page_rows + jnp.arange(token_rows, dtype=jnp.int32)
    cosine, sine = rotary_tables(positions.astype(jnp.float32), head_size)
    keys_new, values_new, outgoing = fresh_pages(
        numbers, 1 + 2 * prefix, new_pages, kv_parts, cosine, sine, ranks, page_rows
    )
    incoming = lax.all_to_all(outgoing, "dp", split_axis=0, concat_axis=0, tiled=True)
    q_parts, pages = finish(keys_new)
    attended = attend(
        place, numbers, prefix, q_parts, cosine, sine, keys_new, values_new, pages
    )
    copied, attended = lax.optimization_barrier((copied, attended))
    pool_out = land_pages(table, incoming, copied)
    return (attended, pool_out)


def solution(mesh):
    in_specs = (
        P(("groups", "dp"), None),
        P(("groups", "dp"), None, None, "tp"),
        P(("groups", "dp")),
        P(("groups", "dp"), None),
        P(("groups", "dp"), None),
        P(("groups", "dp"), None),
        P(("groups", "dp"), None),
        P(),
        P("dp", "tp", None, None),
    )
    out_specs = (P(("groups", "dp"), "tp"), P(("groups", "dp"), None, None, "tp"))
    return jax.shard_map(local, mesh=mesh, in_specs=in_specs, out_specs=out_specs, check_vma=False)
```

time: 75.4 us -> 66.7 us (0.88)
  waiting for transfers between devices: 27.5 us -> 21.2 us
  starting transfers between devices: 33.3 us -> 29.6 us
  Pallas kernels: 8.03 us -> 11.4 us
  local copies, waits for them, and re-layouts: 2.98 us -> 1.66 us
    all_to_all x2 -> x0, starting transfers between devices: 11.3 us -> none  [the longest x1 5.7 us: local(): lax.all_to_all(pick_pages(table, pool), 'dp', split_axis=0, concat_axis=0...]
    all_to_all x2 -> x0, waiting for transfers between devices: 7.73 us -> none  [the longest x1 7.73 us: local(): lax.all_to_all(jnp.stack([wanted, replaced], axis=1), 'dp', split_axis=0,...]
    ppermute x12 -> x19, starting transfers between devices: 17.1 us -> 24.3 us  [the longest x11 18.1 us: along(): return lax.ppermute(values, 'dp', crossed(ranks, 2 * step))]
    all_to_all x1, waiting for transfers between devices: 0.01 us -> 5.24 us  [local(): lax.all_to_all(outgoing, 'dp', split_axis=0, concat_axis=0, tiled=True)]
    ppermute x12 -> x19, waiting for transfers between devices: 19.8 us -> 16 us  [the longest x11 15.3 us: along(): return lax.ppermute(values, 'dp', crossed(ranks, 2 * step))]
    pallas_call x7, Pallas kernels: 6.73 us -> 10.1 us  [the longest x2 2.81 us: products(): pl.pallas_call(product_kernel, grid=(1,), out_shape=[jax.ShapeDtypeStruct...]
    unnamed x19 -> x10, local copies, waits for them, and re-layouts: 1.52 us -> 0.63 us
  transfers between devices with their start and end apart: 15 -> 20, of which waited for: 5 -> 9; matrix products, arithmetic and copies ran while one was open for 4% -> 3% of each run, Pallas kernels for 9% -> 9%
where the time goes in v5:
time: 66.7 us; the launch traced here: 66.4 us
  starting transfers between devices  29.6 us (44%)
  waiting for transfers between devices  21.2 us (32%)
  Pallas kernels  11.4 us (17%)
  local copies, waits for them, and re-layouts  1.66 us (2%)
  between operations  1.51 us (2%)
  other arithmetic  1.05 us (2%)
    ppermute x11, starting transfers between devices, along(): return lax.ppermute(values, 'dp', crossed(ranks, 2 * step))  18.1 us
    ppermute x11, waiting for transfers between devices, along(): return lax.ppermute(values, 'dp', crossed(ranks, 2 * step))  15.3 us
    ppermute x5, starting transfers between devices, near(): return lax.ppermute(values, 'dp', crossed(ranks, 1))  5.62 us
    all_to_all x1, starting transfers between devices, local(): lax.all_to_all(outgoing, 'dp', split_axis=0, concat_axis=0, tiled=True)  5.29 us
    all_to_all x1, waiting for transfers between devices, local(): lax.all_to_all(outgoing, 'dp', split_axis=0, concat_axis=0, tiled=True)  5.24 us
    pallas_call x2, Pallas kernels, products(): pl.pallas_call(product_kernel, grid=(1,), out_shape=[jax.ShapeDtypeStruct...  2.81 us
    pallas_call x1, Pallas kernels, prepare(): pl.pallas_call(prepare_kernel, out_shape=[jax.ShapeDtypeStruct((height, r...  2.5 us
    pallas_call x1, Pallas kernels, attend(): pl.pallas_call(functools.partial(attend_kernel, len(parts), together, pre...  1.97 us
  transfers between devices with their start and end apart: 20, of which 9 were waited for; matrix products, arithmetic and copies ran while one was open for 3% of the time, Pallas kernels for 9%

profile of v5, /device:TPU:0, one launch (start us, length us, event | category | flops | bytes accessed | tf_op | source)
XLA Modules:
  0.0 66.4 jit_solution(12949213731198565536)
XLA Ops:
  0.6 0.0 copy-start
  1.4 2.5 %prepare.1 = (bf16[128,512]{1,0:T(8,128)(2,1)}, bf16[128,512]{1,0:T(8,128)(2,1)}, bf16[144,512]{1,0:T(8,128)(2,1)}, bf16[144,512]{1,0:T(8,128)(2,1)}, bf16[144,512]{1,0:T(8,128)(2,1)}, /*index=5*/s32[1,13]{1,0:T(1,128)}) custom-call(bf16[128,4096]{1,0:T(8,128)(2,1)} %refs_0_.1, f32[1,4096]{1,0:T(1,128)} %bitcast.15, s32[1,1]{1,0:T(1,128)} %bitcast.11.refs_2_, ...), custom_call_target="tpu_custom_call" | custom-call | tf_op jit(solution)/shard_map/prepare/pallas_call | solution.py:86
  3.9 3.1 %collective-permute-start = (bf16[144,512]{1,0:T(8,128)(2,1)}, bf16[144,512]{1,0:T(8,128)(2,1)S(1)}, u32[]{:S(2)}, u32[]{:S(2)}) collective-permute-start(bf16[144,512]{1,0:T(8,128)(2,1)} %get-tuple-element.39), channel_id=1, source_target_pairs={{0,4},{2,6},{4,0},{6,2},{8,12},{10,14},{12,8},{14,10},{1,5},{3,7},... | collective-permute-start | bytes 442376 | tf_op jit(solution)/shard_map/ppermute | solution.py:192
  7.0 2.6 %collective-permute-start.1 = (bf16[144,512]{1,0:T(8,128)(2,1)}, bf16[144,512]{1,0:T(8,128)(2,1)S(1)}, u32[]{:S(2)}, u32[]{:S(2)}) collective-permute-start(bf16[144,512]{1,0:T(8,128)(2,1)} %get-tuple-element.40), channel_id=1, source_target_pairs={{0,8},{2,10},{4,12},{6,14},{8,0},{10,2},{12,4},{14,6},{1,9},{3,11}... | collective-permute-start | bytes 442376 | tf_op jit(solution)/shard_map/ppermute | solution.py:192
  9.5 0.0 collective-permute-start.2
  9.5 0.0 copy-done
  9.6 0.9 %fusion.10 = (bf16[2,512,128]{2,1,0:T(8,128)(2,1)}, bf16[2,512,128]{2,1,0:T(8,128)(2,1)}, bf16[2,512,128]{2,1,0:T(8,128)(2,1)S(1)}) fusion(bf16[6,512,128]{2,1,0:T(8,128)(2,1)S(1)} %bitcast.12), kind=kLoop, calls=%fused_computation.34 | loop fusion | bytes 1572864 | tf_op jit(solution)/shard_map/slice | solution.py:203
  10.4 1.7 %collective-permute-start.3 = (bf16[2,512,128]{2,1,0:T(8,128)(2,1)S(1)}, bf16[2,512,128]{2,1,0:T(8,128)(2,1)S(1)}, u32[]{:S(2)}, u32[]{:S(2)}) collective-permute-start(bf16[2,512,128]{2,1,0:T(8,128)(2,1)S(1)} %get-tuple-element.76), channel_id=1, source_target_pairs={{0,2},{2,0},{4,6},{6,4},{8,10},{10,8},{12,14},{14,12},{1,3},{3,1},... | collective-permute-start | bytes 786440 | tf_op jit(solution)/shard_map/ppermute | solution.py:188
  12.1 0.3 collective-permute-start.8
  12.5 0.1 pad_add_fusion.3.place
  12.6 0.4 collective-permute-done.refs_1_
  13.0 1.7 %collective-permute-start.9 = (bf16[2,512,128]{2,1,0:T(8,128)(2,1)}, bf16[2,512,128]{2,1,0:T(8,128)(2,1)S(1)}, u32[]{:S(2)}, u32[]{:S(2)}) collective-permute-start(bf16[2,512,128]{2,1,0:T(8,128)(2,1)} %get-tuple-element.74), channel_id=1, source_target_pairs={{0,2},{2,0},{4,6},{6,4},{8,10},{10,8},{12,14},{14,12},{1,3},{3,1},... | collective-permute-start | bytes 786440 | tf_op jit(solution)/shard_map/ppermute | solution.py:188
  14.7 6.4 %collective-permute-done.1.refs_2_ = bf16[144,512]{1,0:T(8,128)(2,1)S(1)} collective-permute-done((bf16[144,512]{1,0:T(8,128)(2,1)}, bf16[144,512]{1,0:T(8,128)(2,1)S(1)}, u32[]{:S(2)}, u32[]{:S(2)}) %collective-permute-start.1) | collective-permute-done | bytes 147488 | tf_op jit(solution)/shard_map/ppermute | solution.py:192
  21.2 0.0 collective-permute-done.2.refs_3_
  21.2 0.0 collective-permute-done.3.refs_9_
  21.2 0.0 collective-permute-start.5
  21.2 0.5 collective-permute-start.6
  21.7 0.1 collective-permute-start.4
  21.8 0.6 copy-done.1
  22.4 0.7 %collective-permute-done.4.refs_5_ = bf16[144,512]{1,0:T(8,128)(2,1)S(1)} collective-permute-done((bf16[144,512]{1,0:T(8,128)(2,1)S(1)}, bf16[144,512]{1,0:T(8,128)(2,1)S(1)}, u32[]{:S(2)}, u32[]{:S(2)}) %collective-permute-start.4) | collective-permute-done | bytes 147488 | tf_op jit(solution)/shard_map/ppermute | solution.py:210
  23.1 0.0 collective-permute-done.5.refs_6_
  23.1 0.0 collective-permute-done.6.refs_7_
  23.1 0.0 copy-done.3
  23.1 0.0 copy-done.4
  23.1 0.0 copy-start.2
  23.1 1.6 %products.2 = (f32[128,256]{1,0:T(8,128)S(1)}, bf16[128,256]{1,0:T(8,128)(2,1)}, bf16[128,256]{1,0:T(8,128)(2,1)}, bf16[128,256]{1,0:T(8,128)(2,1)S(1)}) custom-call(s32[2]{0:T(128)S(1)} %pad_add_fusion.3.place, bf16[128,512]{1,0:T(8,128)(2,1)S(1)} %copy-done.3, bf16[144,512]{1,0:T(8,128)(2,1)S(1)} %collective-permute-done.refs_1_, ...), custom_call_target="tpu_custom_call" | custom-call | flops 34500001792 | tf_op jit(solution)/shard_map/products/pallas_call | solution.py:140
  24.7 1.5 %collective-permute-start.7 = (s32[4,13]{1,0:T(4,128)S(1)}, s32[4,13]{1,0:T(4,128)S(1)}, u32[]{:S(2)}, u32[]{:S(2)}) collective-permute-start(s32[4,13]{1,0:T(4,128)S(1)} %pad_add_fusion.2), channel_id=1, source_target_pairs={{0,2},{2,0},{4,6},{6,4},{8,10},{10,8},{12,14},{14,12},{1,3},{3,1},... | collective-permute-start | bytes 632 | tf_op jit(solution)/shard_map/ppermute | solution.py:188
  26.1 2.3 %collective-permute-start.10 = (bf16[128,256]{1,0:T(8,128)(2,1)}, bf16[128,256]{1,0:T(8,128)(2,1)S(1)}, u32[]{:S(2)}, u32[]{:S(2)}) collective-permute-start(bf16[128,256]{1,0:T(8,128)(2,1)} %get-tuple-element.50), channel_id=1, source_target_pairs={{0,4},{2,6},{4,0},{6,2},{8,12},{10,14},{12,8},{14,10},{1,5},{3,7},... | collective-permute-start | bytes 196616 | tf_op jit(solution)/shard_map/ppermute | solution.py:192
  28.4 1.0 %collective-permute-start.11 = (bf16[128,256]{1,0:T(8,128)(2,1)}, bf16[128,256]{1,0:T(8,128)(2,1)S(1)}, u32[]{:S(2)}, u32[]{:S(2)}) collective-permute-start(bf16[128,256]{1,0:T(8,128)(2,1)} %get-tuple-element.51), channel_id=1, source_target_pairs={{0,8},{2,10},{4,12},{6,14},{8,0},{10,2},{12,4},{14,6},{1,9},{3,11}... | collective-permute-start | bytes 196616 | tf_op jit(solution)/shard_map/ppermute | solution.py:192
  29.5 0.0 collective-permute-done.7
  29.5 3.3 %collective-permute-start.12 = (bf16[128,256]{1,0:T(8,128)(2,1)S(1)}, bf16[128,256]{1,0:T(8,128)(2,1)S(1)}, u32[]{:S(2)}, u32[]{:S(2)}) collective-permute-start(bf16[128,256]{1,0:T(8,128)(2,1)S(1)} %get-tuple-element.52), channel_id=1, source_target_pairs={{0,12},{2,14},{4,8},{6,10},{8,4},{10,6},{12,0},{14,2},{1,13},{3,15... | collective-permute-start | bytes 196616 | tf_op jit(solution)/shard_map/ppermute | solution.py:192
  32.7 0.2 select_reduce_fusion.1
  32.9 0.2 select_reduce_fusion
  33.1 0.1 copy.12
  33.2 0.1 copy.13
  33.3 0.1 pad_add_fusion.1.table
  33.4 0.0 copy-done.2
  33.4 1.5 %pick_pages.1 = (bf16[2,2,64,128]{3,2,1,0:T(8,128)(2,1)S(1)}, bf16[2,2,64,128]{3,2,1,0:T(8,128)(2,1)S(1)}, bf16[2,2,64,128]{3,2,1,0:T(8,128)(2,1)S(1)}, bf16[2,2...) custom-call(s32[8,3]{1,0:T(8,128)S(1)} %pad_add_fusion.1.table, bf16[16,2,64,128]{3,2,1,0:T(8,128)(2,1)S(1)} %copy-done.2), custom_call_target="tpu_custom_call" | custom-call | flops 3449999872 | tf_op jit(solution)/shard_map/pick_pages/pallas_call | solution.py:328
  34.8 0.0 collective-permute-done.8.refs_9_
  34.8 0.0 collective-permute-done.9.refs_10_
  34.9 0.0 collective-permute-done.10.refs_1_
  34.9 1.8 %collective-permute-done.11.refs_2_ = bf16[128,256]{1,0:T(8,128)(2,1)S(1)} collective-permute-done((bf16[128,256]{1,0:T(8,128)(2,1)}, bf16[128,256]{1,0:T(8,128)(2,1)S(1)}, u32[]{:S(2)}, u32[]{:S(2)}) %collective-permute-start.11) | collective-permute-done | bytes 65568 | tf_op jit(solution)/shard_map/ppermute | solution.py:192
  36.7 0.0 collective-permute-done.12.refs_3_
  36.7 1.2 %products.3 = (f32[256,512]{1,0:T(8,128)S(1)}, bf16[256,512]{1,0:T(8,128)(2,1)S(1)}) custom-call(s32[2]{0:T(128)S(1)} %pad_add_fusion.3.place, bf16[128,512]{1,0:T(8,128)(2,1)S(1)} %copy-done.3, bf16[144,512]{1,0:T(8,128)(2,1)S(1)} %collective-permute-done.refs_1_, bf16[144,512]{1,0:T(8,128)(2,1)S(1)} %collective-permute-done.1.refs_2_, ...), custom_call_target="tpu_custom_call" | custom-call | flops 11500000256 | tf_op jit(solution)/shard_map/products/pallas_call | solution.py:140
  38.0 1.3 %collective-permute-start.13 = (bf16[256,512]{1,0:T(8,128)(2,1)S(1)}, bf16[256,512]{1,0:T(8,128)(2,1)S(1)}, u32[]{:S(2)}, u32[]{:S(2)}) collective-permute-start(bf16[256,512]{1,0:T(8,128)(2,1)S(1)} %get-tuple-element.57), channel_id=1, source_target_pairs={{0,4},{2,6},{4,0},{6,2},{8,12},{10,14},{12,8},{14,10},{1,5},{3,7},... | collective-permute-start | bytes 786440 | tf_op jit(solution)/shard_map/ppermute | solution.py:192
  39.3 0.3 fusion
  39.6 0.1 pad_maximum_fusion.refs_4_.refs_3_
  39.7 0.8 %collective-permute-start.14 = (bf16[2,2,64,128]{3,2,1,0:T(8,128)(2,1)S(1)}, bf16[2,2,64,128]{3,2,1,0:T(8,128)(2,1)S(1)}, u32[]{:S(2)}, u32[]{:S(2)}) collective-permute-start(bf16[2,2,64,128]{3,2,1,0:T(8,128)(2,1)S(1)} %get-tuple-element.65), channel_id=1, source_target_pairs={{0,4},{2,6},{4,0},{6,2},{8,12},{10,14},{12,8},{14,10},{1,5},{3,7},... | collective-permute-start | bytes 196616 | tf_op jit(solution)/shard_map/ppermute | solution.py:192
  40.5 2.1 %collective-permute-start.15 = (bf16[2,2,64,128]{3,2,1,0:T(8,128)(2,1)S(1)}, bf16[2,2,64,128]{3,2,1,0:T(8,128)(2,1)S(1)}, u32[]{:S(2)}, u32[]{:S(2)}) collective-permute-start(bf16[2,2,64,128]{3,2,1,0:T(8,128)(2,1)S(1)} %get-tuple-element.66), channel_id=1, source_target_pairs={{0,8},{2,10},{4,12},{6,14},{8,0},{10,2},{12,4},{14,6},{1,9},{3,11}... | collective-permute-start | bytes 196616 | tf_op jit(solution)/shard_map/ppermute | solution.py:192
  42.6 1.5 %collective-permute-start.16 = (bf16[2,2,64,128]{3,2,1,0:T(8,128)(2,1)S(1)}, bf16[2,2,64,128]{3,2,1,0:T(8,128)(2,1)S(1)}, u32[]{:S(2)}, u32[]{:S(2)}) collective-permute-start(bf16[2,2,64,128]{3,2,1,0:T(8,128)(2,1)S(1)} %get-tuple-element.67), channel_id=1, source_target_pairs={{0,12},{2,14},{4,8},{6,10},{8,4},{10,6},{12,0},{14,2},{1,13},{3,15... | collective-permute-start | bytes 196616 | tf_op jit(solution)/shard_map/ppermute | solution.py:192
  44.2 0.1 pad_maximum_fusion.1.refs_5_.refs_4_
  44.2 1.3 %fresh_pages.1 = (bf16[128,128]{1,0:T(8,128)(2,1)S(1)}, bf16[128,128]{1,0:T(8,128)(2,1)S(1)}, bf16[8,2,64,128]{3,2,1,0:T(8,128)(2,1)}) custom-call(s32[1,13]{1,0:T(1,128)S(1)} %copy-done.1, f32[128,256]{1,0:T(8,128)S(1)} %get-tuple-element.58.refs_0_, bf16[128,256]{1,0:T(8,128)(2,1)S(1)} %collective-permute-done.10.refs_1_, ...), custom_call_target="tpu_custom_call" | custom-call | tf_op jit(solution)/shard_map/fresh_pages/pallas_call | solution.py:398
  45.5 1.4 %collective-permute-done.13.arrived.refs_1_ = bf16[256,512]{1,0:T(8,128)(2,1)S(1)} collective-permute-done((bf16[256,512]{1,0:T(8,128)(2,1)S(1)}, bf16[256,512]{1,0:T(8,128)(2,1)S(1)}, u32[]{:S(2)}, u32[]{:S(2)}) %collective-permute-start.13) | collective-permute-done | bytes 262176 | tf_op jit(solution)/shard_map/ppermute | solution.py:192
  46.9 0.7 %collective-permute-done.14.refs_1_.refs_8_ = bf16[2,2,64,128]{3,2,1,0:T(8,128)(2,1)S(1)} collective-permute-done((bf16[2,2,64,128]{3,2,1,0:T(8,128)(2,1)S(1)}, bf16[2,2,64,128]{3,2,1,0:T(8,128)(2,1)S(1)}, u32[]{:S(2)}, u32[]{:S(2)}) %collective-permute-start.14) | collective-permute-done | bytes 65568 | tf_op jit(solution)/shard_map/ppermute | solution.py:192
  47.6 0.0 collective-permute-done.15.refs_2_.refs_9_
  47.6 3.5 %collective-permute-done.16.refs_3_.refs_10_ = bf16[2,2,64,128]{3,2,1,0:T(8,128)(2,1)S(1)} collective-permute-done((bf16[2,2,64,128]{3,2,1,0:T(8,128)(2,1)S(1)}, bf16[2,2,64,128]{3,2,1,0:T(8,128)(2,1)S(1)}, u32[]{:S(2)}, u32[]{:S(2)}) %collective-permute-start.16) | collective-permute-done | bytes 65568 | tf_op jit(solution)/shard_map/ppermute | solution.py:192
  51.1 0.1 collective-permute-start.17
  51.2 0.4 collective-permute-start.18
  51.6 5.3 %all-to-all-start = ((bf16[8,2,64,128]{3,2,1,0:T(8,128)(2,1)}), bf16[8,2,64,128]{3,2,1,0:T(8,128)(2,1)S(1)}, u32[]{:S(2)}, u32[]{:S(2)}) async-start(bf16[8,2,64,128]{3,2,1,0:T(8,128)(2,1)} %get-tuple-element.72), calls=%async_computation | async-start | bytes 524288 | tf_op jit(solution)/shard_map/all_to_all | solution.py:518
  56.9 1.0 %collective-permute-done.17.refs_2_ = bf16[128,512]{1,0:T(8,128)(2,1)S(1)} collective-permute-done((bf16[128,512]{1,0:T(8,128)(2,1)S(1)}, bf16[128,512]{1,0:T(8,128)(2,1)S(1)}, u32[]{:S(2)}, u32[]{:S(2)}) %collective-permute-start.17) | collective-permute-done | bytes 131104 | tf_op jit(solution)/shard_map/ppermute | solution.py:192
  57.9 0.0 collective-permute-done.18.refs_11_
  57.9 2.0 %attend.1 = bf16[128,512]{1,0:T(8,128)(2,1)} custom-call(s32[2]{0:T(128)S(1)} %pad_add_fusion.3.place, s32[1,13]{1,0:T(1,128)S(1)} %copy-done.1, f32[256,512]{1,0:T(8,128)S(1)} %get-tuple-element.56.kept.refs_0_, bf16[256,512]{1,0:T(8,128)(2,1)S(1)} %collective-permute-done.13.arrived.refs_1_, bf16[128,512]{1,0:T(8,128)(2,1)S(1)} %collective-permute-done.17.refs_2_, ...), custom_call_target="tpu_custom_call" | custom-call | flops 11500000256 | tf_op jit(solution)/shard_map/attend/pallas_call | solution.py:487
  59.9 5.2 %all-to-all-done.incoming = bf16[8,2,64,128]{3,2,1,0:T(8,128)(2,1)S(1)} async-done(((bf16[8,2,64,128]{3,2,1,0:T(8,128)(2,1)}), bf16[8,2,64,128]{3,2,1,0:T(8,128)(2,1)S(1)}, u32[]{:S(2)}, u32[]{:S(2)}) %all-to-all-start) | async-done | bytes 262176 | tf_op jit(solution)/shard_map/all_to_all | solution.py:518
  65.1 1.3 %land_pages.1 = bf16[16,2,64,128]{3,2,1,0:T(8,128)(2,1)} custom-call(s32[8,3]{1,0:T(8,128)S(1)} %pad_add_fusion.1.table, bf16[8,2,64,128]{3,2,1,0:T(8,128)(2,1)S(1)} %all-to-all-done.incoming, bf16[16,2,64,128]{3,2,1,0:T(8,128)(2,1)} %get-tuple-element.73._), custom_call_target="tpu_custom_call", output_to_operand_aliasing={{}: (2, {})} | custom-call | tf_op jit(solution)/shard_map/land_pages/pallas_call | solution.py:359
  (11 shorter events, 0.1 us)
Async XLA Ops:
  0.6 8.9 %copy-start = (bf16[512,1,6,128]{3,0,2,1:T(8,128)(2,1)S(1)}, bf16[512,1,6,128]{3,0,2,1:T(8,128)(2,1)}, u32[]{:S(2)}) copy-start(bf16[512,1,6,128]{3,0,2,1:T(8,128)(2,1)} %param.17) | copy-start | bytes 2359300
  3.9 9.2 %collective-permute-start = (bf16[144,512]{1,0:T(8,128)(2,1)}, bf16[144,512]{1,0:T(8,128)(2,1)S(1)}, u32[]{:S(2)}, u32[]{:S(2)}) collective-permute-start(bf16[144,512]{1,0:T(8,128)(2,1)} %get-tuple-element.39), channel_id=1, source_target_pairs={{0,4},{2,6},{4,0},{6,2},{8,12},{10,14},{12,8},{14,10},{1,5},{3,7},... | collective-permute-start | bytes 442376 | tf_op jit(solution)/shard_map/ppermute | solution.py:192
  7.0 14.2 %collective-permute-start.1 = (bf16[144,512]{1,0:T(8,128)(2,1)}, bf16[144,512]{1,0:T(8,128)(2,1)S(1)}, u32[]{:S(2)}, u32[]{:S(2)}) collective-permute-start(bf16[144,512]{1,0:T(8,128)(2,1)} %get-tuple-element.40), channel_id=1, source_target_pairs={{0,8},{2,10},{4,12},{6,14},{8,0},{10,2},{12,4},{14,6},{1,9},{3,11}... | collective-permute-start | bytes 442376 | tf_op jit(solution)/shard_map/ppermute | solution.py:192
  9.5 11.6 %collective-permute-start.2 = (bf16[144,512]{1,0:T(8,128)(2,1)}, bf16[144,512]{1,0:T(8,128)(2,1)S(1)}, u32[]{:S(2)}, u32[]{:S(2)}) collective-permute-start(bf16[144,512]{1,0:T(8,128)(2,1)} %get-tuple-element.41), channel_id=1, source_target_pairs={{0,12},{2,14},{4,8},{6,10},{8,4},{10,6},{12,0},{14,2},{1,13},{3,15... | collective-permute-start | bytes 442376 | tf_op jit(solution)/shard_map/ppermute | solution.py:192
  9.6 13.5 %copy-start.3 = (bf16[128,512]{1,0:T(8,128)(2,1)S(1)}, bf16[128,512]{1,0:T(8,128)(2,1)}, u32[]{:S(2)}) copy-start(bf16[128,512]{1,0:T(8,128)(2,1)} %get-tuple-element.45.refs_0_) | copy-start | bytes 393220
  9.6 13.5 %copy-start.4 = (bf16[128,512]{1,0:T(8,128)(2,1)S(1)}, bf16[128,512]{1,0:T(8,128)(2,1)}, u32[]{:S(2)}) copy-start(bf16[128,512]{1,0:T(8,128)(2,1)} %get-tuple-element.46.refs_4_) | copy-start | bytes 393220
  10.4 10.7 %collective-permute-start.3 = (bf16[2,512,128]{2,1,0:T(8,128)(2,1)S(1)}, bf16[2,512,128]{2,1,0:T(8,128)(2,1)S(1)}, u32[]{:S(2)}, u32[]{:S(2)}) collective-permute-start(bf16[2,512,128]{2,1,0:T(8,128)(2,1)S(1)} %get-tuple-element.76), channel_id=1, source_target_pairs={{0,2},{2,0},{4,6},{6,4},{8,10},{10,8},{12,14},{14,12},{1,3},{3,1},... | collective-permute-start | bytes 786440 | tf_op jit(solution)/shard_map/ppermute | solution.py:188
  12.1 22.7 %collective-permute-start.8 = (bf16[2,512,128]{2,1,0:T(8,128)(2,1)}, bf16[2,512,128]{2,1,0:T(8,128)(2,1)S(1)}, u32[]{:S(2)}, u32[]{:S(2)}) collective-permute-start(bf16[2,512,128]{2,1,0:T(8,128)(2,1)} %get-tuple-element.75), channel_id=1, source_target_pairs={{0,2},{2,0},{4,6},{6,4},{8,10},{10,8},{12,14},{14,12},{1,3},{3,1},... | collective-permute-start | bytes 786440 | tf_op jit(solution)/shard_map/ppermute | solution.py:188
  13.0 21.8 %collective-permute-start.9 = (bf16[2,512,128]{2,1,0:T(8,128)(2,1)}, bf16[2,512,128]{2,1,0:T(8,128)(2,1)S(1)}, u32[]{:S(2)}, u32[]{:S(2)}) collective-permute-start(bf16[2,512,128]{2,1,0:T(8,128)(2,1)} %get-tuple-element.74), channel_id=1, source_target_pairs={{0,2},{2,0},{4,6},{6,4},{8,10},{10,8},{12,14},{14,12},{1,3},{3,1},... | collective-permute-start | bytes 786440 | tf_op jit(solution)/shard_map/ppermute | solution.py:188
  21.2 1.9 %collective-permute-start.5 = (bf16[144,512]{1,0:T(8,128)(2,1)S(1)}, bf16[144,512]{1,0:T(8,128)(2,1)S(1)}, u32[]{:S(2)}, u32[]{:S(2)}) collective-permute-start(bf16[144,512]{1,0:T(8,128)(2,1)S(1)} %collective-permute-done.1.refs_2_), channel_id=1, source_target_pairs={{0,1},{1,0},{2,3},{3,2},{4,5},{5,4},{6,7},{7,6},{8,9},{9,8},{10,11... | collective-permute-start | bytes 442376 | tf_op jit(solution)/shard_map/ppermute | solution.py:210
  21.2 1.9 %collective-permute-start.6 = (bf16[144,512]{1,0:T(8,128)(2,1)S(1)}, bf16[144,512]{1,0:T(8,128)(2,1)S(1)}, u32[]{:S(2)}, u32[]{:S(2)}) collective-permute-start(bf16[144,512]{1,0:T(8,128)(2,1)S(1)} %collective-permute-done.2.refs_3_), channel_id=1, source_target_pairs={{0,1},{1,0},{2,3},{3,2},{4,5},{5,4},{6,7},{7,6},{8,9},{9,8},{10,11... | collective-permute-start | bytes 442376 | tf_op jit(solution)/shard_map/ppermute | solution.py:210
  21.7 1.4 %collective-permute-start.4 = (bf16[144,512]{1,0:T(8,128)(2,1)S(1)}, bf16[144,512]{1,0:T(8,128)(2,1)S(1)}, u32[]{:S(2)}, u32[]{:S(2)}) collective-permute-start(bf16[144,512]{1,0:T(8,128)(2,1)S(1)} %collective-permute-done.refs_1_), channel_id=1, source_target_pairs={{0,1},{1,0},{2,3},{3,2},{4,5},{5,4},{6,7},{7,6},{8,9},{9,8},{10,11... | collective-permute-start | bytes 442376 | tf_op jit(solution)/shard_map/ppermute | solution.py:210
  21.8 0.6 copy-start.1
  23.1 10.3 %copy-start.2 = (bf16[16,2,64,128]{3,2,1,0:T(8,128)(2,1)S(1)}, bf16[16,2,64,128]{3,2,1,0:T(8,128)(2,1)}, u32[]{:S(2)}) copy-start(bf16[16,2,64,128]{3,2,1,0:T(8,128)(2,1)} %pool.1) | copy-start | bytes 1572868
  24.7 4.8 %collective-permute-start.7 = (s32[4,13]{1,0:T(4,128)S(1)}, s32[4,13]{1,0:T(4,128)S(1)}, u32[]{:S(2)}, u32[]{:S(2)}) collective-permute-start(s32[4,13]{1,0:T(4,128)S(1)} %pad_add_fusion.2), channel_id=1, source_target_pairs={{0,2},{2,0},{4,6},{6,4},{8,10},{10,8},{12,14},{14,12},{1,3},{3,1},... | collective-permute-start | bytes 632 | tf_op jit(solution)/shard_map/ppermute | solution.py:188
  26.1 8.7 %collective-permute-start.10 = (bf16[128,256]{1,0:T(8,128)(2,1)}, bf16[128,256]{1,0:T(8,128)(2,1)S(1)}, u32[]{:S(2)}, u32[]{:S(2)}) collective-permute-start(bf16[128,256]{1,0:T(8,128)(2,1)} %get-tuple-element.50), channel_id=1, source_target_pairs={{0,4},{2,6},{4,0},{6,2},{8,12},{10,14},{12,8},{14,10},{1,5},{3,7},... | collective-permute-start | bytes 196616 | tf_op jit(solution)/shard_map/ppermute | solution.py:192
  28.4 8.3 %collective-permute-start.11 = (bf16[128,256]{1,0:T(8,128)(2,1)}, bf16[128,256]{1,0:T(8,128)(2,1)S(1)}, u32[]{:S(2)}, u32[]{:S(2)}) collective-permute-start(bf16[128,256]{1,0:T(8,128)(2,1)} %get-tuple-element.51), channel_id=1, source_target_pairs={{0,8},{2,10},{4,12},{6,14},{8,0},{10,2},{12,4},{14,6},{1,9},{3,11}... | collective-permute-start | bytes 196616 | tf_op jit(solution)/shard_map/ppermute | solution.py:192
  29.5 7.2 %collective-permute-start.12 = (bf16[128,256]{1,0:T(8,128)(2,1)S(1)}, bf16[128,256]{1,0:T(8,128)(2,1)S(1)}, u32[]{:S(2)}, u32[]{:S(2)}) collective-permute-start(bf16[128,256]{1,0:T(8,128)(2,1)S(1)} %get-tuple-element.52), channel_id=1, source_target_pairs={{0,12},{2,14},{4,8},{6,10},{8,4},{10,6},{12,0},{14,2},{1,13},{3,15... | collective-permute-start | bytes 196616 | tf_op jit(solution)/shard_map/ppermute | solution.py:192
  38.0 8.9 %collective-permute-start.13 = (bf16[256,512]{1,0:T(8,128)(2,1)S(1)}, bf16[256,512]{1,0:T(8,128)(2,1)S(1)}, u32[]{:S(2)}, u32[]{:S(2)}) collective-permute-start(bf16[256,512]{1,0:T(8,128)(2,1)S(1)} %get-tuple-element.57), channel_id=1, source_target_pairs={{0,4},{2,6},{4,0},{6,2},{8,12},{10,14},{12,8},{14,10},{1,5},{3,7},... | collective-permute-start | bytes 786440 | tf_op jit(solution)/shard_map/ppermute | solution.py:192
  39.7 7.9 %collective-permute-start.14 = (bf16[2,2,64,128]{3,2,1,0:T(8,128)(2,1)S(1)}, bf16[2,2,64,128]{3,2,1,0:T(8,128)(2,1)S(1)}, u32[]{:S(2)}, u32[]{:S(2)}) collective-permute-start(bf16[2,2,64,128]{3,2,1,0:T(8,128)(2,1)S(1)} %get-tuple-element.65), channel_id=1, source_target_pairs={{0,4},{2,6},{4,0},{6,2},{8,12},{10,14},{12,8},{14,10},{1,5},{3,7},... | collective-permute-start | bytes 196616 | tf_op jit(solution)/shard_map/ppermute | solution.py:192
  40.5 7.1 %collective-permute-start.15 = (bf16[2,2,64,128]{3,2,1,0:T(8,128)(2,1)S(1)}, bf16[2,2,64,128]{3,2,1,0:T(8,128)(2,1)S(1)}, u32[]{:S(2)}, u32[]{:S(2)}) collective-permute-start(bf16[2,2,64,128]{3,2,1,0:T(8,128)(2,1)S(1)} %get-tuple-element.66), channel_id=1, source_target_pairs={{0,8},{2,10},{4,12},{6,14},{8,0},{10,2},{12,4},{14,6},{1,9},{3,11}... | collective-permute-start | bytes 196616 | tf_op jit(solution)/shard_map/ppermute | solution.py:192
  42.6 8.5 %collective-permute-start.16 = (bf16[2,2,64,128]{3,2,1,0:T(8,128)(2,1)S(1)}, bf16[2,2,64,128]{3,2,1,0:T(8,128)(2,1)S(1)}, u32[]{:S(2)}, u32[]{:S(2)}) collective-permute-start(bf16[2,2,64,128]{3,2,1,0:T(8,128)(2,1)S(1)} %get-tuple-element.67), channel_id=1, source_target_pairs={{0,12},{2,14},{4,8},{6,10},{8,4},{10,6},{12,0},{14,2},{1,13},{3,15... | collective-permute-start | bytes 196616 | tf_op jit(solution)/shard_map/ppermute | solution.py:192
  51.1 6.7 %collective-permute-start.17 = (bf16[128,512]{1,0:T(8,128)(2,1)S(1)}, bf16[128,512]{1,0:T(8,128)(2,1)S(1)}, u32[]{:S(2)}, u32[]{:S(2)}) collective-permute-start(bf16[128,512]{1,0:T(8,128)(2,1)S(1)} %get-tuple-element.68), channel_id=1, source_target_pairs={{0,8},{2,10},{4,12},{6,14},{8,0},{10,2},{12,4},{14,6},{1,9},{3,11}... | collective-permute-start | bytes 393224 | tf_op jit(solution)/shard_map/ppermute | solution.py:192
  51.2 6.7 %collective-permute-start.18 = (bf16[4,2,64,128]{3,2,1,0:T(8,128)(2,1)S(1)}, bf16[4,2,64,128]{3,2,1,0:T(8,128)(2,1)S(1)}, u32[]{:S(2)}, u32[]{:S(2)}) collective-permute-start(bf16[4,2,64,128]{3,2,1,0:T(8,128)(2,1)S(1)} %get-tuple-element.70), channel_id=1, source_target_pairs={{0,2},{2,0},{4,6},{6,4},{8,10},{10,8},{12,14},{14,12},{1,3},{3,1},... | collective-permute-start | bytes 393224 | tf_op jit(solution)/shard_map/ppermute | solution.py:188
  51.6 13.5 %all-to-all-start = ((bf16[8,2,64,128]{3,2,1,0:T(8,128)(2,1)}), bf16[8,2,64,128]{3,2,1,0:T(8,128)(2,1)S(1)}, u32[]{:S(2)}, u32[]{:S(2)}) async-start(bf16[8,2,64,128]{3,2,1,0:T(8,128)(2,1)} %get-tuple-element.72), calls=%async_computation | async-start | bytes 524288 | tf_op jit(solution)/shard_map/all_to_all | solution.py:518

commit v6 on v5

--- a/solution.py
+++ b/solution.py
@@ -8,7 +8,7 @@
 from jax.experimental.pallas import tpu as pltpu
 from jax.sharding import PartitionSpec as P
 
-WAITS = dict(kv=30, q=10, pick=3, fresh=0, fold=0, attend=10, land=0, prepare=0)
+CFG = {'E': 'rec', 'P': [], 'Q': ['pick'], 'R': ['q'], 'G': ['pages'], 'X': ['fresh'], 'L': 0, 'W': 1, 'N': 0, 'V': 1, 'cost': {'prepare': 3, 'kv': 3, 'q': 0, 'fold': 0, 'pick': 10, 'fresh': 30, 'attend': 3, 'land': 3, 'relay': 10}}
 ANY = pl.BlockSpec(memory_space=pl.ANY)
 SCALARS = pl.BlockSpec(memory_space=pltpu.SMEM)
 VECTORS = pl.BlockSpec(memory_space=pltpu.VMEM)
@@ -16,7 +16,7 @@
 
 
 def wait(name):
-    return pl.CostEstimate(flops=int(WAITS[name] * 1.15e9), bytes_accessed=0, transcendentals=0)
+    return pl.CostEstimate(flops=int(CFG['cost'].get(name, 0) * 1.15e9), bytes_accessed=0, transcendentals=0)
 
 
 def tie(value, *others):
@@ -41,8 +41,7 @@
 
 
 def prepare_kernel(*refs):
-    arguments, pieces, numbers = refs[:7], refs[7:12], refs[12]
-    local_copies, semaphore = refs[13:20], refs[20]
+    arguments, pieces, local_copies, semaphore = refs[:7], refs[7:12], refs[12:19], refs[19]
     copies = [
         pltpu.make_async_copy(here, there, semaphore.at[index])
         for index, (here, there) in enumerate(zip(arguments, local_copies))
@@ -64,7 +63,6 @@
     column = lax.broadcasted_iota(jnp.int32, shape, 1)
     tail = jnp.zeros(shape, jnp.float32)
     for index, value in enumerate(values):
-        numbers[0, index] = value
         tail = jnp.where(column == index, value.astype(jnp.float32), tail)
     wide = tokens[...].astype(jnp.float32)
     row_scale = lax.rsqrt(jnp.sum(wide * wide, axis=1, keepdims=True) / width + 1e-05)
@@ -74,21 +72,17 @@
         span = pl.ds(pl.multiple_of((2 * target + half) * rows, 128), rows)
         part = tokens[:, span].astype(jnp.float32) * row_scale * gain[:, span]
         piece[:token_rows] = part.astype(piece.dtype)
-        if index > 1:
-            piece[token_rows:] = tail.astype(piece.dtype)
+        piece[token_rows:] = tail.astype(piece.dtype)
 
 
 def prepare(tokens, gain, pages_count, requests, rows):
     token_rows, width = tokens.shape
-    heights = [token_rows] * 2 + [token_rows + 16] * 3
     arguments = [tokens, gain.reshape(1, width), pages_count.reshape(1, 1)] + requests
-    count = 1 + sum(part.shape[1] for part in requests)
     return pl.pallas_call(
         prepare_kernel,
-        out_shape=[jax.ShapeDtypeStruct((height, rows), jnp.bfloat16) for height in heights]
-        + [jax.ShapeDtypeStruct((1, count), jnp.int32)],
+        out_shape=[jax.ShapeDtypeStruct((token_rows + 16, rows), jnp.bfloat16)] * 5,
         in_specs=[ANY] * 7,
-        out_specs=[VECTORS] * 5 + [SCALARS],
+        out_specs=[VECTORS] * 5,
         scratch_shapes=[pltpu.VMEM(value.shape, value.dtype) for value in arguments[:2]]
         + [pltpu.SMEM(value.shape, value.dtype) for value in arguments[2:]]
         + [pltpu.SemaphoreType.DMA((7,))],
@@ -105,9 +99,14 @@
 
 
 def product_kernel(place, *refs):
-    own_weight = refs[8]
-    other = [ref for ref in refs[9:] if len(ref.shape) == 3]
-    kept, *leaving = refs[9 + len(other) :]
+    weights = [ref for ref in refs[8:] if len(ref.shape) == 3]
+    own, other = weights[: len(weights) // 2], weights[len(weights) // 2 :]
+    kept, *leaving = refs[8 + len(weights) :]
+    if len(leaving) == 4:
+        table = leaving.pop()
+        for index, ref in enumerate(refs[:4]):
+            head = ref[kept.shape[0] : kept.shape[0] + 8, : table.shape[1]]
+            table[index : index + 1] = head.astype(jnp.float32)[:1].astype(jnp.int32)
     rows = leaving[-1].shape[0] // (1 if len(leaving) == 3 else 2)
     direct = jnp.concatenate([ref[:rows] for ref in refs[:4]], axis=0)
     passed = jnp.concatenate([ref[:rows] for ref in refs[4:8]], axis=0)
@@ -115,7 +114,7 @@
     for_own = jnp.where(own_first, direct, passed)
     for_other = jnp.where(own_first, passed, direct)
     result = jnp.dot(
-        for_own, side_by_side(own_weight), preferred_element_type=jnp.float32
+        for_own, side_by_side(*own), preferred_element_type=jnp.float32
     ) + jnp.dot(for_other, side_by_side(*other), preferred_element_type=jnp.float32)
     result = [result[index * rows : (index + 1) * rows] for index in range(4)]
     kept[:rows] = result[0]
@@ -128,60 +127,59 @@
         leaving[0][rows:] = result[3].astype(leaving[0].dtype)
 
 
-def products(place, direct, passed, own_weight, first, other, paired):
-    rows, head_size = direct[0].shape[0], own_weight.shape[2]
-    shapes = [(2 * rows, jnp.float32), (2 * rows, jnp.bfloat16)]
-    if not paired:
-        shapes = [(rows, jnp.float32)] + [(rows, jnp.bfloat16)] * 3
-    count = sum(part.shape[0] for part in other)
-    columns = count * head_size
-    depth = 2 * own_weight.shape[1]
-    blocks = pl.BlockSpec((count,) + own_weight.shape[1:], lambda step: (first // count, 0, 0))
+def products(place, direct, passed, own, other, paired):
+    rows = direct[0].shape[0] - 16
+    depth = 2 * own[0].shape[1]
+    columns = sum(part.shape[0] * part.shape[2] for part in own)
+    if paired:
+        shapes = [((2 * rows, columns), jnp.float32), ((2 * rows, columns), jnp.bfloat16)]
+    else:
+        shapes = [((rows, columns), jnp.float32)] + [((rows, columns), jnp.bfloat16)] * 3
+        shapes.append(((4, 128), jnp.int32))
     return pl.pallas_call(
         product_kernel,
-        grid=(1,),
-        out_shape=[jax.ShapeDtypeStruct((height, columns), kind) for height, kind in shapes],
-        in_specs=[SCALARS] + [VECTORS] * 8 + [blocks] + [VECTORS] * len(other),
+        out_shape=[jax.ShapeDtypeStruct(shape, kind) for shape, kind in shapes],
+        in_specs=[SCALARS] + [VECTORS] * (8 + 2 * len(own)),
         out_specs=[VECTORS] * len(shapes),
         compiler_params=PARAMS,
-        cost_estimate=wait("q" if first == 0 else "kv"),
+        cost_estimate=wait("q" if paired else "kv"),
         name="products",
-    )(place, *direct, *passed, own_weight, *other)
-
-
-def fold_kernel(kept, arrived, *refs):
-    pages, far, relay = refs[:4], refs[4], refs[5]
+    )(place, *direct, *passed, *own, *other)
+
+
+def fold_kernel(kept, arrived, far):
     rows = far.shape[0]
     far[...] = (kept[rows:] + arrived[rows:].astype(jnp.float32)).astype(far.dtype)
-    for index, page in enumerate(pages):
-        relay[index] = page[1]
-
-
-def fold(kept, arrived, pages):
+
+
+def fold(kept, arrived):
     rows, columns = kept.shape[0] // 2, kept.shape[1]
     return pl.pallas_call(
         fold_kernel,
-        out_shape=[
-            jax.ShapeDtypeStruct((rows, columns), jnp.bfloat16),
-            jax.ShapeDtypeStruct((4,) + pages[0].shape[1:], pages[0].dtype),
-        ],
-        in_specs=[VECTORS] * 6,
-        out_specs=[VECTORS] * 2,
+        out_shape=jax.ShapeDtypeStruct((rows, columns), jnp.bfloat16),
+        in_specs=[VECTORS] * 2,
+        out_specs=VECTORS,
         compiler_params=PARAMS,
         cost_estimate=wait("fold"),
         name="fold",
-    )(kept, arrived, *pages)
-
-
-def answer(numbers, prefix, me, ranks):
-    new_pages = (numbers.shape[1] - 1 - 2 * prefix) // 2
-    starts = [1, 1 + prefix, 1 + 2 * prefix, 1 + 2 * prefix + new_pages, numbers.shape[1]]
-    owners, slots, homes, home_slots = [
-        numbers[:, first:last] for first, last in zip(starts[:-1], starts[1:])
-    ]
-    asked = jnp.max(jnp.where(owners == me, slots, -1), axis=1)
-    replaced = jnp.max(jnp.where(homes == me, home_slots, -1), axis=1)
-    return jnp.stack([asked, replaced, ranks], axis=1).astype(jnp.int32)
+    )(kept, arrived)
+
+
+def relay_kernel(*refs):
+    for index, page in enumerate(refs[:4]):
+        refs[4][index] = page[1]
+
+
+def relay(pages):
+    return pl.pallas_call(
+        relay_kernel,
+        out_shape=jax.ShapeDtypeStruct((4,) + pages[0].shape[1:], pages[0].dtype),
+        in_specs=[VECTORS] * 4,
+        out_specs=VECTORS,
+        compiler_params=PARAMS,
+        cost_estimate=wait("relay"),
+        name="relay",
+    )(*pages)
 
 
 def near(values, ranks):
@@ -194,46 +192,62 @@
 
 def column_plan(tokens, gain, wqkv, pages_count, requests, pool, place, ranks):
     me = place[0]
-    rows = wqkv.shape[0]
-    blocks = wqkv.shape[2]
-    token_rows = tokens.shape[0]
     prefix = requests[0].shape[1]
     weight = wqkv[:, 0].transpose(1, 0, 2)
-    kv_other, *q_other = [
-        near(weight[first : first + 2], ranks) for first in range(blocks - 2, -1, -2)
-    ]
-    own_direct, own_passed, *pieces, numbers = prepare(tokens, gain, pages_count, requests, rows)
+    own_direct, own_passed, *pieces = prepare(tokens, gain, pages_count, requests, wqkv.shape[0])
+    if CFG["V"]:
+        weight = tie(weight, pieces[0])
+    *q_weight, kv_weight = [weight[first : first + 2] for first in range(0, weight.shape[0], 2)]
+    kv_other, *q_other = [near(part, ranks) for part in [kv_weight] + q_weight]
     direct = [None] * 3
     for step in (2, 3, 1):
         direct[step - 1] = along(pieces[step - 1], ranks, step)
-    direct = tie(direct, kv_other)
+    if CFG["W"]:
+        direct = tie(direct, kv_other)
     passed = [lax.ppermute(piece, "tp", crossed(2, 1)) for piece in direct]
-    table = [piece[token_rows : token_rows + 1, : numbers.shape[1]] for piece in direct]
-    table = jnp.concatenate([numbers] + [row.astype(jnp.int32) for row in table], axis=0)
     direct = [own_direct] + direct
     passed = [own_passed] + passed
 
-    kv_own, *leaving = products(place, direct, passed, weight, blocks - 2, [kv_other], False)
+    kv_own, *leaving, table = products(place, direct, passed, [kv_weight], [kv_other], False)
     kv_parts = [kv_own] + [along(part, ranks, step) for step, part in zip((1, 2, 3), leaving)]
-
-    table = tie(table, kv_own)
-    table = jnp.concatenate([table, near(table, ranks)], axis=0)
-    lanes = jnp.arange(ranks, dtype=jnp.int32)
-    table = answer(table, prefix, me, (2 * lanes % ranks + lanes // 4) ^ me)
-    *picked, copied = pick_pages(table, pool, 4)
-    pages = picked[:1] + [along(picked[step], ranks, step) for step in (1, 2, 3)]
-
-    q_other = tie(q_other[::-1], kv_parts, picked[0])
-    q_kept, leaving = products(place, direct, passed, weight, 0, q_other, True)
-    q_arrived = along(leaving, ranks, 1)
-    kv_parts = tie(kv_parts, q_kept)
+    state = dict(kv=kv_own, kvp=kv_parts, kvd=kv_parts[1])
+    get = lambda name: [state[k] for k in CFG[name]]
+
+    def pick():
+        t = [table, near(tie(table, *get("P")), ranks)]
+        *picked, state["copied"] = pick_pages(place, t, pool, prefix)
+        state["table"] = t
+        state["pick"] = picked[0]
+        state["pages"] = picked[:1] + [along(picked[step], ranks, step) for step in (1, 2, 3)]
+
+    def q():
+        w = tie(q_other, *get("Q"))
+        state["q"], *leaving = products(place, direct, passed, q_weight, w, CFG["E"] == "rec")
+        if CFG["E"] == "rec":
+            state["qa"] = along(leaving[0], ranks, 1)
+        else:
+            state["qp"] = [state["q"]] + [along(p, ranks, i) for i, p in zip((1, 2, 3), leaving)]
+            state["qa"] = state["qp"][1]
+
+    if "pick" in CFG["Q"]:
+        pick()
+        q()
+    else:
+        q()
+        pick()
+    kv_parts = tie(kv_parts, *get("R"))
 
     def finish(fresh):
-        far, relay = fold(q_kept, tie(q_arrived, fresh), pages)
-        relayed = near(relay, ranks)
-        return [q_kept, q_arrived, along(far, ranks, 2)], pages + [relayed]
-
-    return kv_parts, finish, table, copied, numbers
+        state["fresh"] = fresh
+        state["relay"] = tie(relay(state["pages"]), *get("X"))
+        relayed = near(state["relay"], ranks)
+        if CFG["E"] != "rec":
+            return state["qp"], state["pages"] + [relayed], state["qa"]
+        far = fold(state["q"], tie(state["qa"], *get("G")))
+        state["far"] = far
+        return [state["q"], state["qa"], along(far, ranks, 2)], state["pages"] + [relayed], far
+
+    return kv_parts, finish, state["table"], state["copied"], table
 
 
 def general_plan(tokens, gain, wqkv, pages_count, requests, pool, place, ranks):
@@ -272,101 +286,115 @@
     )
     total = jnp.sum(parts.astype(jnp.float32), axis=0)
     q_columns = (blocks - 2) * wqkv.shape[3]
-    lanes = jnp.arange(ranks, dtype=jnp.int32)
     listed = jnp.arange(prefix, dtype=jnp.int32) < pages_count[0]
     numbers = jnp.concatenate(
         [pages_count[:, None], jnp.where(listed, requests[0], -1)] + requests[1:], axis=1
     )
-    table = answer(jnp.broadcast_to(numbers, (ranks,) + numbers.shape[1:]), prefix, lanes[:, None], lanes)
-    table = lax.all_to_all(table[:, :2], "dp", split_axis=0, concat_axis=0, tiled=True)
-    table = jnp.concatenate([table, lanes[:, None]], axis=1)
-    chosen, copied = pick_pages(table, pool, 1)
+    table = [
+        lax.all_to_all(
+            jnp.broadcast_to(numbers, (ranks,) + numbers.shape[1:]),
+            "dp",
+            split_axis=0,
+            concat_axis=0,
+            tiled=True,
+        )
+    ]
+    chosen, copied = pick_pages(place, table, pool, prefix)
     replies = lax.all_to_all(chosen, "dp", split_axis=0, concat_axis=0, tiled=True)
 
     def finish(fresh):
-        return [total[:, :q_columns]], [replies]
+        return [total[:, :q_columns]], [replies], fresh
 
     return [total[:, q_columns:]], finish, table, copied, numbers
 
 
-def each_row(rows, visit):
-    if rows <= 8:
-        for row in range(rows):
-            visit(row)
-    else:
-        def step(row, carry):
-            visit(row)
-            return carry
-
-        lax.fori_loop(0, rows, step, 0)
-
-
-def pick_kernel(table, pool, *refs):
-    *outs, copied, semaphore = refs
-    rows = table.shape[0]
-    whole = pltpu.make_async_copy(pool, copied, semaphore.at[rows])
+def each_row(tables, visit):
+    base = 0
+    for table in tables:
+        rows = table.shape[0]
+        if rows <= 8:
+            for row in range(rows):
+                visit(table, row, base + row)
+        else:
+            def step(row, carry, table=table, base=base):
+                visit(table, row, base + row)
+                return carry
+
+            lax.fori_loop(0, rows, step, 0)
+        base += rows
+
+
+def slot_for(table, row, me, first, count):
+    slot = jnp.int32(-1)
+    for item in range(first, first + count):
+        slot = jnp.where(table[row, item] == me, table[row, item + count], slot)
+    return slot
+
+
+def pick_kernel(count, prefix, place, *refs):
+    tables, pool, copied, semaphore = refs[:count], refs[count], refs[-2], refs[-1]
+    outs = refs[count + 1 : -2]
+    whole = pltpu.make_async_copy(pool, copied, semaphore.at[semaphore.shape[0] - 1])
     whole.start()
 
-    def visit(act, row):
-        @pl.when(table[row, 0] >= 0)
+    def visit(act, table, row, index):
+        slot = slot_for(table, row, place[0], 1, prefix)
+
+        @pl.when(slot >= 0)
         def _():
-            place = (0, table[row, 2]) if len(outs) == 1 else (row % len(outs), row // len(outs))
-            act(
-                pltpu.make_async_copy(
-                    pool.at[table[row, 0]], outs[place[0]].at[place[1]], semaphore.at[row]
-                )
-            )
-
-    each_row(rows, functools.partial(visit, lambda copy: copy.start()))
-    each_row(rows, functools.partial(visit, lambda copy: copy.wait()))
+            target = outs[0].at[row] if count == 1 else outs[row].at[index // 4]
+            act(pltpu.make_async_copy(pool.at[slot], target, semaphore.at[index]))
+
+    each_row(tables, functools.partial(visit, lambda copy: copy.start()))
+    each_row(tables, functools.partial(visit, lambda copy: copy.wait()))
     whole.wait()
 
 
-def pick_pages(table, pool, count):
-    rows = table.shape[0]
+def pick_pages(place, tables, pool, prefix):
     page = pool.shape[1:]
-    return pl.pallas_call(
-        pick_kernel,
-        out_shape=[jax.ShapeDtypeStruct((rows // count,) + page, pool.dtype)] * count
+    rows = sum(table.shape[0] for table in tables)
+    heights = [rows] if len(tables) == 1 else [len(tables)] * 4
+    return pl.pallas_call(
+        functools.partial(pick_kernel, len(tables), prefix),
+        out_shape=[jax.ShapeDtypeStruct((height,) + page, pool.dtype) for height in heights]
         + [jax.ShapeDtypeStruct(pool.shape, pool.dtype)],
-        in_specs=[SCALARS, ANY],
-        out_specs=[ANY] * (count + 1),
+        in_specs=[SCALARS] * (1 + len(tables)) + [ANY],
+        out_specs=[ANY] * (len(heights) + 1),
         scratch_shapes=[pltpu.SemaphoreType.DMA((rows + 1,))],
         compiler_params=PARAMS,
         cost_estimate=wait("pick"),
         name="pick_pages",
-    )(table, pool)
-
-
-def land_kernel(table, incoming, _, pool, semaphore):
+    )(place, *tables, pool)
+
+
+def land_kernel(count, first, new_pages, place, *refs):
+    tables, incoming, pool, semaphore = refs[:count], refs[count], refs[-2], refs[-1]
+
+    def visit(act, table, row, index):
+        slot = slot_for(table, row, place[0], first, new_pages)
+        rank = row if count == 1 else place[0] ^ (2 * row + index // 4)
+
+        @pl.when(slot >= 0)
+        def _():
+            act(pltpu.make_async_copy(incoming.at[rank], pool.at[slot], semaphore.at[index]))
+
+    each_row(tables, functools.partial(visit, lambda copy: copy.start()))
+    each_row(tables, functools.partial(visit, lambda copy: copy.wait()))
+
+
+def land_pages(place, tables, incoming, pool, first, new_pages):
     ranks = incoming.shape[0]
-
-    def visit(act, row):
-        @pl.when(table[row, 1] >= 0)
-        def _():
-            act(
-                pltpu.make_async_copy(
-                    incoming.at[table[row, 2]], pool.at[table[row, 1]], semaphore.at[row]
-                )
-            )
-
-    each_row(ranks, functools.partial(visit, lambda copy: copy.start()))
-    each_row(ranks, functools.partial(visit, lambda copy: copy.wait()))
-
-
-def land_pages(table, incoming, pool):
-    ranks = incoming.shape[0]
-    return pl.pallas_call(
-        land_kernel,
+    return pl.pallas_call(
+        functools.partial(land_kernel, len(tables), first, new_pages),
         out_shape=jax.ShapeDtypeStruct(pool.shape, pool.dtype),
-        in_specs=[SCALARS, ANY, ANY],
+        in_specs=[SCALARS] * (1 + len(tables)) + [ANY, ANY],
         out_specs=ANY,
         scratch_shapes=[pltpu.SemaphoreType.DMA((ranks,))],
-        input_output_aliases={2: 0},
+        input_output_aliases={2 + len(tables): 0},
         compiler_params=PARAMS,
         cost_estimate=wait("land"),
         name="land_pages",
-    )(table, incoming, pool)
+    )(place, *tables, incoming, pool)
 
 
 def fresh_kernel(pieces, first, numbers, *refs):
@@ -515,13 +543,20 @@
     keys_new, values_new, outgoing = fresh_pages(
         numbers, 1 + 2 * prefix, new_pages, kv_parts, cosine, sine, ranks, page_rows
     )
+    q_parts, pages, far = finish(keys_new)
+    if CFG["N"]:
+        outgoing = tie(outgoing, far)
     incoming = lax.all_to_all(outgoing, "dp", split_axis=0, concat_axis=0, tiled=True)
-    q_parts, pages = finish(keys_new)
+    if CFG["L"] == 2:
+        pool_out = land_pages(place, table, incoming, copied, 1 + 2 * prefix, new_pages)
+        q_parts = tie(q_parts, pool_out)
     attended = attend(
         place, numbers, prefix, q_parts, cosine, sine, keys_new, values_new, pages
     )
-    copied, attended = lax.optimization_barrier((copied, attended))
-    pool_out = land_pages(table, incoming, copied)
+    if CFG["L"] < 2:
+        if CFG["L"]:
+            copied, attended = lax.optimization_barrier((copied, attended))
+        pool_out = land_pages(place, table, incoming, copied, 1 + 2 * prefix, new_pages)
     return (attended, pool_out)
 
 

time: 66.7 us -> 61.5 us (0.922)
  local copies, waits for them, and re-layouts: 1.66 us -> 0.08 us
  starting transfers between devices: 29.6 us -> 28.2 us
  waiting for transfers between devices: 21.2 us -> 20.1 us
    all_to_all x1, waiting for transfers between devices: 5.24 us -> 0.01 us  [local(): lax.all_to_all(outgoing, 'dp', split_axis=0, concat_axis=0, tiled=True)]
    ppermute x11, waiting for transfers between devices: 15.3 us -> 18.3 us  [along(): return lax.ppermute(values, 'dp', crossed(ranks, 2 * step))]
    ppermute x11, starting transfers between devices: 18.1 us -> 15.2 us  [along(): return lax.ppermute(values, 'dp', crossed(ranks, 2 * step))]
    ppermute x5, starting transfers between devices: 5.62 us -> 7.98 us  [near(): return lax.ppermute(values, 'dp', crossed(ranks, 1))]
    all_to_all x1, starting transfers between devices: 5.29 us -> 4.4 us  [local(): lax.all_to_all(outgoing, 'dp', split_axis=0, concat_axis=0, tiled=True)]
    ppermute x5, waiting for transfers between devices: 0.01 us -> 0.89 us  [near(): return lax.ppermute(values, 'dp', crossed(ranks, 1))]
    slice x1, local copies, waits for them, and re-layouts: 0.86 us -> 0.05 us  [column_plan(): weight[first:first + 2]]
    pallas_call x6 -> x7, Pallas kernels: 8.11 us -> 7.62 us  [the longest x1 2.56 us: prepare(): pl.pallas_call(prepare_kernel, out_shape=[jax.ShapeDtypeStruct((token_row...]
  transfers between devices with their start and end apart: 20 -> 20, of which waited for: 9 -> 8; matrix products, arithmetic and copies ran while one was open for 3% -> 1% of each run, Pallas kernels for 9% -> 11%
where the time goes in v6:
time: 61.5 us; the launch traced here: 61.2 us
  starting transfers between devices  28.2 us (46%)
  waiting for transfers between devices  20.1 us (33%)
  Pallas kernels  10.9 us (18%)
  between operations  1.48 us (2%)
    ppermute x11, waiting for transfers between devices, along(): return lax.ppermute(values, 'dp', crossed(ranks, 2 * step))  18.3 us
    ppermute x11, starting transfers between devices, along(): return lax.ppermute(values, 'dp', crossed(ranks, 2 * step))  15.2 us
    ppermute x5, starting transfers between devices, near(): return lax.ppermute(values, 'dp', crossed(ranks, 1))  7.98 us
    all_to_all x1, starting transfers between devices, local(): lax.all_to_all(outgoing, 'dp', split_axis=0, concat_axis=0, tiled=True)  4.4 us
    pallas_call x1, Pallas kernels, prepare(): pl.pallas_call(prepare_kernel, out_shape=[jax.ShapeDtypeStruct((token_row...  2.56 us
    pallas_call x2, Pallas kernels, products(): pl.pallas_call(product_kernel, out_shape=[jax.ShapeDtypeStruct(shape, kin...  2.22 us
    pallas_call x1, Pallas kernels, attend(): pl.pallas_call(functools.partial(attend_kernel, len(parts), together, pre...  1.99 us
    pallas_call x1, Pallas kernels, pick_pages(): pl.pallas_call(functools.partial(pick_kernel, len(tables), prefix), out_s...  1.47 us
  transfers between devices with their start and end apart: 20, of which 8 were waited for; matrix products, arithmetic and copies ran while one was open for 1% of the time, Pallas kernels for 11%

profile of v6, /device:TPU:0, one launch (start us, length us, event | category | flops | bytes accessed | tf_op | source)
XLA Modules:
  0.0 61.2 jit_solution(4481743740696396216)
XLA Ops:
  1.3 0.0 copy-start.3
  1.3 2.6 %prepare.1 = (bf16[144,512]{1,0:T(8,128)(2,1)}, bf16[144,512]{1,0:T(8,128)(2,1)}, bf16[144,512]{1,0:T(8,128)(2,1)}, bf16[144,512]{1,0:T(8,128)(2,1)}, bf16[144,512]{1,0:T(8,128)(2,1)}) custom-call(bf16[128,4096]{1,0:T(8,128)(2,1)} %refs_0_.1, f32[1,4096]{1,0:T(1,128)} %bitcast.11, s32[1,1]{1,0:T(1,128)} %bitcast.9.refs_2_, s32[1,4]{1,0:T(1,128)} %refs_3_.1, ...), custom_call_target="tpu_custom_call" | custom-call | flops 3449999872 | tf_op jit(solution)/shard_map/prepare/pallas_call | solution.py:81
  3.9 0.0 copy-done.3
  3.9 0.0 copy-start.6
  3.9 0.0 copy-start.5
  3.9 0.0 copy-start.4
  3.9 0.0 copy-start.1
  3.9 0.1 fusion.1
  4.0 0.0 copy-start
  4.0 3.0 %collective-permute-start.3 = (bf16[2,512,128]{2,1,0:T(8,128)(2,1)S(1)}, bf16[2,512,128]{2,1,0:T(8,128)(2,1)S(1)}, u32[]{:S(2)}, u32[]{:S(2)}) collective-permute-start(bf16[2,512,128]{2,1,0:T(8,128)(2,1)S(1)} %get-tuple-element.70.refs_8_), channel_id=1, source_target_pairs={{0,2},{2,0},{4,6},{6,4},{8,10},{10,8},{12,14},{14,12},{1,3},{3,1},... | collective-permute-start | bytes 786440 | tf_op jit(solution)/shard_map/ppermute | solution.py:186
  7.0 0.0 copy-done.6
  7.0 1.6 %collective-permute-start = (bf16[144,512]{1,0:T(8,128)(2,1)S(1)}, bf16[144,512]{1,0:T(8,128)(2,1)S(1)}, u32[]{:S(2)}, u32[]{:S(2)}) collective-permute-start(bf16[144,512]{1,0:T(8,128)(2,1)S(1)} %copy-done.6), channel_id=1, source_target_pairs={{0,4},{2,6},{4,0},{6,2},{8,12},{10,14},{12,8},{14,10},{1,5},{3,7},... | collective-permute-start | bytes 442376 | tf_op jit(solution)/shard_map/ppermute | solution.py:190
  8.6 0.0 copy-done.5
  8.6 2.6 %collective-permute-start.1 = (bf16[144,512]{1,0:T(8,128)(2,1)S(1)}, bf16[144,512]{1,0:T(8,128)(2,1)S(1)}, u32[]{:S(2)}, u32[]{:S(2)}) collective-permute-start(bf16[144,512]{1,0:T(8,128)(2,1)S(1)} %copy-done.5), channel_id=1, source_target_pairs={{0,8},{2,10},{4,12},{6,14},{8,0},{10,2},{12,4},{14,6},{1,9},{3,11}... | collective-permute-start | bytes 442376 | tf_op jit(solution)/shard_map/ppermute | solution.py:190
  11.2 0.0 copy-done.4
  11.2 0.2 collective-permute-start.2
  11.4 0.7 %collective-permute-start.7 = (bf16[2,512,128]{2,1,0:T(8,128)(2,1)S(1)}, bf16[2,512,128]{2,1,0:T(8,128)(2,1)S(1)}, u32[]{:S(2)}, u32[]{:S(2)}) collective-permute-start(bf16[2,512,128]{2,1,0:T(8,128)(2,1)S(1)} %get-tuple-element.69.refs_8_), channel_id=1, source_target_pairs={{0,2},{2,0},{4,6},{6,4},{8,10},{10,8},{12,14},{14,12},{1,3},{3,1},... | collective-permute-start | bytes 786440 | tf_op jit(solution)/shard_map/ppermute | solution.py:186
  12.1 2.0 %collective-permute-done.refs_1_ = bf16[144,512]{1,0:T(8,128)(2,1)S(1)} collective-permute-done((bf16[144,512]{1,0:T(8,128)(2,1)S(1)}, bf16[144,512]{1,0:T(8,128)(2,1)S(1)}, u32[]{:S(2)}, u32[]{:S(2)}) %collective-permute-start) | collective-permute-done | bytes 147488 | tf_op jit(solution)/shard_map/ppermute | solution.py:190
  14.1 1.3 %collective-permute-start.8 = (bf16[2,512,128]{2,1,0:T(8,128)(2,1)S(1)}, bf16[2,512,128]{2,1,0:T(8,128)(2,1)S(1)}, u32[]{:S(2)}, u32[]{:S(2)}) collective-permute-start(bf16[2,512,128]{2,1,0:T(8,128)(2,1)S(1)} %get-tuple-element.68.refs_9_), channel_id=1, source_target_pairs={{0,2},{2,0},{4,6},{6,4},{8,10},{10,8},{12,14},{14,12},{1,3},{3,1},... | collective-permute-start | bytes 786440 | tf_op jit(solution)/shard_map/ppermute | solution.py:186
  15.4 7.1 %collective-permute-done.1.refs_2_ = bf16[144,512]{1,0:T(8,128)(2,1)S(1)} collective-permute-done((bf16[144,512]{1,0:T(8,128)(2,1)S(1)}, bf16[144,512]{1,0:T(8,128)(2,1)S(1)}, u32[]{:S(2)}, u32[]{:S(2)}) %collective-permute-start.1) | collective-permute-done | bytes 147488 | tf_op jit(solution)/shard_map/ppermute | solution.py:190
  22.4 0.0 collective-permute-done.2.refs_3_
  22.4 0.0 collective-permute-done.3.refs_9_
  22.4 0.0 collective-permute-start.4
  22.5 0.5 collective-permute-start.5
  23.0 0.1 collective-permute-start.6
  23.0 0.3 fusion
  23.4 0.1 pad_add_fusion.place
  23.4 0.4 collective-permute-done.4.refs_5_
  23.8 0.2 collective-permute-done.5.refs_6_
  24.0 0.3 collective-permute-done.6.refs_7_
  24.3 0.0 copy-done.1
  24.3 0.0 copy-done
  24.3 1.0 %products.2 = (f32[128,256]{1,0:T(8,128)S(1)}, bf16[128,256]{1,0:T(8,128)(2,1)S(1)}, bf16[128,256]{1,0:T(8,128)(2,1)S(1)}, bf16[128,256]{1,0:T(8,128)(2,1)S(1)}, s32[4,128]{1,0:T(4,128)S(1)}) custom-call(s32[2]{0:T(128)S(1)} %pad_add_fusion.place, bf16[144,512]{1,0:T(8,128)(2,1)S(1)} %copy-done, bf16[144,512]{1,0:T(8,128)(2,1)S(1)} %collective-permute-done.refs_1_, ...), custom_call_target="tpu_custom_call" | custom-call | flops 3449999872 | tf_op jit(solution)/shard_map/products/pallas_call | solution.py:139
  25.3 0.9 %collective-permute-start.9 = (s32[4,128]{1,0:T(4,128)S(1)}, s32[4,128]{1,0:T(4,128)S(1)}, u32[]{:S(2)}, u32[]{:S(2)}) collective-permute-start(s32[4,128]{1,0:T(4,128)S(1)} %get-tuple-element.44.refs_0_.numbers), channel_id=1, source_target_pairs={{0,2},{2,0},{4,6},{6,4},{8,10},{10,8},{12,14},{14,12},{1,3},{3,1},... | collective-permute-start | bytes 6152 | tf_op jit(solution)/shard_map/ppermute | solution.py:186
  26.2 0.1 pad_maximum_fusion
  26.3 2.4 %collective-permute-start.15 = (bf16[128,256]{1,0:T(8,128)(2,1)S(1)}, bf16[128,256]{1,0:T(8,128)(2,1)S(1)}, u32[]{:S(2)}, u32[]{:S(2)}) collective-permute-start(bf16[128,256]{1,0:T(8,128)(2,1)S(1)} %get-tuple-element.55), channel_id=1, source_target_pairs={{0,4},{2,6},{4,0},{6,2},{8,12},{10,14},{12,8},{14,10},{1,5},{3,7},... | collective-permute-start | bytes 196616 | tf_op jit(solution)/shard_map/ppermute | solution.py:190
  28.7 1.1 %collective-permute-start.16 = (bf16[128,256]{1,0:T(8,128)(2,1)S(1)}, bf16[128,256]{1,0:T(8,128)(2,1)S(1)}, u32[]{:S(2)}, u32[]{:S(2)}) collective-permute-start(bf16[128,256]{1,0:T(8,128)(2,1)S(1)} %get-tuple-element.56), channel_id=1, source_target_pairs={{0,8},{2,10},{4,12},{6,14},{8,0},{10,2},{12,4},{14,6},{1,9},{3,11}... | collective-permute-start | bytes 196616 | tf_op jit(solution)/shard_map/ppermute | solution.py:190
  29.8 0.0 collective-permute-done.9.refs_1_
  29.8 1.4 %collective-permute-start.17 = (bf16[128,256]{1,0:T(8,128)(2,1)S(1)}, bf16[128,256]{1,0:T(8,128)(2,1)S(1)}, u32[]{:S(2)}, u32[]{:S(2)}) collective-permute-start(bf16[128,256]{1,0:T(8,128)(2,1)S(1)} %get-tuple-element.57), channel_id=1, source_target_pairs={{0,12},{2,14},{4,8},{6,10},{8,4},{10,6},{12,0},{14,2},{1,13},{3,15... | collective-permute-start | bytes 196616 | tf_op jit(solution)/shard_map/ppermute | solution.py:190
  31.2 0.0 copy-done.2
  31.2 1.5 %pick_pages.1 = (bf16[2,2,64,128]{3,2,1,0:T(8,128)(2,1)S(1)}, bf16[2,2,64,128]{3,2,1,0:T(8,128)(2,1)S(1)}, bf16[2,2,64,128]{3,2,1,0:T(8,128)(2,1)S(1)}, bf16[2,2...) custom-call(s32[2]{0:T(128)S(1)} %pad_add_fusion.place, s32[4,128]{1,0:T(4,128)S(1)} %get-tuple-element.44.refs_0_.numbers, ...), custom_call_target="tpu_custom_call" | custom-call | flops 11500000256 | tf_op jit(solution)/shard_map/pick_pages/pallas_call | solution.py:357
  32.7 0.0 collective-permute-done.7.refs_10_
  32.7 0.0 collective-permute-done.8.refs_11_
  32.7 1.5 %collective-permute-start.11 = (bf16[2,2,64,128]{3,2,1,0:T(8,128)(2,1)S(1)}, bf16[2,2,64,128]{3,2,1,0:T(8,128)(2,1)S(1)}, u32[]{:S(2)}, u32[]{:S(2)}) collective-permute-start(bf16[2,2,64,128]{3,2,1,0:T(8,128)(2,1)S(1)} %get-tuple-element.50), channel_id=1, source_target_pairs={{0,4},{2,6},{4,0},{6,2},{8,12},{10,14},{12,8},{14,10},{1,5},{3,7},... | collective-permute-start | bytes 196616 | tf_op jit(solution)/shard_map/ppermute | solution.py:190
  34.3 1.5 %collective-permute-start.12 = (bf16[2,2,64,128]{3,2,1,0:T(8,128)(2,1)S(1)}, bf16[2,2,64,128]{3,2,1,0:T(8,128)(2,1)S(1)}, u32[]{:S(2)}, u32[]{:S(2)}) collective-permute-start(bf16[2,2,64,128]{3,2,1,0:T(8,128)(2,1)S(1)} %get-tuple-element.51), channel_id=1, source_target_pairs={{0,8},{2,10},{4,12},{6,14},{8,0},{10,2},{12,4},{14,6},{1,9},{3,11}... | collective-permute-start | bytes 196616 | tf_op jit(solution)/shard_map/ppermute | solution.py:190
  35.8 1.2 %products.3 = (f32[256,512]{1,0:T(8,128)S(1)}, bf16[256,512]{1,0:T(8,128)(2,1)S(1)}) custom-call(s32[2]{0:T(128)S(1)} %pad_add_fusion.place, bf16[144,512]{1,0:T(8,128)(2,1)S(1)} %copy-done, bf16[144,512]{1,0:T(8,128)(2,1)S(1)} %collective-permute-done.refs_1_, bf16[144,512]{1,0:T(8,128)(2,1)S(1)} %collective-permute-done.1.refs_2_, ...), custom_call_target="tpu_custom_call" | custom-call | tf_op jit(solution)/shard_map/products/pallas_call | solution.py:139
  37.0 0.0 collective-permute-done.15.refs_1_
  37.0 1.5 %collective-permute-start.13 = (bf16[2,2,64,128]{3,2,1,0:T(8,128)(2,1)S(1)}, bf16[2,2,64,128]{3,2,1,0:T(8,128)(2,1)S(1)}, u32[]{:S(2)}, u32[]{:S(2)}) collective-permute-start(bf16[2,2,64,128]{3,2,1,0:T(8,128)(2,1)S(1)} %get-tuple-element.52), channel_id=1, source_target_pairs={{0,12},{2,14},{4,8},{6,10},{8,4},{10,6},{12,0},{14,2},{1,13},{3,15... | collective-permute-start | bytes 196616 | tf_op jit(solution)/shard_map/ppermute | solution.py:190
  38.5 0.0 collective-permute-done.16.refs_2_
  38.5 0.6 collective-permute-start.10
  39.1 0.0 collective-permute-done.17.refs_3_
  39.1 1.3 %fresh_pages.1 = (bf16[128,128]{1,0:T(8,128)(2,1)S(1)}, bf16[128,128]{1,0:T(8,128)(2,1)S(1)}, bf16[8,2,64,128]{3,2,1,0:T(8,128)(2,1)}) custom-call(s32[4,128]{1,0:T(4,128)S(1)} %get-tuple-element.44.refs_0_.numbers, f32[128,256]{1,0:T(8,128)S(1)} %get-tuple-element.58.refs_0_, bf16[128,256]{1,0:T(8,128)(2,1)S(1)} %collective-permute-done.15.refs_1_, ...), custom_call_target="tpu_custom_call" | custom-call | flops 34500001792 | tf_op jit(solution)/shard_map/fresh_pages/pallas_call | solution.py:426
  40.4 4.4 %all-to-all-start = ((bf16[8,2,64,128]{3,2,1,0:T(8,128)(2,1)}), bf16[8,2,64,128]{3,2,1,0:T(8,128)(2,1)S(1)}, u32[]{:S(2)}, u32[]{:S(2)}) async-start(bf16[8,2,64,128]{3,2,1,0:T(8,128)(2,1)} %get-tuple-element.66), calls=%async_computation | async-start | bytes 524288 | tf_op jit(solution)/shard_map/all_to_all | solution.py:549
  44.8 0.0 collective-permute-done.11.refs_1_.refs_8_
  44.8 0.0 collective-permute-done.12.refs_2_.refs_9_
  44.8 0.0 collective-permute-done.13.refs_3_.refs_10_
  44.8 2.1 %collective-permute-start.18 = (bf16[4,2,64,128]{3,2,1,0:T(8,128)(2,1)S(1)}, bf16[4,2,64,128]{3,2,1,0:T(8,128)(2,1)S(1)}, u32[]{:S(2)}, u32[]{:S(2)}) collective-permute-start(bf16[4,2,64,128]{3,2,1,0:T(8,128)(2,1)S(1)} %relay.1), channel_id=1, source_target_pairs={{0,2},{2,0},{4,6},{6,4},{8,10},{10,8},{12,14},{14,12},{1,3},{3,1},... | collective-permute-start | bytes 393224 | tf_op jit(solution)/shard_map/ppermute | solution.py:186
  46.9 2.5 %collective-permute-done.10.arrived.refs_1_ = bf16[256,512]{1,0:T(8,128)(2,1)S(1)} collective-permute-done((bf16[256,512]{1,0:T(8,128)(2,1)S(1)}, bf16[256,512]{1,0:T(8,128)(2,1)S(1)}, u32[]{:S(2)}, u32[]{:S(2)}) %collective-permute-start.10) | collective-permute-done | bytes 262176 | tf_op jit(solution)/shard_map/ppermute | solution.py:190
  49.5 0.9 %collective-permute-start.14 = (bf16[128,512]{1,0:T(8,128)(2,1)S(1)}, bf16[128,512]{1,0:T(8,128)(2,1)S(1)}, u32[]{:S(2)}, u32[]{:S(2)}) collective-permute-start(bf16[128,512]{1,0:T(8,128)(2,1)S(1)} %fold.1), channel_id=1, source_target_pairs={{0,8},{2,10},{4,12},{6,14},{8,0},{10,2},{12,4},{14,6},{1,9},{3,11}... | collective-permute-start | bytes 393224 | tf_op jit(solution)/shard_map/ppermute | solution.py:190
  50.4 0.9 %collective-permute-done.18.refs_11_ = bf16[4,2,64,128]{3,2,1,0:T(8,128)(2,1)S(1)} collective-permute-done((bf16[4,2,64,128]{3,2,1,0:T(8,128)(2,1)S(1)}, bf16[4,2,64,128]{3,2,1,0:T(8,128)(2,1)S(1)}, u32[]{:S(2)}, u32[]{:S(2)}) %collective-permute-start.18) | collective-permute-done | bytes 131104 | tf_op jit(solution)/shard_map/ppermute | solution.py:186
  51.2 6.6 %collective-permute-done.14.refs_2_ = bf16[128,512]{1,0:T(8,128)(2,1)S(1)} collective-permute-done((bf16[128,512]{1,0:T(8,128)(2,1)S(1)}, bf16[128,512]{1,0:T(8,128)(2,1)S(1)}, u32[]{:S(2)}, u32[]{:S(2)}) %collective-permute-start.14) | collective-permute-done | bytes 131104 | tf_op jit(solution)/shard_map/ppermute | solution.py:190
  57.9 2.0 %attend.1 = bf16[128,512]{1,0:T(8,128)(2,1)} custom-call(s32[2]{0:T(128)S(1)} %pad_add_fusion.place, s32[4,128]{1,0:T(4,128)S(1)} %get-tuple-element.44.refs_0_.numbers, f32[256,512]{1,0:T(8,128)S(1)} %get-tuple-element.48.kept.refs_0_, bf16[256,512]{1,0:T(8,128)(2,1)S(1)} %collective-permute-done.10.arrived.refs_1_, ...), custom_call_target="tpu_custom_call" | custom-call | flops 3449999872 | tf_op jit(solution)/shard_map/attend/pallas_call | solution.py:515
  59.9 0.0 all-to-all-done.refs_2_
  59.9 1.3 %land_pages.1 = bf16[16,2,64,128]{3,2,1,0:T(8,128)(2,1)} custom-call(s32[2]{0:T(128)S(1)} %pad_add_fusion.place, s32[4,128]{1,0:T(4,128)S(1)} %get-tuple-element.44.refs_0_.numbers, s32[4,128]{1,0:T(4,128)S(1)} %collective-permute-done.9.refs_1_, bf16[8,2,64,128]{3,2,1,0:T(8,128)(2,1)S(1)} %all-to-all-done.refs_2_, ...), custom_call_target="tpu_custom_call", output_to_operand_aliasing={{}: (4, {})} | custom-call | flops 3449999872 | tf_op jit(solution)/shard_map/land_pages/pallas_call | solution.py:387
  (5 shorter events, 0.1 us)
Async XLA Ops:
  1.3 2.6 %copy-start.3 = (bf16[512,1,6,128]{3,0,2,1:T(8,128)(2,1)S(1)}, bf16[512,1,6,128]{3,0,2,1:T(8,128)(2,1)}, u32[]{:S(2)}) copy-start(bf16[512,1,6,128]{3,0,2,1:T(8,128)(2,1)} %param.17) | copy-start | bytes 2359300
  3.9 3.1 %copy-start.6 = (bf16[144,512]{1,0:T(8,128)(2,1)S(1)}, bf16[144,512]{1,0:T(8,128)(2,1)}, u32[]{:S(2)}) copy-start(bf16[144,512]{1,0:T(8,128)(2,1)} %get-tuple-element.36) | copy-start | bytes 442372
  3.9 4.7 %copy-start.5 = (bf16[144,512]{1,0:T(8,128)(2,1)S(1)}, bf16[144,512]{1,0:T(8,128)(2,1)}, u32[]{:S(2)}) copy-start(bf16[144,512]{1,0:T(8,128)(2,1)} %get-tuple-element.37) | copy-start | bytes 442372
  3.9 7.3 %copy-start.4 = (bf16[144,512]{1,0:T(8,128)(2,1)S(1)}, bf16[144,512]{1,0:T(8,128)(2,1)}, u32[]{:S(2)}) copy-start(bf16[144,512]{1,0:T(8,128)(2,1)} %get-tuple-element.38) | copy-start | bytes 442372
  3.9 20.4 %copy-start.1 = (bf16[144,512]{1,0:T(8,128)(2,1)S(1)}, bf16[144,512]{1,0:T(8,128)(2,1)}, u32[]{:S(2)}) copy-start(bf16[144,512]{1,0:T(8,128)(2,1)} %get-tuple-element.43.refs_4_) | copy-start | bytes 442372
  4.0 20.4 %copy-start = (bf16[144,512]{1,0:T(8,128)(2,1)S(1)}, bf16[144,512]{1,0:T(8,128)(2,1)}, u32[]{:S(2)}) copy-start(bf16[144,512]{1,0:T(8,128)(2,1)} %get-tuple-element.35.refs_0_) | copy-start | bytes 442372
  4.0 18.5 %collective-permute-start.3 = (bf16[2,512,128]{2,1,0:T(8,128)(2,1)S(1)}, bf16[2,512,128]{2,1,0:T(8,128)(2,1)S(1)}, u32[]{:S(2)}, u32[]{:S(2)}) collective-permute-start(bf16[2,512,128]{2,1,0:T(8,128)(2,1)S(1)} %get-tuple-element.70.refs_8_), channel_id=1, source_target_pairs={{0,2},{2,0},{4,6},{6,4},{8,10},{10,8},{12,14},{14,12},{1,3},{3,1},... | collective-permute-start | bytes 786440 | tf_op jit(solution)/shard_map/ppermute | solution.py:186
  7.0 7.1 %collective-permute-start = (bf16[144,512]{1,0:T(8,128)(2,1)S(1)}, bf16[144,512]{1,0:T(8,128)(2,1)S(1)}, u32[]{:S(2)}, u32[]{:S(2)}) collective-permute-start(bf16[144,512]{1,0:T(8,128)(2,1)S(1)} %copy-done.6), channel_id=1, source_target_pairs={{0,4},{2,6},{4,0},{6,2},{8,12},{10,14},{12,8},{14,10},{1,5},{3,7},... | collective-permute-start | bytes 442376 | tf_op jit(solution)/shard_map/ppermute | solution.py:190
  8.6 13.9 %collective-permute-start.1 = (bf16[144,512]{1,0:T(8,128)(2,1)S(1)}, bf16[144,512]{1,0:T(8,128)(2,1)S(1)}, u32[]{:S(2)}, u32[]{:S(2)}) collective-permute-start(bf16[144,512]{1,0:T(8,128)(2,1)S(1)} %copy-done.5), channel_id=1, source_target_pairs={{0,8},{2,10},{4,12},{6,14},{8,0},{10,2},{12,4},{14,6},{1,9},{3,11}... | collective-permute-start | bytes 442376 | tf_op jit(solution)/shard_map/ppermute | solution.py:190
  11.2 11.3 %collective-permute-start.2 = (bf16[144,512]{1,0:T(8,128)(2,1)S(1)}, bf16[144,512]{1,0:T(8,128)(2,1)S(1)}, u32[]{:S(2)}, u32[]{:S(2)}) collective-permute-start(bf16[144,512]{1,0:T(8,128)(2,1)S(1)} %copy-done.4), channel_id=1, source_target_pairs={{0,12},{2,14},{4,8},{6,10},{8,4},{10,6},{12,0},{14,2},{1,13},{3,15... | collective-permute-start | bytes 442376 | tf_op jit(solution)/shard_map/ppermute | solution.py:190
  11.4 21.3 %collective-permute-start.7 = (bf16[2,512,128]{2,1,0:T(8,128)(2,1)S(1)}, bf16[2,512,128]{2,1,0:T(8,128)(2,1)S(1)}, u32[]{:S(2)}, u32[]{:S(2)}) collective-permute-start(bf16[2,512,128]{2,1,0:T(8,128)(2,1)S(1)} %get-tuple-element.69.refs_8_), channel_id=1, source_target_pairs={{0,2},{2,0},{4,6},{6,4},{8,10},{10,8},{12,14},{14,12},{1,3},{3,1},... | collective-permute-start | bytes 786440 | tf_op jit(solution)/shard_map/ppermute | solution.py:186
  14.1 18.6 %collective-permute-start.8 = (bf16[2,512,128]{2,1,0:T(8,128)(2,1)S(1)}, bf16[2,512,128]{2,1,0:T(8,128)(2,1)S(1)}, u32[]{:S(2)}, u32[]{:S(2)}) collective-permute-start(bf16[2,512,128]{2,1,0:T(8,128)(2,1)S(1)} %get-tuple-element.68.refs_9_), channel_id=1, source_target_pairs={{0,2},{2,0},{4,6},{6,4},{8,10},{10,8},{12,14},{14,12},{1,3},{3,1},... | collective-permute-start | bytes 786440 | tf_op jit(solution)/shard_map/ppermute | solution.py:186
  22.4 1.4 %collective-permute-start.4 = (bf16[144,512]{1,0:T(8,128)(2,1)S(1)}, bf16[144,512]{1,0:T(8,128)(2,1)S(1)}, u32[]{:S(2)}, u32[]{:S(2)}) collective-permute-start(bf16[144,512]{1,0:T(8,128)(2,1)S(1)} %collective-permute-done.refs_1_), channel_id=1, source_target_pairs={{0,1},{1,0},{2,3},{3,2},{4,5},{5,4},{6,7},{7,6},{8,9},{9,8},{10,11... | collective-permute-start | bytes 442376 | tf_op jit(solution)/shard_map/ppermute | solution.py:207
  22.5 1.6 %collective-permute-start.5 = (bf16[144,512]{1,0:T(8,128)(2,1)S(1)}, bf16[144,512]{1,0:T(8,128)(2,1)S(1)}, u32[]{:S(2)}, u32[]{:S(2)}) collective-permute-start(bf16[144,512]{1,0:T(8,128)(2,1)S(1)} %collective-permute-done.1.refs_2_), channel_id=1, source_target_pairs={{0,1},{1,0},{2,3},{3,2},{4,5},{5,4},{6,7},{7,6},{8,9},{9,8},{10,11... | collective-permute-start | bytes 442376 | tf_op jit(solution)/shard_map/ppermute | solution.py:207
  23.0 1.4 %collective-permute-start.6 = (bf16[144,512]{1,0:T(8,128)(2,1)S(1)}, bf16[144,512]{1,0:T(8,128)(2,1)S(1)}, u32[]{:S(2)}, u32[]{:S(2)}) collective-permute-start(bf16[144,512]{1,0:T(8,128)(2,1)S(1)} %collective-permute-done.2.refs_3_), channel_id=1, source_target_pairs={{0,1},{1,0},{2,3},{3,2},{4,5},{5,4},{6,7},{7,6},{8,9},{9,8},{10,11... | collective-permute-start | bytes 442376 | tf_op jit(solution)/shard_map/ppermute | solution.py:207
  24.3 6.9 %copy-start.2 = (bf16[16,2,64,128]{3,2,1,0:T(8,128)(2,1)S(1)}, bf16[16,2,64,128]{3,2,1,0:T(8,128)(2,1)}, u32[]{:S(2)}) copy-start(bf16[16,2,64,128]{3,2,1,0:T(8,128)(2,1)} %refs_2_.1) | copy-start | bytes 1572868
  25.3 4.5 %collective-permute-start.9 = (s32[4,128]{1,0:T(4,128)S(1)}, s32[4,128]{1,0:T(4,128)S(1)}, u32[]{:S(2)}, u32[]{:S(2)}) collective-permute-start(s32[4,128]{1,0:T(4,128)S(1)} %get-tuple-element.44.refs_0_.numbers), channel_id=1, source_target_pairs={{0,2},{2,0},{4,6},{6,4},{8,10},{10,8},{12,14},{14,12},{1,3},{3,1},... | collective-permute-start | bytes 6152 | tf_op jit(solution)/shard_map/ppermute | solution.py:186
  26.3 10.7 %collective-permute-start.15 = (bf16[128,256]{1,0:T(8,128)(2,1)S(1)}, bf16[128,256]{1,0:T(8,128)(2,1)S(1)}, u32[]{:S(2)}, u32[]{:S(2)}) collective-permute-start(bf16[128,256]{1,0:T(8,128)(2,1)S(1)} %get-tuple-element.55), channel_id=1, source_target_pairs={{0,4},{2,6},{4,0},{6,2},{8,12},{10,14},{12,8},{14,10},{1,5},{3,7},... | collective-permute-start | bytes 196616 | tf_op jit(solution)/shard_map/ppermute | solution.py:190
  28.7 9.8 %collective-permute-start.16 = (bf16[128,256]{1,0:T(8,128)(2,1)S(1)}, bf16[128,256]{1,0:T(8,128)(2,1)S(1)}, u32[]{:S(2)}, u32[]{:S(2)}) collective-permute-start(bf16[128,256]{1,0:T(8,128)(2,1)S(1)} %get-tuple-element.56), channel_id=1, source_target_pairs={{0,8},{2,10},{4,12},{6,14},{8,0},{10,2},{12,4},{14,6},{1,9},{3,11}... | collective-permute-start | bytes 196616 | tf_op jit(solution)/shard_map/ppermute | solution.py:190
  29.8 9.3 %collective-permute-start.17 = (bf16[128,256]{1,0:T(8,128)(2,1)S(1)}, bf16[128,256]{1,0:T(8,128)(2,1)S(1)}, u32[]{:S(2)}, u32[]{:S(2)}) collective-permute-start(bf16[128,256]{1,0:T(8,128)(2,1)S(1)} %get-tuple-element.57), channel_id=1, source_target_pairs={{0,12},{2,14},{4,8},{6,10},{8,4},{10,6},{12,0},{14,2},{1,13},{3,15... | collective-permute-start | bytes 196616 | tf_op jit(solution)/shard_map/ppermute | solution.py:190
  32.7 12.1 %collective-permute-start.11 = (bf16[2,2,64,128]{3,2,1,0:T(8,128)(2,1)S(1)}, bf16[2,2,64,128]{3,2,1,0:T(8,128)(2,1)S(1)}, u32[]{:S(2)}, u32[]{:S(2)}) collective-permute-start(bf16[2,2,64,128]{3,2,1,0:T(8,128)(2,1)S(1)} %get-tuple-element.50), channel_id=1, source_target_pairs={{0,4},{2,6},{4,0},{6,2},{8,12},{10,14},{12,8},{14,10},{1,5},{3,7},... | collective-permute-start | bytes 196616 | tf_op jit(solution)/shard_map/ppermute | solution.py:190
  34.3 10.5 %collective-permute-start.12 = (bf16[2,2,64,128]{3,2,1,0:T(8,128)(2,1)S(1)}, bf16[2,2,64,128]{3,2,1,0:T(8,128)(2,1)S(1)}, u32[]{:S(2)}, u32[]{:S(2)}) collective-permute-start(bf16[2,2,64,128]{3,2,1,0:T(8,128)(2,1)S(1)} %get-tuple-element.51), channel_id=1, source_target_pairs={{0,8},{2,10},{4,12},{6,14},{8,0},{10,2},{12,4},{14,6},{1,9},{3,11}... | collective-permute-start | bytes 196616 | tf_op jit(solution)/shard_map/ppermute | solution.py:190
  37.0 7.8 %collective-permute-start.13 = (bf16[2,2,64,128]{3,2,1,0:T(8,128)(2,1)S(1)}, bf16[2,2,64,128]{3,2,1,0:T(8,128)(2,1)S(1)}, u32[]{:S(2)}, u32[]{:S(2)}) collective-permute-start(bf16[2,2,64,128]{3,2,1,0:T(8,128)(2,1)S(1)} %get-tuple-element.52), channel_id=1, source_target_pairs={{0,12},{2,14},{4,8},{6,10},{8,4},{10,6},{12,0},{14,2},{1,13},{3,15... | collective-permute-start | bytes 196616 | tf_op jit(solution)/shard_map/ppermute | solution.py:190
  38.5 10.9 %collective-permute-start.10 = (bf16[256,512]{1,0:T(8,128)(2,1)S(1)}, bf16[256,512]{1,0:T(8,128)(2,1)S(1)}, u32[]{:S(2)}, u32[]{:S(2)}) collective-permute-start(bf16[256,512]{1,0:T(8,128)(2,1)S(1)} %get-tuple-element.49), channel_id=1, source_target_pairs={{0,4},{2,6},{4,0},{6,2},{8,12},{10,14},{12,8},{14,10},{1,5},{3,7},... | collective-permute-start | bytes 786440 | tf_op jit(solution)/shard_map/ppermute | solution.py:190
  40.4 19.5 %all-to-all-start = ((bf16[8,2,64,128]{3,2,1,0:T(8,128)(2,1)}), bf16[8,2,64,128]{3,2,1,0:T(8,128)(2,1)S(1)}, u32[]{:S(2)}, u32[]{:S(2)}) async-start(bf16[8,2,64,128]{3,2,1,0:T(8,128)(2,1)} %get-tuple-element.66), calls=%async_computation | async-start | bytes 524288 | tf_op jit(solution)/shard_map/all_to_all | solution.py:549
  44.8 6.4 %collective-permute-start.18 = (bf16[4,2,64,128]{3,2,1,0:T(8,128)(2,1)S(1)}, bf16[4,2,64,128]{3,2,1,0:T(8,128)(2,1)S(1)}, u32[]{:S(2)}, u32[]{:S(2)}) collective-permute-start(bf16[4,2,64,128]{3,2,1,0:T(8,128)(2,1)S(1)} %relay.1), channel_id=1, source_target_pairs={{0,2},{2,0},{4,6},{6,4},{8,10},{10,8},{12,14},{14,12},{1,3},{3,1},... | collective-permute-start | bytes 393224 | tf_op jit(solution)/shard_map/ppermute | solution.py:186
  49.5 8.4 %collective-permute-start.14 = (bf16[128,512]{1,0:T(8,128)(2,1)S(1)}, bf16[128,512]{1,0:T(8,128)(2,1)S(1)}, u32[]{:S(2)}, u32[]{:S(2)}) collective-permute-start(bf16[128,512]{1,0:T(8,128)(2,1)S(1)} %fold.1), channel_id=1, source_target_pairs={{0,8},{2,10},{4,12},{6,14},{8,0},{10,2},{12,4},{14,6},{1,9},{3,11}... | collective-permute-start | bytes 393224 | tf_op jit(solution)/shard_map/ppermute | solution.py:190

commit v7 on v6

--- a/solution.py
+++ b/solution.py
@@ -8,7 +8,7 @@
 from jax.experimental.pallas import tpu as pltpu
 from jax.sharding import PartitionSpec as P
 
-CFG = {'E': 'rec', 'P': [], 'Q': ['pick'], 'R': ['q'], 'G': ['pages'], 'X': ['fresh'], 'L': 0, 'W': 1, 'N': 0, 'V': 1, 'cost': {'prepare': 3, 'kv': 3, 'q': 0, 'fold': 0, 'pick': 10, 'fresh': 30, 'attend': 3, 'land': 3, 'relay': 10}}
+WAITS = {'prepare': 30, 'kv': 0, 'q': 1, 'settle': 10, 'relay': 0, 'pick': 10, 'fresh': 30, 'attend': 3, 'land': 0}
 ANY = pl.BlockSpec(memory_space=pl.ANY)
 SCALARS = pl.BlockSpec(memory_space=pltpu.SMEM)
 VECTORS = pl.BlockSpec(memory_space=pltpu.VMEM)
@@ -16,7 +16,7 @@
 
 
 def wait(name):
-    return pl.CostEstimate(flops=int(CFG['cost'].get(name, 0) * 1.15e9), bytes_accessed=0, transcendentals=0)
+    return pl.CostEstimate(flops=int(WAITS[name] * 1.15e9), bytes_accessed=0, transcendentals=0)
 
 
 def tie(value, *others):
@@ -98,53 +98,106 @@
     )
 
 
-def product_kernel(place, *refs):
-    weights = [ref for ref in refs[8:] if len(ref.shape) == 3]
+def multiply(place, tokens, weights, rows):
+    direct = jnp.concatenate([ref[:rows] for ref in tokens[:4]], axis=0)
+    passed = jnp.concatenate([ref[:rows] for ref in tokens[4:]], axis=0)
     own, other = weights[: len(weights) // 2], weights[len(weights) // 2 :]
-    kept, *leaving = refs[8 + len(weights) :]
-    if len(leaving) == 4:
-        table = leaving.pop()
-        for index, ref in enumerate(refs[:4]):
-            head = ref[kept.shape[0] : kept.shape[0] + 8, : table.shape[1]]
-            table[index : index + 1] = head.astype(jnp.float32)[:1].astype(jnp.int32)
-    rows = leaving[-1].shape[0] // (1 if len(leaving) == 3 else 2)
-    direct = jnp.concatenate([ref[:rows] for ref in refs[:4]], axis=0)
-    passed = jnp.concatenate([ref[:rows] for ref in refs[4:8]], axis=0)
     own_first = (place[0] % 2) == place[1]
     for_own = jnp.where(own_first, direct, passed)
     for_other = jnp.where(own_first, passed, direct)
     result = jnp.dot(
         for_own, side_by_side(*own), preferred_element_type=jnp.float32
     ) + jnp.dot(for_other, side_by_side(*other), preferred_element_type=jnp.float32)
-    result = [result[index * rows : (index + 1) * rows] for index in range(4)]
-    kept[:rows] = result[0]
-    if len(leaving) == 3:
-        for out, part in zip(leaving, result[1:]):
-            out[...] = part.astype(out.dtype)
-    else:
-        kept[rows:] = result[2]
-        leaving[0][:rows] = result[1].astype(leaving[0].dtype)
-        leaving[0][rows:] = result[3].astype(leaving[0].dtype)
-
-
-def products(place, direct, passed, own, other, paired):
-    rows = direct[0].shape[0] - 16
-    depth = 2 * own[0].shape[1]
+    return [result[index * rows : (index + 1) * rows] for index in range(4)]
+
+
+def kv_kernel(place, *refs):
+    tokens, weights, (kept, *leaving), table = refs[:8], refs[8:10], refs[10:14], refs[14]
+    for index, ref in enumerate(tokens[:4]):
+        head = ref[kept.shape[0] : kept.shape[0] + 8, : table.shape[1]]
+        table[index : index + 1] = head.astype(jnp.float32)[:1].astype(jnp.int32)
+    parts = multiply(place, tokens, weights, kept.shape[0])
+    for out, part in zip((kept, *leaving), parts):
+        out[...] = part.astype(out.dtype)
+
+
+def kv_products(place, tokens, own, other):
+    rows = tokens[0].shape[0] - 16
+    columns = own.shape[0] * own.shape[2]
+    return pl.pallas_call(
+        kv_kernel,
+        out_shape=[jax.ShapeDtypeStruct((rows, columns), jnp.float32)]
+        + [jax.ShapeDtypeStruct((rows, columns), jnp.bfloat16)] * 3
+        + [jax.ShapeDtypeStruct((4, 128), jnp.int32)],
+        in_specs=[SCALARS] + [VECTORS] * 10,
+        out_specs=[VECTORS] * 5,
+        compiler_params=PARAMS,
+        cost_estimate=wait("kv"),
+        name="kv_products",
+    )(place, *tokens, own, other)
+
+
+def q_kernel(place, *refs):
+    tokens, weights, kept, leaving = refs[:8], refs[8:-2], refs[-2], refs[-1]
+    rows = kept.shape[0] // 2
+    parts = multiply(place, tokens, weights, rows)
+    kept[:rows], kept[rows:] = parts[0], parts[2]
+    leaving[:rows] = parts[1].astype(leaving.dtype)
+    leaving[rows:] = parts[3].astype(leaving.dtype)
+
+
+def q_products(place, tokens, own, other):
+    rows = tokens[0].shape[0] - 16
     columns = sum(part.shape[0] * part.shape[2] for part in own)
-    if paired:
-        shapes = [((2 * rows, columns), jnp.float32), ((2 * rows, columns), jnp.bfloat16)]
-    else:
-        shapes = [((rows, columns), jnp.float32)] + [((rows, columns), jnp.bfloat16)] * 3
-        shapes.append(((4, 128), jnp.int32))
-    return pl.pallas_call(
-        product_kernel,
-        out_shape=[jax.ShapeDtypeStruct(shape, kind) for shape, kind in shapes],
+    return pl.pallas_call(
+        q_kernel,
+        out_shape=[
+            jax.ShapeDtypeStruct((2 * rows, columns), kind) for kind in (jnp.float32, jnp.bfloat16)
+        ],
         in_specs=[SCALARS] + [VECTORS] * (8 + 2 * len(own)),
-        out_specs=[VECTORS] * len(shapes),
-        compiler_params=PARAMS,
-        cost_estimate=wait("q" if paired else "kv"),
-        name="products",
-    )(place, *direct, *passed, *own, *other)
+        out_specs=[VECTORS] * 2,
+        compiler_params=PARAMS,
+        cost_estimate=wait("q"),
+        name="q_products",
+    )(place, *tokens, *own, *other)
+
+
+def choose_kernel(prefix, place, *refs):
+    tables, pool, outs, copied, semaphore = refs[:2], refs[2], refs[3:7], refs[7], refs[8]
+    page_rows = pool.shape[2]
+    whole = pltpu.make_async_copy(pool, copied, semaphore.at[16])
+    whole.start()
+
+    def visit(act, table, row, index):
+        slot = slot_for(table, row, place[0], 1, prefix)
+
+        @pl.when(slot >= 0)
+        def _():
+            for half in range(2):
+                target = outs[row].at[pl.ds((2 * (index // 4) + half) * page_rows, page_rows)]
+                act(
+                    pltpu.make_async_copy(
+                        pool.at[slot, half], target, semaphore.at[2 * index + half]
+                    )
+                )
+
+    each_row(tables, functools.partial(visit, lambda copy: copy.start()))
+    each_row(tables, functools.partial(visit, lambda copy: copy.wait()))
+    whole.wait()
+
+
+def choose_pages(place, tables, pool, prefix):
+    pages = jax.ShapeDtypeStruct((4 * pool.shape[2], pool.shape[3]), pool.dtype)
+    return pl.pallas_call(
+        functools.partial(choose_kernel, prefix),
+        out_shape=[pages] * 4 + [jax.ShapeDtypeStruct(pool.shape, pool.dtype)],
+        in_specs=[SCALARS] * 3 + [ANY],
+        out_specs=[VECTORS] * 4 + [ANY],
+        scratch_shapes=[pltpu.SemaphoreType.DMA((17,))],
+        compiler_params=PARAMS,
+        cost_estimate=wait("pick"),
+        name="choose_pages",
+    )(place, *tables, pool)
 
 
 def fold_kernel(kept, arrived, far):
@@ -160,20 +213,21 @@
         in_specs=[VECTORS] * 2,
         out_specs=VECTORS,
         compiler_params=PARAMS,
-        cost_estimate=wait("fold"),
+        cost_estimate=wait("settle"),
         name="fold",
     )(kept, arrived)
 
 
 def relay_kernel(*refs):
+    rows = refs[4].shape[0] // 4
     for index, page in enumerate(refs[:4]):
-        refs[4][index] = page[1]
+        refs[4][index * rows : (index + 1) * rows] = page[rows:]
 
 
 def relay(pages):
     return pl.pallas_call(
         relay_kernel,
-        out_shape=jax.ShapeDtypeStruct((4,) + pages[0].shape[1:], pages[0].dtype),
+        out_shape=jax.ShapeDtypeStruct((2 * pages[0].shape[0], pages[0].shape[1]), pages[0].dtype),
         in_specs=[VECTORS] * 4,
         out_specs=VECTORS,
         compiler_params=PARAMS,
@@ -191,63 +245,33 @@
 
 
 def column_plan(tokens, gain, wqkv, pages_count, requests, pool, place, ranks):
-    me = place[0]
     prefix = requests[0].shape[1]
-    weight = wqkv[:, 0].transpose(1, 0, 2)
     own_direct, own_passed, *pieces = prepare(tokens, gain, pages_count, requests, wqkv.shape[0])
-    if CFG["V"]:
-        weight = tie(weight, pieces[0])
+    weight = tie(wqkv[:, 0].transpose(1, 0, 2), pieces[0])
     *q_weight, kv_weight = [weight[first : first + 2] for first in range(0, weight.shape[0], 2)]
     kv_other, *q_other = [near(part, ranks) for part in [kv_weight] + q_weight]
     direct = [None] * 3
     for step in (2, 3, 1):
         direct[step - 1] = along(pieces[step - 1], ranks, step)
-    if CFG["W"]:
-        direct = tie(direct, kv_other)
     passed = [lax.ppermute(piece, "tp", crossed(2, 1)) for piece in direct]
-    direct = [own_direct] + direct
-    passed = [own_passed] + passed
-
-    kv_own, *leaving, table = products(place, direct, passed, [kv_weight], [kv_other], False)
+    sources = [own_direct, *direct, own_passed, *passed]
+
+    kv_own, *leaving, table = kv_products(place, sources, kv_weight, kv_other)
     kv_parts = [kv_own] + [along(part, ranks, step) for step, part in zip((1, 2, 3), leaving)]
-    state = dict(kv=kv_own, kvp=kv_parts, kvd=kv_parts[1])
-    get = lambda name: [state[k] for k in CFG[name]]
-
-    def pick():
-        t = [table, near(tie(table, *get("P")), ranks)]
-        *picked, state["copied"] = pick_pages(place, t, pool, prefix)
-        state["table"] = t
-        state["pick"] = picked[0]
-        state["pages"] = picked[:1] + [along(picked[step], ranks, step) for step in (1, 2, 3)]
-
-    def q():
-        w = tie(q_other, *get("Q"))
-        state["q"], *leaving = products(place, direct, passed, q_weight, w, CFG["E"] == "rec")
-        if CFG["E"] == "rec":
-            state["qa"] = along(leaving[0], ranks, 1)
-        else:
-            state["qp"] = [state["q"]] + [along(p, ranks, i) for i, p in zip((1, 2, 3), leaving)]
-            state["qa"] = state["qp"][1]
-
-    if "pick" in CFG["Q"]:
-        pick()
-        q()
-    else:
-        q()
-        pick()
-    kv_parts = tie(kv_parts, *get("R"))
+    tables = [table, near(table, ranks)]
+    q_kept, leaving = q_products(place, sources, q_weight, tie(q_other, kv_own))
+    arrived = along(leaving, ranks, 1)
+    *chosen, copied = choose_pages(place, tie(tables, q_kept), pool, prefix)
+    pages = chosen[:1] + [along(chosen[step], ranks, step) for step in (1, 2, 3)]
+    kv_parts = tie(kv_parts, q_kept)
 
     def finish(fresh):
-        state["fresh"] = fresh
-        state["relay"] = tie(relay(state["pages"]), *get("X"))
-        relayed = near(state["relay"], ranks)
-        if CFG["E"] != "rec":
-            return state["qp"], state["pages"] + [relayed], state["qa"]
-        far = fold(state["q"], tie(state["qa"], *get("G")))
-        state["far"] = far
-        return [state["q"], state["qa"], along(far, ranks, 2)], state["pages"] + [relayed], far
-
-    return kv_parts, finish, state["table"], state["copied"], table
+        far = fold(q_kept, tie(arrived, fresh))
+        passed_on = relay(pages)
+        terms = [q_kept, arrived, along(far, ranks, 2)]
+        return terms, pages + [near(passed_on, ranks)], copied
+
+    return kv_parts, finish, tables, table
 
 
 def general_plan(tokens, gain, wqkv, pages_count, requests, pool, place, ranks):
@@ -299,13 +323,13 @@
             tiled=True,
         )
     ]
-    chosen, copied = pick_pages(place, table, pool, prefix)
+    chosen, copied = pick_pages(place, table[0], pool, prefix)
     replies = lax.all_to_all(chosen, "dp", split_axis=0, concat_axis=0, tiled=True)
 
     def finish(fresh):
-        return [total[:, :q_columns]], [replies], fresh
-
-    return [total[:, q_columns:]], finish, table, copied, numbers
+        return [total[:, :q_columns]], [replies], copied
+
+    return [total[:, q_columns:]], finish, table, numbers
 
 
 def each_row(tables, visit):
@@ -331,10 +355,8 @@
     return slot
 
 
-def pick_kernel(count, prefix, place, *refs):
-    tables, pool, copied, semaphore = refs[:count], refs[count], refs[-2], refs[-1]
-    outs = refs[count + 1 : -2]
-    whole = pltpu.make_async_copy(pool, copied, semaphore.at[semaphore.shape[0] - 1])
+def pick_kernel(prefix, place, table, pool, chosen, copied, semaphore):
+    whole = pltpu.make_async_copy(pool, copied, semaphore.at[table.shape[0]])
     whole.start()
 
     def visit(act, table, row, index):
@@ -342,29 +364,28 @@
 
         @pl.when(slot >= 0)
         def _():
-            target = outs[0].at[row] if count == 1 else outs[row].at[index // 4]
-            act(pltpu.make_async_copy(pool.at[slot], target, semaphore.at[index]))
-
-    each_row(tables, functools.partial(visit, lambda copy: copy.start()))
-    each_row(tables, functools.partial(visit, lambda copy: copy.wait()))
+            act(pltpu.make_async_copy(pool.at[slot], chosen.at[row], semaphore.at[index]))
+
+    each_row([table], functools.partial(visit, lambda copy: copy.start()))
+    each_row([table], functools.partial(visit, lambda copy: copy.wait()))
     whole.wait()
 
 
-def pick_pages(place, tables, pool, prefix):
-    page = pool.shape[1:]
-    rows = sum(table.shape[0] for table in tables)
-    heights = [rows] if len(tables) == 1 else [len(tables)] * 4
-    return pl.pallas_call(
-        functools.partial(pick_kernel, len(tables), prefix),
-        out_shape=[jax.ShapeDtypeStruct((height,) + page, pool.dtype) for height in heights]
-        + [jax.ShapeDtypeStruct(pool.shape, pool.dtype)],
-        in_specs=[SCALARS] * (1 + len(tables)) + [ANY],
-        out_specs=[ANY] * (len(heights) + 1),
+def pick_pages(place, table, pool, prefix):
+    rows = table.shape[0]
+    return pl.pallas_call(
+        functools.partial(pick_kernel, prefix),
+        out_shape=[
+            jax.ShapeDtypeStruct((rows,) + pool.shape[1:], pool.dtype),
+            jax.ShapeDtypeStruct(pool.shape, pool.dtype),
+        ],
+        in_specs=[SCALARS] * 2 + [ANY],
+        out_specs=[ANY] * 2,
         scratch_shapes=[pltpu.SemaphoreType.DMA((rows + 1,))],
         compiler_params=PARAMS,
         cost_estimate=wait("pick"),
         name="pick_pages",
-    )(place, *tables, pool)
+    )(place, table, pool)
 
 
 def land_kernel(count, first, new_pages, place, *refs):
@@ -399,28 +420,20 @@
 
 def fresh_kernel(pieces, first, numbers, *refs):
     parts = refs[:pieces]
-    cosine, sine, keys, values, outgoing, pages, semaphore = refs[pieces:]
+    cosine, sine, keys, values, outgoing = refs[pieces:]
     token_rows, head_size = keys.shape
     total = sum(part[:token_rows].astype(jnp.float32) for part in parts)
     keys[...] = turn(total[:, :head_size], cosine[...], sine[...]).astype(keys.dtype)
     values[...] = total[:, head_size:].astype(values.dtype)
-    count, _, page_rows, _ = pages.shape
-    copies = []
-    for page in range(count):
+    page_rows = outgoing.shape[2]
+    for page in range(keys.shape[0] // page_rows):
         span = pl.ds(page * page_rows, page_rows)
-        pages[page, 0] = keys[span, :]
-        pages[page, 1] = values[span, :]
-        copies.append(
-            pltpu.make_async_copy(
-                pages.at[page], outgoing.at[numbers[0, first + page]], semaphore.at[page]
-            )
-        )
-        copies[-1].start()
-    for copy in copies:
-        copy.wait()
-
-
-def fresh_pages(numbers, first, count, parts, cosine, sine, ranks, page_rows):
+        home = numbers[0, first + page]
+        outgoing[home, 0] = keys[span, :]
+        outgoing[home, 1] = values[span, :]
+
+
+def fresh_pages(numbers, first, parts, cosine, sine, ranks, page_rows):
     token_rows, head_size = cosine.shape
     shape = jax.ShapeDtypeStruct((token_rows, head_size), jnp.bfloat16)
     return pl.pallas_call(
@@ -431,11 +444,7 @@
             jax.ShapeDtypeStruct((ranks, 2, page_rows, head_size), jnp.bfloat16),
         ],
         in_specs=[SCALARS] + [VECTORS] * (len(parts) + 2),
-        out_specs=[VECTORS, VECTORS, ANY],
-        scratch_shapes=[
-            pltpu.VMEM((count, 2, page_rows, head_size), jnp.bfloat16),
-            pltpu.SemaphoreType.DMA((count,)),
-        ],
+        out_specs=[VECTORS] * 3,
         compiler_params=PARAMS,
         cost_estimate=wait("fresh"),
         name="fresh_pages",
@@ -446,7 +455,7 @@
     parts, (cosine, sine, keys_new, values_new) = refs[:terms], refs[terms : terms + 4]
     *pages, out, keys, values = refs[terms + 4 :]
     token_rows, head_size = keys_new.shape
-    page_rows = pages[0].shape[2]
+    page_rows = (keys.shape[0] - token_rows) // prefix
     group = out.shape[1] // head_size
     count = numbers[0, 0]
     scale = 1.0 / math.sqrt(head_size)
@@ -455,6 +464,11 @@
         span = pl.ds(page * page_rows, page_rows)
         keys[span, :] = key
         values[span, :] = jnp.where(page < count, value, jnp.zeros_like(value))
+
+    def take(page, source, first):
+        columns = slice(source.shape[1] - head_size, source.shape[1])
+        middle = first + page_rows
+        store(page, source[first:middle, columns], source[middle : middle + page_rows, columns])
 
     for page in range(prefix):
         owner = numbers[0, 1 + page]
@@ -463,14 +477,13 @@
             store(page, pages[0][source, 0], pages[0][source, 1])
         else:
             distance = place[0] ^ owner
-            store(page, pages[0][0, 0], pages[0][0, 1])
-            for index in range(2 * (len(pages) - 1)):
+            take(page, pages[0], 0)
+            for index in range(1, 2 * (len(pages) - 1)):
                 source = (-1, index // 2) if index % 2 else (index // 2, 0)
 
                 @pl.when(distance == index)
                 def _(page=page, source=source):
-                    taken = pages[source[0]]
-                    store(page, taken[source[1], 0], taken[source[1], 1])
+                    take(page, pages[source[0]], 2 * page_rows * source[1])
 
     keys[prefix * page_rows :, :] = keys_new[...]
     values[prefix * page_rows :, :] = values_new[...]
@@ -507,10 +520,10 @@
             ]
 
 
-def attend(place, numbers, prefix, parts, cosine, sine, keys_new, values_new, pages):
+def attend(place, numbers, prefix, page_rows, parts, cosine, sine, keys_new, values_new, pages):
     token_rows, head_size = cosine.shape
     group = parts[0].shape[1] // head_size
-    total_rows = prefix * pages[0].shape[2] + token_rows
+    total_rows = prefix * page_rows + token_rows
     together = group if total_rows <= 1024 else 1
     return pl.pallas_call(
         functools.partial(attend_kernel, len(parts), together, prefix),
@@ -535,28 +548,21 @@
 
     requests = [owners, slots, homes, home_slots]
     plan = column_plan if ranks == 8 else general_plan
-    kv_parts, finish, table, copied, numbers = plan(
+    kv_parts, finish, tables, numbers = plan(
         tokens, norm_attn, wqkv, pages_count, requests, pool, place, ranks
     )
     positions = tie(pages_count[0], kv_parts[0]) * page_rows + jnp.arange(token_rows, dtype=jnp.int32)
     cosine, sine = rotary_tables(positions.astype(jnp.float32), head_size)
     keys_new, values_new, outgoing = fresh_pages(
-        numbers, 1 + 2 * prefix, new_pages, kv_parts, cosine, sine, ranks, page_rows
-    )
-    q_parts, pages, far = finish(keys_new)
-    if CFG["N"]:
-        outgoing = tie(outgoing, far)
+        numbers, 1 + 2 * prefix, kv_parts, cosine, sine, ranks, page_rows
+    )
     incoming = lax.all_to_all(outgoing, "dp", split_axis=0, concat_axis=0, tiled=True)
-    if CFG["L"] == 2:
-        pool_out = land_pages(place, table, incoming, copied, 1 + 2 * prefix, new_pages)
-        q_parts = tie(q_parts, pool_out)
+    q_parts, pages, copied = finish(keys_new)
+    pool_out = land_pages(place, tables, incoming, copied, 1 + 2 * prefix, new_pages)
+    q_parts = tie(q_parts, pool_out)
     attended = attend(
-        place, numbers, prefix, q_parts, cosine, sine, keys_new, values_new, pages
-    )
-    if CFG["L"] < 2:
-        if CFG["L"]:
-            copied, attended = lax.optimization_barrier((copied, attended))
-        pool_out = land_pages(place, table, incoming, copied, 1 + 2 * prefix, new_pages)
+        place, numbers, prefix, page_rows, q_parts, cosine, sine, keys_new, values_new, pages
+    )
     return (attended, pool_out)
 
 

time: 61.5 us -> 59.7 us (0.971)
  waiting for transfers between devices: 20.1 us -> 16 us
  starting transfers between devices: 28.2 us -> 30.4 us
    ppermute x11, waiting for transfers between devices: 18.3 us -> 7.91 us  [along(): return lax.ppermute(values, 'dp', crossed(ranks, 2 * step))]
    all_to_all x1, waiting for transfers between devices: 0.01 us -> 5.29 us  [local(): lax.all_to_all(outgoing, 'dp', split_axis=0, concat_axis=0, tiled=True)]
    ppermute x11, starting transfers between devices: 15.2 us -> 18 us  [along(): return lax.ppermute(values, 'dp', crossed(ranks, 2 * step))]
    ppermute x5, starting transfers between devices: 7.98 us -> 7.13 us  [near(): return lax.ppermute(values, 'dp', crossed(ranks, 1))]
    ppermute x5, waiting for transfers between devices: 0.89 us -> 1.64 us  [near(): return lax.ppermute(values, 'dp', crossed(ranks, 1))]
where the time goes in v7:
time: 59.7 us; the launch traced here: 59.4 us
  starting transfers between devices  30.4 us (51%)
  waiting for transfers between devices  16 us (27%)
  Pallas kernels  11.1 us (19%)
  between operations  1.41 us (2%)
    ppermute x11, starting transfers between devices, along(): return lax.ppermute(values, 'dp', crossed(ranks, 2 * step))  18 us
    ppermute x11, waiting for transfers between devices, along(): return lax.ppermute(values, 'dp', crossed(ranks, 2 * step))  7.91 us
    ppermute x5, starting transfers between devices, near(): return lax.ppermute(values, 'dp', crossed(ranks, 1))  7.13 us
    all_to_all x1, waiting for transfers between devices, local(): lax.all_to_all(outgoing, 'dp', split_axis=0, concat_axis=0, tiled=True)  5.29 us
    all_to_all x1, starting transfers between devices, local(): lax.all_to_all(outgoing, 'dp', split_axis=0, concat_axis=0, tiled=True)  4.68 us
    pallas_call x1, Pallas kernels, prepare(): pl.pallas_call(prepare_kernel, out_shape=[jax.ShapeDtypeStruct((token_row...  2.57 us
    pallas_call x1, Pallas kernels, attend(): pl.pallas_call(functools.partial(attend_kernel, len(parts), together, pre...  1.98 us
    ppermute x5, waiting for transfers between devices, near(): return lax.ppermute(values, 'dp', crossed(ranks, 1))  1.64 us
  transfers between devices with their start and end apart: 20, of which 8 were waited for; matrix products, arithmetic and copies ran while one was open for 1% of the time, Pallas kernels for 11%

profile of v7, /device:TPU:0, one launch (start us, length us, event | category | flops | bytes accessed | tf_op | source)
XLA Modules:
  0.0 59.4 jit_solution(8432633211617287287)
XLA Ops:
  1.3 0.0 copy-start.3
  1.3 2.6 %prepare.1 = (bf16[144,512]{1,0:T(8,128)(2,1)}, bf16[144,512]{1,0:T(8,128)(2,1)}, bf16[144,512]{1,0:T(8,128)(2,1)}, bf16[144,512]{1,0:T(8,128)(2,1)}, bf16[144,512]{1,0:T(8,128)(2,1)}) custom-call(bf16[128,4096]{1,0:T(8,128)(2,1)} %refs_0_.1, f32[1,4096]{1,0:T(1,128)} %bitcast.11, s32[1,1]{1,0:T(1,128)} %bitcast.9.refs_2_, s32[1,4]{1,0:T(1,128)} %refs_3_.1, ...), custom_call_target="tpu_custom_call" | custom-call | flops 34500001792 | tf_op jit(solution)/shard_map/prepare/pallas_call | solution.py:81
  3.9 3.1 %collective-permute-start = (bf16[144,512]{1,0:T(8,128)(2,1)}, bf16[144,512]{1,0:T(8,128)(2,1)S(1)}, u32[]{:S(2)}, u32[]{:S(2)}) collective-permute-start(bf16[144,512]{1,0:T(8,128)(2,1)} %get-tuple-element.37), channel_id=1, source_target_pairs={{0,4},{2,6},{4,0},{6,2},{8,12},{10,14},{12,8},{14,10},{1,5},{3,7},... | collective-permute-start | bytes 442376 | tf_op jit(solution)/shard_map/ppermute | solution.py:244
  7.0 0.0 copy-done.3
  7.0 0.0 copy-start.5
  7.0 0.0 copy-start.4
  7.0 0.1 fusion.1
  7.0 1.6 %collective-permute-start.6 = (bf16[2,512,128]{2,1,0:T(8,128)(2,1)S(1)}, bf16[2,512,128]{2,1,0:T(8,128)(2,1)S(1)}, u32[]{:S(2)}, u32[]{:S(2)}) collective-permute-start(bf16[2,512,128]{2,1,0:T(8,128)(2,1)S(1)} %get-tuple-element.72.refs_8_), channel_id=1, source_target_pairs={{0,2},{2,0},{4,6},{6,4},{8,10},{10,8},{12,14},{14,12},{1,3},{3,1},... | collective-permute-start | bytes 786440 | tf_op jit(solution)/shard_map/ppermute | solution.py:240
  8.6 0.0 copy-done.5
  8.6 2.6 %collective-permute-start.1 = (bf16[144,512]{1,0:T(8,128)(2,1)S(1)}, bf16[144,512]{1,0:T(8,128)(2,1)S(1)}, u32[]{:S(2)}, u32[]{:S(2)}) collective-permute-start(bf16[144,512]{1,0:T(8,128)(2,1)S(1)} %copy-done.5), channel_id=1, source_target_pairs={{0,8},{2,10},{4,12},{6,14},{8,0},{10,2},{12,4},{14,6},{1,9},{3,11}... | collective-permute-start | bytes 442376 | tf_op jit(solution)/shard_map/ppermute | solution.py:244
  11.2 0.0 copy-done.4
  11.2 0.2 collective-permute-start.2
  11.4 0.8 %collective-permute-start.7 = (bf16[2,512,128]{2,1,0:T(8,128)(2,1)S(1)}, bf16[2,512,128]{2,1,0:T(8,128)(2,1)S(1)}, u32[]{:S(2)}, u32[]{:S(2)}) collective-permute-start(bf16[2,512,128]{2,1,0:T(8,128)(2,1)S(1)} %get-tuple-element.71.refs_8_), channel_id=1, source_target_pairs={{0,2},{2,0},{4,6},{6,4},{8,10},{10,8},{12,14},{14,12},{1,3},{3,1},... | collective-permute-start | bytes 786440 | tf_op jit(solution)/shard_map/ppermute | solution.py:240
  12.2 0.0 collective-permute-done.refs_1_
  12.2 1.8 %collective-permute-start.8 = (bf16[2,512,128]{2,1,0:T(8,128)(2,1)S(1)}, bf16[2,512,128]{2,1,0:T(8,128)(2,1)S(1)}, u32[]{:S(2)}, u32[]{:S(2)}) collective-permute-start(bf16[2,512,128]{2,1,0:T(8,128)(2,1)S(1)} %get-tuple-element.70.refs_9_), channel_id=1, source_target_pairs={{0,2},{2,0},{4,6},{6,4},{8,10},{10,8},{12,14},{14,12},{1,3},{3,1},... | collective-permute-start | bytes 786440 | tf_op jit(solution)/shard_map/ppermute | solution.py:240
  14.0 0.3 fusion
  14.3 7.8 %collective-permute-done.1.refs_2_ = bf16[144,512]{1,0:T(8,128)(2,1)S(1)} collective-permute-done((bf16[144,512]{1,0:T(8,128)(2,1)S(1)}, bf16[144,512]{1,0:T(8,128)(2,1)S(1)}, u32[]{:S(2)}, u32[]{:S(2)}) %collective-permute-start.1) | collective-permute-done | bytes 147488 | tf_op jit(solution)/shard_map/ppermute | solution.py:244
  22.1 0.0 collective-permute-start.3
  22.1 0.0 collective-permute-done.2.refs_3_
  22.1 0.5 collective-permute-start.4
  22.6 0.0 collective-permute-done.6.refs_9_
  22.6 0.1 collective-permute-start.5
  22.7 0.1 pad_add_fusion.place
  22.8 0.0 copy-start
  22.8 0.0 copy-start.1
  22.8 0.1 pad_maximum_fusion
  22.9 0.6 %collective-permute-done.3.refs_5_ = bf16[144,512]{1,0:T(8,128)(2,1)S(1)} collective-permute-done((bf16[144,512]{1,0:T(8,128)(2,1)S(1)}, bf16[144,512]{1,0:T(8,128)(2,1)S(1)}, u32[]{:S(2)}, u32[]{:S(2)}) %collective-permute-start.3) | collective-permute-done | bytes 147488 | tf_op jit(solution)/shard_map/ppermute | solution.py:256
  23.5 0.2 collective-permute-done.4.refs_6_
  23.7 0.3 collective-permute-done.5.refs_7_
  24.0 0.0 copy-done
  24.0 0.0 copy-done.1
  24.0 1.0 %kv_products.1 = (f32[128,256]{1,0:T(8,128)S(1)}, bf16[128,256]{1,0:T(8,128)(2,1)S(1)}, bf16[128,256]{1,0:T(8,128)(2,1)S(1)}, bf16[128,256]{1,0:T(8,128)(2,1)S(1)}, s32[4,128]{1,0:T(4,128)S(1)}) custom-call(s32[2]{0:T(128)S(1)} %pad_add_fusion.place, bf16[144,512]{1,0:T(8,128)(2,1)S(1)} %copy-done, bf16[144,512]{1,0:T(8,128)(2,1)S(1)} %collective-permute-done.refs_1_, ...), custom_call_target="tpu_custom_call" | custom-call | tf_op jit(solution)/shard_map/kv_products/pallas_call | solution.py:127
  25.0 0.0 collective-permute-done.7.refs_10_
  25.0 1.1 %collective-permute-done.8.refs_11_ = bf16[2,512,128]{2,1,0:T(8,128)(2,1)S(1)} collective-permute-done((bf16[2,512,128]{2,1,0:T(8,128)(2,1)S(1)}, bf16[2,512,128]{2,1,0:T(8,128)(2,1)S(1)}, u32[]{:S(2)}, u32[]{:S(2)}) %collective-permute-start.8) | collective-permute-done | bytes 262176 | tf_op jit(solution)/shard_map/ppermute | solution.py:240
  26.1 1.1 %collective-permute-start.10 = (bf16[128,256]{1,0:T(8,128)(2,1)S(1)}, bf16[128,256]{1,0:T(8,128)(2,1)S(1)}, u32[]{:S(2)}, u32[]{:S(2)}) collective-permute-start(bf16[128,256]{1,0:T(8,128)(2,1)S(1)} %get-tuple-element.48), channel_id=1, source_target_pairs={{0,4},{2,6},{4,0},{6,2},{8,12},{10,14},{12,8},{14,10},{1,5},{3,7},... | collective-permute-start | bytes 196616 | tf_op jit(solution)/shard_map/ppermute | solution.py:244
  27.2 1.9 %collective-permute-start.11 = (bf16[128,256]{1,0:T(8,128)(2,1)S(1)}, bf16[128,256]{1,0:T(8,128)(2,1)S(1)}, u32[]{:S(2)}, u32[]{:S(2)}) collective-permute-start(bf16[128,256]{1,0:T(8,128)(2,1)S(1)} %get-tuple-element.49), channel_id=1, source_target_pairs={{0,8},{2,10},{4,12},{6,14},{8,0},{10,2},{12,4},{14,6},{1,9},{3,11}... | collective-permute-start | bytes 196616 | tf_op jit(solution)/shard_map/ppermute | solution.py:244
  29.1 1.3 %collective-permute-start.12 = (bf16[128,256]{1,0:T(8,128)(2,1)S(1)}, bf16[128,256]{1,0:T(8,128)(2,1)S(1)}, u32[]{:S(2)}, u32[]{:S(2)}) collective-permute-start(bf16[128,256]{1,0:T(8,128)(2,1)S(1)} %get-tuple-element.50), channel_id=1, source_target_pairs={{0,12},{2,14},{4,8},{6,10},{8,4},{10,6},{12,0},{14,2},{1,13},{3,15... | collective-permute-start | bytes 196616 | tf_op jit(solution)/shard_map/ppermute | solution.py:244
  30.5 0.0 copy-start.2
  30.5 1.5 %collective-permute-start.14 = (s32[4,128]{1,0:T(4,128)S(1)}, s32[4,128]{1,0:T(4,128)S(1)}, u32[]{:S(2)}, u32[]{:S(2)}) collective-permute-start(s32[4,128]{1,0:T(4,128)S(1)} %get-tuple-element.59.numbers.refs_0_), channel_id=1, source_target_pairs={{0,2},{2,0},{4,6},{6,4},{8,10},{10,8},{12,14},{14,12},{1,3},{3,1},... | collective-permute-start | bytes 6152 | tf_op jit(solution)/shard_map/ppermute | solution.py:240
  32.0 1.3 %q_products.1 = (f32[256,512]{1,0:T(8,128)S(1)}, bf16[256,512]{1,0:T(8,128)(2,1)S(1)}) custom-call(s32[2]{0:T(128)S(1)} %pad_add_fusion.place, bf16[144,512]{1,0:T(8,128)(2,1)S(1)} %copy-done, bf16[144,512]{1,0:T(8,128)(2,1)S(1)} %collective-permute-done.refs_1_, bf16[144,512]{1,0:T(8,128)(2,1)S(1)} %collective-permute-done.1.refs_2_, ...), custom_call_target="tpu_custom_call" | custom-call | flops 1150000000 | tf_op jit(solution)/shard_map/q_products/pallas_call | solution.py:152
  33.2 0.3 collective-permute-start.9
  33.5 0.5 collective-permute-done.14.refs_1_
  34.1 0.0 copy-done.2
  34.1 1.5 %choose_pages.1 = (bf16[256,128]{1,0:T(8,128)(2,1)S(1)}, bf16[256,128]{1,0:T(8,128)(2,1)S(1)}, bf16[256,128]{1,0:T(8,128)(2,1)S(1)}, bf16[256,128]{1,0:T(8,128)(2,1)S(1)}, bf16[16,2,64,128]{3,2,1,0:T(8,128)(2,1)}) custom-call(s32[2]{0:T(128)S(1)} %pad_add_fusion.place, s32[4,128]{1,0:T(4,128)S(1)} %get-tuple-element.59.numbers.refs_0_, ...), custom_call_target="tpu_custom_call" | custom-call | flops 11500000256 | tf_op jit(solution)/shard_map/choose_pages/pallas_call | solution.py:191
  35.6 1.3 %collective-permute-start.15 = (bf16[256,128]{1,0:T(8,128)(2,1)S(1)}, bf16[256,128]{1,0:T(8,128)(2,1)S(1)}, u32[]{:S(2)}, u32[]{:S(2)}) collective-permute-start(bf16[256,128]{1,0:T(8,128)(2,1)S(1)} %get-tuple-element.67), channel_id=1, source_target_pairs={{0,4},{2,6},{4,0},{6,2},{8,12},{10,14},{12,8},{14,10},{1,5},{3,7},... | collective-permute-start | bytes 196616 | tf_op jit(solution)/shard_map/ppermute | solution.py:244
  36.9 0.0 collective-permute-done.10.refs_1_
  37.0 1.8 %collective-permute-start.16 = (bf16[256,128]{1,0:T(8,128)(2,1)S(1)}, bf16[256,128]{1,0:T(8,128)(2,1)S(1)}, u32[]{:S(2)}, u32[]{:S(2)}) collective-permute-start(bf16[256,128]{1,0:T(8,128)(2,1)S(1)} %get-tuple-element.68), channel_id=1, source_target_pairs={{0,8},{2,10},{4,12},{6,14},{8,0},{10,2},{12,4},{14,6},{1,9},{3,11}... | collective-permute-start | bytes 196616 | tf_op jit(solution)/shard_map/ppermute | solution.py:244
  38.7 0.0 collective-permute-done.11.refs_2_
  38.7 1.3 %collective-permute-start.17 = (bf16[256,128]{1,0:T(8,128)(2,1)S(1)}, bf16[256,128]{1,0:T(8,128)(2,1)S(1)}, u32[]{:S(2)}, u32[]{:S(2)}) collective-permute-start(bf16[256,128]{1,0:T(8,128)(2,1)S(1)} %get-tuple-element.69), channel_id=1, source_target_pairs={{0,12},{2,14},{4,8},{6,10},{8,4},{10,6},{12,0},{14,2},{1,13},{3,15... | collective-permute-start | bytes 196616 | tf_op jit(solution)/shard_map/ppermute | solution.py:244
  40.1 0.0 collective-permute-done.12.refs_3_
  40.1 1.4 %fresh_pages.1 = (bf16[128,128]{1,0:T(8,128)(2,1)S(1)}, bf16[128,128]{1,0:T(8,128)(2,1)S(1)}, bf16[8,2,64,128]{3,2,1,0:T(8,128)(2,1)}) custom-call(s32[4,128]{1,0:T(4,128)S(1)} %get-tuple-element.59.numbers.refs_0_, f32[128,256]{1,0:T(8,128)S(1)} %get-tuple-element.51.refs_0_, bf16[128,256]{1,0:T(8,128)(2,1)S(1)} %collective-permute-done.10.refs_1_, ...), custom_call_target="tpu_custom_call" | custom-call | flops 34500001792 | tf_op jit(solution)/shard_map/fresh_pages/pallas_call | solution.py:439
  41.5 4.7 %all-to-all-start = ((bf16[8,2,64,128]{3,2,1,0:T(8,128)(2,1)}), bf16[8,2,64,128]{3,2,1,0:T(8,128)(2,1)S(1)}, u32[]{:S(2)}, u32[]{:S(2)}) async-start(bf16[8,2,64,128]{3,2,1,0:T(8,128)(2,1)} %get-tuple-element.58), calls=%async_computation | async-start | bytes 524288 | tf_op jit(solution)/shard_map/all_to_all | solution.py:559
  46.1 0.0 collective-permute-done.9.arrived.refs_1_
  46.2 3.0 %collective-permute-start.13 = (bf16[128,512]{1,0:T(8,128)(2,1)S(1)}, bf16[128,512]{1,0:T(8,128)(2,1)S(1)}, u32[]{:S(2)}, u32[]{:S(2)}) collective-permute-start(bf16[128,512]{1,0:T(8,128)(2,1)S(1)} %fold.1), channel_id=1, source_target_pairs={{0,8},{2,10},{4,12},{6,14},{8,0},{10,2},{12,4},{14,6},{1,9},{3,11}... | collective-permute-start | bytes 393224 | tf_op jit(solution)/shard_map/ppermute | solution.py:244
  49.2 0.0 collective-permute-done.15.refs_1_.refs_8_
  49.2 0.0 collective-permute-done.16.refs_2_.refs_9_
  49.2 0.0 collective-permute-done.17.refs_3_.refs_10_
  49.2 1.5 %collective-permute-start.18 = (bf16[512,128]{1,0:T(8,128)(2,1)S(1)}, bf16[512,128]{1,0:T(8,128)(2,1)S(1)}, u32[]{:S(2)}, u32[]{:S(2)}) collective-permute-start(bf16[512,128]{1,0:T(8,128)(2,1)S(1)} %relay.1), channel_id=1, source_target_pairs={{0,2},{2,0},{4,6},{6,4},{8,10},{10,8},{12,14},{14,12},{1,3},{3,1},... | collective-permute-start | bytes 393224 | tf_op jit(solution)/shard_map/ppermute | solution.py:240
  50.7 5.3 %all-to-all-done.refs_2_ = bf16[8,2,64,128]{3,2,1,0:T(8,128)(2,1)S(1)} async-done(((bf16[8,2,64,128]{3,2,1,0:T(8,128)(2,1)}), bf16[8,2,64,128]{3,2,1,0:T(8,128)(2,1)S(1)}, u32[]{:S(2)}, u32[]{:S(2)}) %all-to-all-start) | async-done | bytes 262176 | tf_op jit(solution)/shard_map/all_to_all | solution.py:559
  56.0 1.3 %land_pages.1 = bf16[16,2,64,128]{3,2,1,0:T(8,128)(2,1)} custom-call(s32[2]{0:T(128)S(1)} %pad_add_fusion.place, s32[4,128]{1,0:T(4,128)S(1)} %get-tuple-element.59.numbers.refs_0_, s32[4,128]{1,0:T(4,128)S(1)} %collective-permute-done.14.refs_1_, bf16[8,2,64,128]{3,2,1,0:T(8,128)(2,1)S(1)} %all-to-all-done.refs_2_, ...), custom_call_target="tpu_custom_call", output_to_operand_aliasing={{}: (4, {})} | custom-call | tf_op jit(solution)/shard_map/land_pages/pallas_call | solution.py:408
  57.3 0.1 collective-permute-done.13.refs_2_
  57.4 0.0 collective-permute-done.18.refs_11_
  57.4 2.0 %attend.1 = bf16[128,512]{1,0:T(8,128)(2,1)} custom-call(s32[2]{0:T(128)S(1)} %pad_add_fusion.place, s32[4,128]{1,0:T(4,128)S(1)} %get-tuple-element.59.numbers.refs_0_, f32[256,512]{1,0:T(8,128)S(1)} %get-tuple-element.62.kept.refs_0_, bf16[256,512]{1,0:T(8,128)(2,1)S(1)} %collective-permute-done.9.arrived.refs_1_, ...), custom_call_target="tpu_custom_call" | custom-call | flops 3449999872 | tf_op jit(solution)/shard_map/attend/pallas_call | solution.py:528
  (4 shorter events, 0.1 us)
Async XLA Ops:
  1.3 5.7 %copy-start.3 = (bf16[512,1,6,128]{3,0,2,1:T(8,128)(2,1)S(1)}, bf16[512,1,6,128]{3,0,2,1:T(8,128)(2,1)}, u32[]{:S(2)}) copy-start(bf16[512,1,6,128]{3,0,2,1:T(8,128)(2,1)} %param.17) | copy-start | bytes 2359300
  3.9 8.3 %collective-permute-start = (bf16[144,512]{1,0:T(8,128)(2,1)}, bf16[144,512]{1,0:T(8,128)(2,1)S(1)}, u32[]{:S(2)}, u32[]{:S(2)}) collective-permute-start(bf16[144,512]{1,0:T(8,128)(2,1)} %get-tuple-element.37), channel_id=1, source_target_pairs={{0,4},{2,6},{4,0},{6,2},{8,12},{10,14},{12,8},{14,10},{1,5},{3,7},... | collective-permute-start | bytes 442376 | tf_op jit(solution)/shard_map/ppermute | solution.py:244
  7.0 1.6 %copy-start.5 = (bf16[144,512]{1,0:T(8,128)(2,1)S(1)}, bf16[144,512]{1,0:T(8,128)(2,1)}, u32[]{:S(2)}) copy-start(bf16[144,512]{1,0:T(8,128)(2,1)} %get-tuple-element.38) | copy-start | bytes 442372
  7.0 4.2 %copy-start.4 = (bf16[144,512]{1,0:T(8,128)(2,1)S(1)}, bf16[144,512]{1,0:T(8,128)(2,1)}, u32[]{:S(2)}) copy-start(bf16[144,512]{1,0:T(8,128)(2,1)} %get-tuple-element.39) | copy-start | bytes 442372
  7.0 15.6 %collective-permute-start.6 = (bf16[2,512,128]{2,1,0:T(8,128)(2,1)S(1)}, bf16[2,512,128]{2,1,0:T(8,128)(2,1)S(1)}, u32[]{:S(2)}, u32[]{:S(2)}) collective-permute-start(bf16[2,512,128]{2,1,0:T(8,128)(2,1)S(1)} %get-tuple-element.72.refs_8_), channel_id=1, source_target_pairs={{0,2},{2,0},{4,6},{6,4},{8,10},{10,8},{12,14},{14,12},{1,3},{3,1},... | collective-permute-start | bytes 786440 | tf_op jit(solution)/shard_map/ppermute | solution.py:240
  8.6 13.5 %collective-permute-start.1 = (bf16[144,512]{1,0:T(8,128)(2,1)S(1)}, bf16[144,512]{1,0:T(8,128)(2,1)S(1)}, u32[]{:S(2)}, u32[]{:S(2)}) collective-permute-start(bf16[144,512]{1,0:T(8,128)(2,1)S(1)} %copy-done.5), channel_id=1, source_target_pairs={{0,8},{2,10},{4,12},{6,14},{8,0},{10,2},{12,4},{14,6},{1,9},{3,11}... | collective-permute-start | bytes 442376 | tf_op jit(solution)/shard_map/ppermute | solution.py:244
  11.2 10.9 %collective-permute-start.2 = (bf16[144,512]{1,0:T(8,128)(2,1)S(1)}, bf16[144,512]{1,0:T(8,128)(2,1)S(1)}, u32[]{:S(2)}, u32[]{:S(2)}) collective-permute-start(bf16[144,512]{1,0:T(8,128)(2,1)S(1)} %copy-done.4), channel_id=1, source_target_pairs={{0,12},{2,14},{4,8},{6,10},{8,4},{10,6},{12,0},{14,2},{1,13},{3,15... | collective-permute-start | bytes 442376 | tf_op jit(solution)/shard_map/ppermute | solution.py:244
  11.4 13.6 %collective-permute-start.7 = (bf16[2,512,128]{2,1,0:T(8,128)(2,1)S(1)}, bf16[2,512,128]{2,1,0:T(8,128)(2,1)S(1)}, u32[]{:S(2)}, u32[]{:S(2)}) collective-permute-start(bf16[2,512,128]{2,1,0:T(8,128)(2,1)S(1)} %get-tuple-element.71.refs_8_), channel_id=1, source_target_pairs={{0,2},{2,0},{4,6},{6,4},{8,10},{10,8},{12,14},{14,12},{1,3},{3,1},... | collective-permute-start | bytes 786440 | tf_op jit(solution)/shard_map/ppermute | solution.py:240
  12.2 13.9 %collective-permute-start.8 = (bf16[2,512,128]{2,1,0:T(8,128)(2,1)S(1)}, bf16[2,512,128]{2,1,0:T(8,128)(2,1)S(1)}, u32[]{:S(2)}, u32[]{:S(2)}) collective-permute-start(bf16[2,512,128]{2,1,0:T(8,128)(2,1)S(1)} %get-tuple-element.70.refs_9_), channel_id=1, source_target_pairs={{0,2},{2,0},{4,6},{6,4},{8,10},{10,8},{12,14},{14,12},{1,3},{3,1},... | collective-permute-start | bytes 786440 | tf_op jit(solution)/shard_map/ppermute | solution.py:240
  22.1 1.4 %collective-permute-start.3 = (bf16[144,512]{1,0:T(8,128)(2,1)S(1)}, bf16[144,512]{1,0:T(8,128)(2,1)S(1)}, u32[]{:S(2)}, u32[]{:S(2)}) collective-permute-start(bf16[144,512]{1,0:T(8,128)(2,1)S(1)} %collective-permute-done.refs_1_), channel_id=1, source_target_pairs={{0,1},{1,0},{2,3},{3,2},{4,5},{5,4},{6,7},{7,6},{8,9},{9,8},{10,11... | collective-permute-start | bytes 442376 | tf_op jit(solution)/shard_map/ppermute | solution.py:256
  22.1 1.6 %collective-permute-start.4 = (bf16[144,512]{1,0:T(8,128)(2,1)S(1)}, bf16[144,512]{1,0:T(8,128)(2,1)S(1)}, u32[]{:S(2)}, u32[]{:S(2)}) collective-permute-start(bf16[144,512]{1,0:T(8,128)(2,1)S(1)} %collective-permute-done.1.refs_2_), channel_id=1, source_target_pairs={{0,1},{1,0},{2,3},{3,2},{4,5},{5,4},{6,7},{7,6},{8,9},{9,8},{10,11... | collective-permute-start | bytes 442376 | tf_op jit(solution)/shard_map/ppermute | solution.py:256
  22.6 1.4 %collective-permute-start.5 = (bf16[144,512]{1,0:T(8,128)(2,1)S(1)}, bf16[144,512]{1,0:T(8,128)(2,1)S(1)}, u32[]{:S(2)}, u32[]{:S(2)}) collective-permute-start(bf16[144,512]{1,0:T(8,128)(2,1)S(1)} %collective-permute-done.2.refs_3_), channel_id=1, source_target_pairs={{0,1},{1,0},{2,3},{3,2},{4,5},{5,4},{6,7},{7,6},{8,9},{9,8},{10,11... | collective-permute-start | bytes 442376 | tf_op jit(solution)/shard_map/ppermute | solution.py:256
  22.8 1.2 %copy-start = (bf16[144,512]{1,0:T(8,128)(2,1)S(1)}, bf16[144,512]{1,0:T(8,128)(2,1)}, u32[]{:S(2)}) copy-start(bf16[144,512]{1,0:T(8,128)(2,1)} %get-tuple-element.36.refs_0_) | copy-start | bytes 442372
  22.8 1.2 %copy-start.1 = (bf16[144,512]{1,0:T(8,128)(2,1)S(1)}, bf16[144,512]{1,0:T(8,128)(2,1)}, u32[]{:S(2)}) copy-start(bf16[144,512]{1,0:T(8,128)(2,1)} %get-tuple-element.40.refs_4_) | copy-start | bytes 442372
  26.1 10.9 %collective-permute-start.10 = (bf16[128,256]{1,0:T(8,128)(2,1)S(1)}, bf16[128,256]{1,0:T(8,128)(2,1)S(1)}, u32[]{:S(2)}, u32[]{:S(2)}) collective-permute-start(bf16[128,256]{1,0:T(8,128)(2,1)S(1)} %get-tuple-element.48), channel_id=1, source_target_pairs={{0,4},{2,6},{4,0},{6,2},{8,12},{10,14},{12,8},{14,10},{1,5},{3,7},... | collective-permute-start | bytes 196616 | tf_op jit(solution)/shard_map/ppermute | solution.py:244
  27.2 11.5 %collective-permute-start.11 = (bf16[128,256]{1,0:T(8,128)(2,1)S(1)}, bf16[128,256]{1,0:T(8,128)(2,1)S(1)}, u32[]{:S(2)}, u32[]{:S(2)}) collective-permute-start(bf16[128,256]{1,0:T(8,128)(2,1)S(1)} %get-tuple-element.49), channel_id=1, source_target_pairs={{0,8},{2,10},{4,12},{6,14},{8,0},{10,2},{12,4},{14,6},{1,9},{3,11}... | collective-permute-start | bytes 196616 | tf_op jit(solution)/shard_map/ppermute | solution.py:244
  29.1 11.0 %collective-permute-start.12 = (bf16[128,256]{1,0:T(8,128)(2,1)S(1)}, bf16[128,256]{1,0:T(8,128)(2,1)S(1)}, u32[]{:S(2)}, u32[]{:S(2)}) collective-permute-start(bf16[128,256]{1,0:T(8,128)(2,1)S(1)} %get-tuple-element.50), channel_id=1, source_target_pairs={{0,12},{2,14},{4,8},{6,10},{8,4},{10,6},{12,0},{14,2},{1,13},{3,15... | collective-permute-start | bytes 196616 | tf_op jit(solution)/shard_map/ppermute | solution.py:244
  30.5 3.6 %copy-start.2 = (bf16[16,2,64,128]{3,2,1,0:T(8,128)(2,1)S(1)}, bf16[16,2,64,128]{3,2,1,0:T(8,128)(2,1)}, u32[]{:S(2)}) copy-start(bf16[16,2,64,128]{3,2,1,0:T(8,128)(2,1)} %refs_2_.1) | copy-start | bytes 1572868
  30.5 3.6 %collective-permute-start.14 = (s32[4,128]{1,0:T(4,128)S(1)}, s32[4,128]{1,0:T(4,128)S(1)}, u32[]{:S(2)}, u32[]{:S(2)}) collective-permute-start(s32[4,128]{1,0:T(4,128)S(1)} %get-tuple-element.59.numbers.refs_0_), channel_id=1, source_target_pairs={{0,2},{2,0},{4,6},{6,4},{8,10},{10,8},{12,14},{14,12},{1,3},{3,1},... | collective-permute-start | bytes 6152 | tf_op jit(solution)/shard_map/ppermute | solution.py:240
  33.2 12.9 %collective-permute-start.9 = (bf16[256,512]{1,0:T(8,128)(2,1)S(1)}, bf16[256,512]{1,0:T(8,128)(2,1)S(1)}, u32[]{:S(2)}, u32[]{:S(2)}) collective-permute-start(bf16[256,512]{1,0:T(8,128)(2,1)S(1)} %get-tuple-element.47), channel_id=1, source_target_pairs={{0,4},{2,6},{4,0},{6,2},{8,12},{10,14},{12,8},{14,10},{1,5},{3,7},... | collective-permute-start | bytes 786440 | tf_op jit(solution)/shard_map/ppermute | solution.py:244
  35.6 13.5 %collective-permute-start.15 = (bf16[256,128]{1,0:T(8,128)(2,1)S(1)}, bf16[256,128]{1,0:T(8,128)(2,1)S(1)}, u32[]{:S(2)}, u32[]{:S(2)}) collective-permute-start(bf16[256,128]{1,0:T(8,128)(2,1)S(1)} %get-tuple-element.67), channel_id=1, source_target_pairs={{0,4},{2,6},{4,0},{6,2},{8,12},{10,14},{12,8},{14,10},{1,5},{3,7},... | collective-permute-start | bytes 196616 | tf_op jit(solution)/shard_map/ppermute | solution.py:244
  37.0 12.2 %collective-permute-start.16 = (bf16[256,128]{1,0:T(8,128)(2,1)S(1)}, bf16[256,128]{1,0:T(8,128)(2,1)S(1)}, u32[]{:S(2)}, u32[]{:S(2)}) collective-permute-start(bf16[256,128]{1,0:T(8,128)(2,1)S(1)} %get-tuple-element.68), channel_id=1, source_target_pairs={{0,8},{2,10},{4,12},{6,14},{8,0},{10,2},{12,4},{14,6},{1,9},{3,11}... | collective-permute-start | bytes 196616 | tf_op jit(solution)/shard_map/ppermute | solution.py:244
  38.7 10.4 %collective-permute-start.17 = (bf16[256,128]{1,0:T(8,128)(2,1)S(1)}, bf16[256,128]{1,0:T(8,128)(2,1)S(1)}, u32[]{:S(2)}, u32[]{:S(2)}) collective-permute-start(bf16[256,128]{1,0:T(8,128)(2,1)S(1)} %get-tuple-element.69), channel_id=1, source_target_pairs={{0,12},{2,14},{4,8},{6,10},{8,4},{10,6},{12,0},{14,2},{1,13},{3,15... | collective-permute-start | bytes 196616 | tf_op jit(solution)/shard_map/ppermute | solution.py:244
  41.5 14.6 %all-to-all-start = ((bf16[8,2,64,128]{3,2,1,0:T(8,128)(2,1)}), bf16[8,2,64,128]{3,2,1,0:T(8,128)(2,1)S(1)}, u32[]{:S(2)}, u32[]{:S(2)}) async-start(bf16[8,2,64,128]{3,2,1,0:T(8,128)(2,1)} %get-tuple-element.58), calls=%async_computation | async-start | bytes 524288 | tf_op jit(solution)/shard_map/all_to_all | solution.py:559
  46.2 11.2 %collective-permute-start.13 = (bf16[128,512]{1,0:T(8,128)(2,1)S(1)}, bf16[128,512]{1,0:T(8,128)(2,1)S(1)}, u32[]{:S(2)}, u32[]{:S(2)}) collective-permute-start(bf16[128,512]{1,0:T(8,128)(2,1)S(1)} %fold.1), channel_id=1, source_target_pairs={{0,8},{2,10},{4,12},{6,14},{8,0},{10,2},{12,4},{14,6},{1,9},{3,11}... | collective-permute-start | bytes 393224 | tf_op jit(solution)/shard_map/ppermute | solution.py:244
  49.2 8.2 %collective-permute-start.18 = (bf16[512,128]{1,0:T(8,128)(2,1)S(1)}, bf16[512,128]{1,0:T(8,128)(2,1)S(1)}, u32[]{:S(2)}, u32[]{:S(2)}) collective-permute-start(bf16[512,128]{1,0:T(8,128)(2,1)S(1)} %relay.1), channel_id=1, source_target_pairs={{0,2},{2,0},{4,6},{6,4},{8,10},{10,8},{12,14},{14,12},{1,3},{3,1},... | collective-permute-start | bytes 393224 | tf_op jit(solution)/shard_map/ppermute | solution.py:240
